TPU v7x, 256 devices: a whole 4x4x8 slice. The times are simulated.
256 devices in a mesh: ctx: 8 (over z), expert: 32 (over y, x, core).
Axes of the slice: x: 4, y: 4, z: 8, core: 2. Of those that a mesh axis runs over, the one named last changes fastest.
Arguments:
- tokens: bfloat16 [32, 1024, 1024], P('expert', 'ctx'), may hold values from -6 to 6
- chain_ids: int32 [32, 1024], P('expert', 'ctx'), may hold values from 0 to 7, never falling along the last dimension, each value on 1 to 256 neighbouring positions
- route_ids: int32 [32, 1024, 6], P('expert', 'ctx'), may hold values from 0 to 31, all different within a row; in each aligned block of 128 rows (0 to 127, 128 to 255, ..., all dimensions but the last counted through in order) at most 32 rows name the same one
- route_weights: float32 [32, 1024, 6], P('expert', 'ctx'), may hold values from 0.1 to 0.5
- attn_gain: float32 [1024], replicated, may hold values from 0.6 to 12
- ffn_gain: float32 [1024], replicated, may hold values from 0.1 to 1.9
- chain_bias: float32 [8], replicated, may hold values from 0.5 to 2.5
- w_qkv: bfloat16 [3, 1024, 1024], P(None, 'expert', 'ctx'), may hold values from -0.1875 to 0.1875
- w_out: bfloat16 [1024, 1024], P('ctx', 'expert'), may hold values from -0.75 to 0.75
- w_gateup: bfloat16 [32, 1024, 2816], P('expert'), may hold values from -0.1875 to 0.1875
- w_down: bfloat16 [32, 1408, 1024], P('expert'), may hold values from -0.15625 to 0.15625
Outputs:
- layer_out: bfloat16 [32, 1024, 1024], P('expert', 'ctx')
Inputs may be any that keep to these rules, and one draw needn't show every extreme that they name: `route_ids`: each residue names 6 different experts. Among the 128 residues of one device (aligned blocks of the residues in order, crop after crop), no expert is named by more than 32 of them, and in every draw some expert is named by exactly 32. `chain_ids`: chain numbers never fall along a crop; a chain spans 1 to 256 residues, and some chain exactly that many.
All inputs are finite; a program needn't handle non-finite values.
Results may differ from a plain program's by a relative error of at most 0.02.
The roundings to bfloat16 on the way count: a program that leaves them out, or rounds other values in their place, can miss the bound.
Values may be sent and summed in bfloat16 or wider, within the bound.
No kernel may reach another device: no remote copies, remote signals or barrier semaphores. Data moves between devices by JAX's collectives and lax.ppermute only.
A program may use at most 64 MiB of HBM per device.

v0:
```python
import math

import jax
import jax.numpy as jnp
from jax import lax
from jax.sharding import PartitionSpec as P


def rms_scale(values, gain):
    wide = values.astype(jnp.float32)
    return wide * lax.rsqrt(jnp.mean(wide * wide, axis=-1, keepdims=True) + 1e-05) * gain


def attend(query, key, value, chains, bias):
    length = query.shape[0]
    group = bias.shape[0]
    head_dim = query.shape[1] // group
    block = min(512, length)
    scale = 1.0 / math.sqrt(head_dim)
    keys = key.reshape(length, group, head_dim)
    values = value.reshape(length, group, head_dim)
    query_blocks = query.reshape(length // block, block, group, head_dim)
    chain_blocks = chains.reshape(length // block, block)

    def one_block(items):
        q_block, c_block = items
        scores = (
            jnp.einsum("qhd,khd->hqk", q_block, keys, preferred_element_type=jnp.float32) * scale
        )
        same = (c_block[:, None] == chains[None, :]).astype(jnp.float32)
        scores = scores + bias[:, None, None] * same[None]
        top = jnp.max(scores, axis=-1, keepdims=True)
        raised = jnp.exp(scores - top)
        probs = (raised / jnp.sum(raised, axis=-1, keepdims=True)).astype(jnp.bfloat16)
        return jnp.einsum("hqk,khd->qhd", probs, values, preferred_element_type=jnp.float32).astype(
            jnp.bfloat16
        )

    return lax.map(one_block, (query_blocks, chain_blocks)).reshape(length, group * head_dim)


def per_device(
    tokens,
    chain_ids,
    route_ids,
    route_weights,
    attn_gain,
    ffn_gain,
    chain_bias,
    w_qkv,
    w_out,
    w_gateup,
    w_down,
):
    tok = tokens.shape[1]
    width = tokens.shape[2]
    inputs = tokens[0]
    normed = rms_scale(inputs, attn_gain).astype(jnp.bfloat16)
    chains = lax.all_gather(chain_ids[0], "ctx", axis=0, tiled=True)
    groups = lax.axis_size("ctx")
    per_group = chain_bias.shape[0] // groups
    bias = lax.dynamic_slice_in_dim(chain_bias, lax.axis_index("ctx") * per_group, per_group)
    qkv_columns, out_full_rows = (
        lax.all_gather(w_qkv, "ctx", axis=2, tiled=True),
        lax.all_gather(w_out, "ctx", axis=0, tiled=True),
    )
    projected = jnp.einsum(
        "tr,ird->itd",
        normed,
        lax.all_gather(qkv_columns, "expert", axis=1, tiled=True),
        preferred_element_type=jnp.float32,
    ).astype(jnp.bfloat16)
    regrouped = lax.all_to_all(projected, "ctx", split_axis=2, concat_axis=1, tiled=True)
    attended = attend(regrouped[0], regrouped[1], regrouped[2], chains, bias)
    local_rows = lax.all_to_all(attended, "ctx", split_axis=0, concat_axis=1, tiled=True)
    mixed = inputs.astype(jnp.float32) + jnp.dot(
        local_rows,
        lax.all_gather(out_full_rows, "expert", axis=1, tiled=True),
        preferred_element_type=jnp.float32,
    )
    ffn_in = rms_scale(mixed, ffn_gain).astype(jnp.bfloat16)
    held = w_gateup.shape[0]
    experts = lax.axis_size("expert") * held
    topk = route_ids.shape[2]
    cap = min(tok, tok * topk * 4 // (experts * 3))
    hidden = w_down.shape[1]
    flat_ids = route_ids[0].reshape(-1)
    onehot = (flat_ids[:, None] == jnp.arange(experts, dtype=jnp.int32)[None, :]).astype(jnp.int32)
    rank = jnp.sum((jnp.cumsum(onehot, axis=0) - onehot) * onehot, axis=1)
    slots = flat_ids * cap + rank
    select = jnp.sum(
        (
            slots.reshape(tok, topk)[:, :, None]
            == jnp.arange(experts * cap, dtype=jnp.int32)[None, None, :]
        ).astype(jnp.bfloat16),
        axis=1,
    )
    outgoing = lax.dot_general(
        select, ffn_in, (((0,), (0,)), ((), ())), preferred_element_type=jnp.float32
    )
    outgoing = outgoing.astype(jnp.bfloat16).reshape(experts, cap, width)
    block = lax.all_to_all(outgoing, "expert", split_axis=0, concat_axis=0, tiled=True)
    count = block.shape[1]
    grouped = block.reshape(-1, held, count, width)
    both = jnp.einsum("sxcd,xdf->sxcf", grouped, w_gateup, preferred_element_type=jnp.float32)
    active = (jax.nn.silu(both[..., :hidden]) * both[..., hidden:]).astype(jnp.bfloat16)
    result = jnp.einsum(
        "sxcf,xfd->sxcd", active, w_down, preferred_element_type=jnp.float32
    ).astype(jnp.bfloat16)
    returned = lax.all_to_all(
        result.reshape(-1, count, width), "expert", split_axis=0, concat_axis=0, tiled=True
    )
    picked = jnp.take(returned.reshape(-1, width), slots, axis=0).reshape(tok, topk, width)
    weights = route_weights[0]
    moe_sum = mixed
    for route in range(topk):
        moe_sum = moe_sum + weights[:, route : route + 1] * picked[:, route].astype(jnp.float32)
    return moe_sum.astype(jnp.bfloat16)[None]


def solution(mesh):
    placed = (
        P("expert", "ctx", None),
        P("expert", "ctx"),
        P("expert", "ctx", None),
        P("expert", "ctx", None),
        P(),
        P(),
        P(),
        P(None, "expert", "ctx"),
        P("ctx", "expert"),
        P("expert", None, None),
        P("expert", None, None),
    )
    return jax.shard_map(
        per_device, mesh=mesh, in_specs=placed, out_specs=P("expert", "ctx", None), check_vma=False
    )
```

profile of v0, /device:TPU:1, one launch (start us, length us, event | category | flops | bytes accessed | tf_op | source)
XLA Modules:
  0.0 299.5 jit_solution(6906347522959631811)
XLA Ops:
  6.5 23.7 %all_gather.15 = bf16[3,32,1024]{2,1,0:T(8,128)(2,1)} all-gather(bf16[3,32,128]{2,1,0:T(8,128)(2,1)} %param.20), channel_id=1, replica_groups=mesh['ctx'=8,'expert'=32] {'ctx'}, dimensions={2}, use_global_device_ids=true | all-gather | bytes 221184 | tf_op jit(solution)/shard_map/all_gather | solution.py:64
  30.3 1.1 fusion.22
  31.4 57.7 %all-gather.4.cloned.1.call-done = bf16[3,1024,1024]{2,1,0:T(8,128)(2,1)} async-done(((bf16[3,32,1024]{2,1,0:T(8,128)(2,1)}), bf16[3,1024,1024]{2,1,0:T(8,128)(2,1)}) %all-gather.4.cloned.1.call-update) | async-done | bytes 6291472 | tf_op jit(solution)/shard_map/all_gather | solution.py:70
  89.0 4.8 %fusion.21 = bf16[3,128,1024]{2,1,0:T(8,128)(2,1)} fusion(bf16[3,1024,1024]{2,1,0:T(8,128)(2,1)} %all-gather.4.cloned.1.call-done, bf16[1,128,1024]{2,1,0:T(8,128)(2,1)} %param.13, f32[1024]{0:T(1024)} %param.17, f32[128]{0:T(128)S(1)} %add_rsqrt_fusion.1), kind=kOutput, calls=%fused_computation.28 | convolution fusion | flops 806223872 | bytes 7344640 | tf_op jit(solution)/shard_map/tr,ird->itd/dot_general | solution.py:67
  93.9 2.4 copy.69
  96.3 6.7 %all-to-all-start = ((bf16[3,128,1024]{1,0,2:T(4,128)(2,1)}), bf16[3,128,1024]{1,0,2:T(4,128)(2,1)}, u32[]{:S(2)}, u32[]{:S(2)}) async-start(bf16[3,128,1024]{1,0,2:T(4,128)(2,1)} %copy.69), calls=%async_computation | async-start | bytes 2097152 | tf_op jit(solution)/shard_map/all_to_all | solution.py:73
  103.1 39.4 %all_gather.18 = bf16[1024,32]{0,1:T(8,128)(2,1)} all-gather(bf16[128,32]{0,1:T(8,128)(2,1)S(1)} %copy-done.6), channel_id=1, replica_groups=mesh['ctx'=8,'expert'=32] {'ctx'}, dimensions={0}, use_global_device_ids=true | all-gather | bytes 73728 | tf_op jit(solution)/shard_map/all_gather | solution.py:65
  142.6 0.1 copy.77
  142.7 0.1 eq.54
  142.8 0.1 reshape_squeeze.15
  143.0 11.5 %all-gather = s32[1,1024]{1,0:T(1,128)S(1)} all-gather(s32[1,128]{1,0:T(1,128)S(1)} %copy-done.9), channel_id=2, replica_groups=mesh['ctx'=8,'expert'=32] {'ctx'}, dimensions={1}, use_global_device_ids=true | all-gather | bytes 4608 | tf_op jit(solution)/shard_map/all_gather | solution.py:59
  154.5 0.5 broadcast.132
  155.0 0.7 reduce.12
  155.7 1.7 reduce-window.6
  157.4 0.3 slice_reduce_fusion
  157.7 0.6 dynamic_slice.11
  158.3 1.3 copy.70
  159.7 0.8 fusion.47
  160.5 1.8 copy.71
  162.3 0.8 copy.72
  163.1 0.8 copy.73
  164.0 8.2 %while.10 = (s32[]{:T(128)}, bf16[2,512,1,128]{3,1,2,0:T(8,128)(2,1)}, bf16[2,512,1,128]{3,1,2,0:T(8,128)(2,1)}, bf16[1024,1,128]{2,0,1:T(8,128)(2,1)}, s32[2,51...) while((s32[]{:T(128)}, ...), condition=%wide.region_4.5_spmd, body=%wide.region_1.4_spmd.sunk | while | flops 273742848 | bytes 10245305 | solution.py:39
  164.0 2.3 fusion.58
  166.3 0.5 fusion.59
  166.8 0.6 fusion.60
  167.4 0.7 copy-done.3
  168.1 2.3 fusion.58
  170.4 0.5 fusion.59
  170.9 0.6 fusion.60
  171.5 0.7 copy-done.3
  172.2 4.2 %all-to-all-start.1 = ((bf16[8,128,128]{2,1,0:T(8,128)(2,1)}), bf16[8,128,128]{2,1,0:T(8,128)(2,1)S(1)}, u32[]{:S(2)}, u32[]{:S(2)}) async-start(bf16[8,128,128]{2,1,0:T(8,128)(2,1)} %bitcast.176), calls=%async_computation.1 | async-start | bytes 524288 | tf_op jit(solution)/shard_map/all_to_all | solution.py:75
  176.5 0.1 reduce_sum.54
  176.8 1.1 fusion.20
  177.9 7.9 %all-to-all-done.1 = bf16[8,128,128]{2,1,0:T(8,128)(2,1)S(1)} async-done(((bf16[8,128,128]{2,1,0:T(8,128)(2,1)}), bf16[8,128,128]{2,1,0:T(8,128)(2,1)S(1)}, u32[]{:S(2)}, u32[]{:S(2)}) %all-to-all-start.1) | async-done | bytes 262176 | tf_op jit(solution)/shard_map/all_to_all | solution.py:75
  185.8 0.9 copy.75
  186.6 6.5 %all-gather.6.cloned.1.call-done = bf16[1024,1024]{0,1:T(8,128)(2,1)} async-done(((bf16[1024,32]{0,1:T(8,128)(2,1)}), bf16[1024,1024]{0,1:T(8,128)(2,1)}) %all-gather.6.cloned.1.call-update) | async-done | bytes 2097168 | tf_op jit(solution)/shard_map/all_gather | solution.py:78
  193.2 2.6 multiply_reduce_fusion
  195.8 0.8 convolution_convert_fusion.1
  196.6 37.6 %all_to_all.44 = bf16[32,32,1024]{2,1,0:T(8,128)(2,1)S(1)} all-to-all(bf16[32,32,1024]{2,1,0:T(8,128)(2,1)S(1)} %bitcast.172), channel_id=1, replica_groups=mesh['ctx'=8,'expert'=32] {'expert'}, dimensions={0} | all-to-all | bytes 4194304 | tf_op jit(solution)/shard_map/all_to_all | solution.py:102
  234.2 6.1 %convolution_bitcast_fusion = f32[32,1,32,2816]{3,2,0,1:T(8,128)S(1)} fusion(bf16[32,32,1024]{2,1,0:T(8,128)(2,1)S(1)} %all_to_all.44, bf16[1,1024,2816]{2,1,0:T(8,128)(2,1)S(1)} %copy-done.10), kind=kOutput, calls=%fused_computation.14 | convolution fusion | flops 5905580032 | bytes 19398656 | tf_op jit(solution)/shard_map/sxcd,xdf->sxcf/dot_general | solution.py:105
  240.4 4.8 %fusion.15 = bf16[32,32,1024]{2,1,0:T(8,128)(2,1)} fusion(bf16[1,1408,1024]{2,1,0:T(8,128)(2,1)S(1)} %copy-done, f32[32,1,32,2816]{3,2,0,1:T(8,128)S(1)} %convolution_bitcast_fusion), kind=kOutput, calls=%fused_computation.23 | convolution fusion | flops 2962489344 | bytes 16515072 | tf_op jit(solution)/shard_map/sxcf,xfd->sxcd/dot_general | solution.py:107
  245.2 4.9 %all-to-all-start.3 = ((bf16[32,32,1024]{2,1,0:T(8,128)(2,1)}), bf16[32,32,1024]{2,1,0:T(8,128)(2,1)}, u32[]{:S(2)}, u32[]{:S(2)}) async-start(bf16[32,32,1024]{2,1,0:T(8,128)(2,1)} %fusion.15), calls=%async_computation.3 | async-start | bytes 4194304 | tf_op jit(solution)/shard_map/all_to_all | solution.py:110
  250.2 0.1 mul.167
  250.4 27.6 %all-to-all-done.3 = bf16[32,32,1024]{2,1,0:T(8,128)(2,1)} async-done(((bf16[32,32,1024]{2,1,0:T(8,128)(2,1)}), bf16[32,32,1024]{2,1,0:T(8,128)(2,1)}, u32[]{:S(2)}, u32[]{:S(2)}) %all-to-all-start.3) | async-done | bytes 2097184 | tf_op jit(solution)/shard_map/all_to_all | solution.py:110
  278.0 6.4 %gather_fusion = bf16[768,1024]{1,0:T(8,128)(2,1)} fusion(bf16[1024,1024]{1,0:T(8,128)(2,1)} %bitcast.38, s32[1024]{0:T(1024)S(1)} %pad_clamp_fusion), kind=kCustom, calls=%fused_computation | custom fusion | bytes 3148800 | tf_op jit(solution)/shard_map/jit(_take)/gather | solution.py:113
  284.4 3.7 %gather.7 = bf16[128,6,1024]{2,1,0:T(8,128)(2,1)} reshape(bf16[768,1024]{1,0:T(8,128)(2,1)} %gather_fusion) | data formatting | bytes 3145728 | tf_op jit(solution)/shard_map/jit(_take)/gather | solution.py:113
  288.1 3.4 %copy_select_fusion = bf16[128,6,1024]{2,0,1:T(8,128)(2,1)S(1)} fusion(bf16[128,6,1024]{2,1,0:T(8,128)(2,1)} %gather.7, pred[128,6]{0,1:T(8,128)(4,1)S(1)} %get-tuple-element.112), kind=kLoop, calls=%fused_computation.26 | loop fusion | flops 786432 | bytes 3146496 | tf_op jit(solution)/shard_map/jit(_take)/select_n | solution.py:113
  291.6 1.1 fusion.39
  (50 shorter events, 0.5 us)
Async XLA Ops:
  6.5 233.8 %copy-start = (bf16[1,1408,1024]{2,1,0:T(8,128)(2,1)S(1)}, bf16[1,1408,1024]{2,1,0:T(8,128)(2,1)}, u32[]{:S(2)}) copy-start(bf16[1,1408,1024]{2,1,0:T(8,128)(2,1)} %param.23) | copy-start | bytes 8650756
  6.5 82.5 %all-gather.4.cloned.1.call-start = ((), (), s32[]{:S(2)}) async-start(), calls=%async_computation.4 | async-start | bytes 6488064 | tf_op jit(solution)/shard_map/all_gather | solution.py:70
  93.9 9.2 %copy-start.6 = (bf16[128,32]{0,1:T(8,128)(2,1)S(1)}, bf16[128,32]{0,1:T(8,128)(2,1)}, u32[]{:S(2)}) copy-start(bf16[128,32]{0,1:T(8,128)(2,1)} %param.21) | copy-start | bytes 24580
  93.9 48.7 %copy-start.5 = (s32[1,128,6]{1,0,2:T(1,128)S(1)}, s32[1,128,6]{1,0,2:T(1,128)}, u32[]{:S(2)}) copy-start(s32[1,128,6]{1,0,2:T(1,128)} %param.15) | copy-start | bytes 9220
  93.9 49.1 %copy-start.9 = (s32[1,128]{1,0:T(1,128)S(1)}, s32[1,128]{1,0:T(1,128)}, u32[]{:S(2)}) copy-start(s32[1,128]{1,0:T(1,128)} %param.14) | copy-start | bytes 1540
  93.9 63.8 %copy-start.11 = (f32[8]{0:T(128)S(1)}, f32[8]{0:T(128)}, u32[]{:S(2)}) copy-start(f32[8]{0:T(128)} %param.19) | copy-start | bytes 100
  96.3 62.0 %all-to-all-start = ((bf16[3,128,1024]{1,0,2:T(4,128)(2,1)}), bf16[3,128,1024]{1,0,2:T(4,128)(2,1)}, u32[]{:S(2)}, u32[]{:S(2)}) async-start(bf16[3,128,1024]{1,0,2:T(4,128)(2,1)} %copy.69), calls=%async_computation | async-start | bytes 2097152 | tf_op jit(solution)/shard_map/all_to_all | solution.py:73
  103.0 90.1 %all-gather.6.cloned.1.call-start = ((), (), s32[]{:S(2)}) async-start(), calls=%async_computation.5 | async-start | bytes 2162688 | tf_op jit(solution)/shard_map/all_gather | solution.py:78
  164.0 2.8 copy-start.2
  164.0 2.8 copy-start.4
  167.4 0.7 copy-start.3
  168.1 2.8 copy-start.2
  168.1 2.8 copy-start.4
  171.5 0.7 copy-start.3
  172.2 13.6 %all-to-all-start.1 = ((bf16[8,128,128]{2,1,0:T(8,128)(2,1)}), bf16[8,128,128]{2,1,0:T(8,128)(2,1)S(1)}, u32[]{:S(2)}, u32[]{:S(2)}) async-start(bf16[8,128,128]{2,1,0:T(8,128)(2,1)} %bitcast.176), calls=%async_computation.1 | async-start | bytes 524288 | tf_op jit(solution)/shard_map/all_to_all | solution.py:75
  176.4 19.4 %copy-start.7 = (f32[1024]{0:T(1024)S(1)}, f32[1024]{0:T(1024)}, u32[]{:S(2)}) copy-start(f32[1024]{0:T(1024)} %param.18) | copy-start | bytes 12292
  193.2 2.6 copy-start.1
  195.8 38.4 %copy-start.10 = (bf16[1,1024,2816]{2,1,0:T(8,128)(2,1)S(1)}, bf16[1,1024,2816]{2,1,0:T(8,128)(2,1)}, u32[]{:S(2)}) copy-start(bf16[1,1024,2816]{2,1,0:T(8,128)(2,1)} %param.22) | copy-start | bytes 17301508
  245.2 5.2 %copy-start.8 = (f32[1,128,6]{1,0,2:T(1,128)S(1)}, f32[1,128,6]{1,0,2:T(1,128)}, u32[]{:S(2)}) copy-start(f32[1,128,6]{1,0,2:T(1,128)} %param.16) | copy-start | bytes 9220
  245.2 32.9 %all-to-all-start.3 = ((bf16[32,32,1024]{2,1,0:T(8,128)(2,1)}), bf16[32,32,1024]{2,1,0:T(8,128)(2,1)}, u32[]{:S(2)}, u32[]{:S(2)}) async-start(bf16[32,32,1024]{2,1,0:T(8,128)(2,1)} %fusion.15), calls=%async_computation.3 | async-start | bytes 4194304 | tf_op jit(solution)/shard_map/all_to_all | solution.py:110
Sparse Core Ops, SparseCore 0:
  30.4 58.5 all-gather.3
  142.7 50.4 all-gather.5
where the time goes:
time: 300 us
  blocking collectives  112 us (37%)
  waiting for transfers between devices  99.7 us (33%)
  matrix products  24.9 us (8%)
  local copies, waits for them, and re-layouts  22.7 us (8%)
  starting transfers between devices  15.9 us (5%)
  between operations  13.6 us (5%)
  other arithmetic  10.4 us (3%)
    all_gather x1, waiting for transfers between devices, per_device(): lax.all_gather(qkv_columns, 'expert', axis=1, tiled=True)  57.7 us
    all_gather x1, blocking collectives, per_device(): lax.all_gather(w_out, 'ctx', axis=0, tiled=True)  39.4 us
    all_to_all x1, blocking collectives, per_device(): lax.all_to_all(outgoing, 'expert', split_axis=0, concat_axis=0, tiled=True)  37.6 us
    all_to_all x1, waiting for transfers between devices, per_device(): lax.all_to_all(result.reshape(-1, count, width), 'expert', split_axis=0,...  27.6 us
    all_gather x1, blocking collectives, per_device(): lax.all_gather(w_qkv, 'ctx', axis=2, tiled=True)  23.7 us
    all_gather x1, blocking collectives, per_device(): chains = lax.all_gather(chain_ids[0], 'ctx', axis=0, tiled=True)  11.5 us
    gather x2, local copies, waits for them, and re-layouts, per_device(): jnp.take(returned.reshape(-1, width), slots, axis=0)  10.1 us
    all_to_all x1, waiting for transfers between devices, per_device(): lax.all_to_all(attended, 'ctx', split_axis=0, concat_axis=1, tiled=True)  7.86 us
  transfers between devices with their start and end apart: 5, of which 4 were waited for; matrix products, arithmetic and copies ran while one was open for 7% of the time, Pallas kernels for 0%

commit v1 on v0

v1 whole, which is shorter than its diff:
```python
import functools
import math

import jax
import jax.numpy as jnp
from jax import lax
from jax.experimental import pallas as pl
from jax.experimental.pallas import tpu as pltpu
from jax.sharding import PartitionSpec as P

F32 = jnp.float32
BF16 = jnp.bfloat16
MIB = 1 << 20
CHUNKS = 1
CAP = 32


def vmem_spec():
    return pl.BlockSpec(memory_space=pltpu.VMEM)


def smem_spec():
    return pl.BlockSpec(memory_space=pltpu.SMEM)


def rms_scale(values, gain):
    wide = values.astype(F32)
    return wide * lax.rsqrt(jnp.mean(wide * wide, axis=-1, keepdims=True) + 1e-05) * gain


def slot_parts(shape, dim, experts, cap):
    slot = lax.broadcasted_iota(jnp.int32, shape, dim)
    part = cap // CHUNKS
    per_chunk = experts * part
    within = lax.rem(slot, per_chunk)
    return within // part, (slot // per_chunk) * part + lax.rem(within, part)


def route_kernel(experts, cap, ids_ref, idst_ref, weights_ref, pick_ref, high_ref, low_ref):
    tok, topk = ids_ref.shape
    slots = experts * cap
    named = jnp.zeros((tok, experts), F32)
    gates = jnp.zeros((tok, experts), F32)
    lane = lax.broadcasted_iota(jnp.int32, (tok, experts), 1)
    for route in range(topk):
        hit = ids_ref[:, route : route + 1] == lane
        named = named + jnp.where(hit, 1.0, 0.0)
        gates = gates + jnp.where(hit, weights_ref[:, route : route + 1], 0.0)
    row = lax.broadcasted_iota(jnp.int32, (tok, tok), 0)
    col = lax.broadcasted_iota(jnp.int32, (tok, tok), 1)
    before = jnp.where(col < row, 1.0, 0.0).astype(BF16)
    named16 = named.astype(BF16)
    rank = jnp.dot(before, named16, preferred_element_type=F32)
    expert_of, place_of = slot_parts((experts, slots), 1, experts, cap)
    spread = jnp.where(
        lax.broadcasted_iota(jnp.int32, (experts, slots), 0) == expert_of, 1.0, 0.0
    ).astype(BF16)
    place = place_of[0:1, :].astype(F32)
    mine = jnp.where(named > 0.5, rank, -1.0).astype(BF16)
    here = jnp.dot(mine, spread, preferred_element_type=F32) == place
    high = gates.astype(BF16)
    low = (gates - high.astype(F32)).astype(BF16)
    high_ref[...] = jnp.where(
        here, jnp.dot(high, spread, preferred_element_type=F32), 0.0
    ).astype(BF16)
    low_ref[...] = jnp.where(
        here, jnp.dot(low, spread, preferred_element_type=F32), 0.0
    ).astype(BF16)

    named_t = jnp.zeros((experts, tok), F32)
    sub = lax.broadcasted_iota(jnp.int32, (experts, tok), 0)
    for route in range(topk):
        named_t = named_t + jnp.where(idst_ref[route : route + 1, :] == sub, 1.0, 0.0)
    after = jnp.where(row < col, 1.0, 0.0).astype(BF16)
    rank_t = jnp.dot(named_t.astype(BF16), after, preferred_element_type=F32)
    mine_t = jnp.where(named_t > 0.5, rank_t, -1.0).astype(BF16)
    expert_t, place_t = slot_parts((slots, experts), 0, experts, cap)
    spread_t = jnp.where(
        lax.broadcasted_iota(jnp.int32, (slots, experts), 1) == expert_t, 1.0, 0.0
    ).astype(BF16)
    here_t = jnp.dot(spread_t, mine_t, preferred_element_type=F32) == place_t[:, 0:1].astype(F32)
    pick_ref[...] = jnp.where(here_t, 1.0, 0.0).astype(BF16)


def route_tables(ids, weights, experts, cap):
    tok, topk = ids.shape
    slots = experts * cap
    return pl.pallas_call(
        functools.partial(route_kernel, experts, cap),
        out_shape=[
            jax.ShapeDtypeStruct((slots, tok), BF16),
            jax.ShapeDtypeStruct((tok, slots), BF16),
            jax.ShapeDtypeStruct((tok, slots), BF16),
        ],
        in_specs=[vmem_spec()] * 3,
        out_specs=[vmem_spec()] * 3,
        compiler_params=pltpu.CompilerParams(vmem_limit_bytes=8 * MIB),
        cost_estimate=pl.CostEstimate(flops=2 * 10**8, bytes_accessed=10**6, transcendentals=0),
        name="route_tables",
    )(ids, ids.T, weights)


def attention_kernel(
    steps, me_ref, bias_ref, chain_ref, w_ref, *refs
):
    blocks, (out_ref, w_buf, q_buf, k_buf, v_buf) = refs[:-5], refs[-5:]
    me = me_ref[0]
    ring = len(steps)
    tok = out_ref.shape[1]
    head_dim = out_ref.shape[2]
    width = w_buf.shape[0]
    for i in range(3):
        w_buf[:, i * head_dim : (i + 1) * head_dim] = w_ref[:, i].reshape(width, head_dim)
    start = 0
    for block in blocks:
        rows = block.shape[0]
        both = jnp.dot(block[...], w_buf[...], preferred_element_type=F32).astype(BF16)
        q_buf[start : start + rows] = both[:, :head_dim]
        k_buf[start : start + rows] = both[:, head_dim : 2 * head_dim]
        v_buf[start : start + rows] = both[:, 2 * head_dim :]
        start += rows
    owner = [lax.rem(me + (s + ring), ring) for s in steps]
    rows_of = [chain_ref[o] for o in owner]
    key_chain = jnp.concatenate(rows_of, axis=1)
    scale = 1.0 / math.sqrt(head_dim)
    bias = bias_ref[me]
    pair = 2
    for first in range(0, ring, pair):
        query_chain = jnp.concatenate(
            [
                jnp.broadcast_to(rows_of[first + j], (tok, tok)).T
                for j in range(pair)
            ],
            axis=0,
        )
        query_chain = jnp.concatenate([query_chain] * ring, axis=1)
        query = q_buf[first * tok : (first + pair) * tok]
        scores = (
            lax.dot_general(
                query, k_buf[...], (((1,), (1,)), ((), ())), preferred_element_type=F32
            )
            * scale
        )
        scores = scores + jnp.where(query_chain == key_chain, bias, 0.0)
        top = jnp.max(scores, axis=-1, keepdims=True)
        raised = jnp.exp(scores - top)
        probs = (raised * (1.0 / jnp.sum(raised, axis=-1, keepdims=True))).astype(BF16)
        mixed = jnp.dot(probs, v_buf[...], preferred_element_type=F32).astype(BF16)
        for j in range(pair):
            out_ref[owner[first + j]] = mixed[j * tok : (j + 1) * tok]


def attention(me, bias, chains, weights, blocks, steps):
    ring = len(steps)
    tok = chains.shape[2]
    head_dim = weights.shape[3]
    width = weights.shape[0] * weights.shape[2]
    length = ring * tok
    return pl.pallas_call(
        functools.partial(attention_kernel, steps),
        out_shape=jax.ShapeDtypeStruct((ring, tok, head_dim), BF16),
        in_specs=[smem_spec(), smem_spec()] + [vmem_spec()] * (2 + len(blocks)),
        out_specs=vmem_spec(),
        scratch_shapes=[
            pltpu.VMEM((width, 3 * head_dim), BF16),
            pltpu.VMEM((length, head_dim), BF16),
            pltpu.VMEM((length, head_dim), BF16),
            pltpu.VMEM((length, head_dim), BF16),
        ],
        compiler_params=pltpu.CompilerParams(vmem_limit_bytes=24 * MIB),
        cost_estimate=pl.CostEstimate(
            flops=1400 * 10**6, bytes_accessed=3 * 10**6, transcendentals=10**6
        ),
        name="attention",
    )(me, bias, chains, weights, *blocks)


def dispatch_kernel(heads_ref, w_ref, tokens_ref, gain_ref, pick_ref, mixed_ref, *out_refs):
    local = jnp.concatenate([heads_ref[h] for h in range(heads_ref.shape[0])], axis=1)
    mixed = tokens_ref[...].astype(F32) + lax.dot_general(
        local, w_ref[...], (((1,), (1,)), ((), ())), preferred_element_type=F32
    )
    mixed_ref[...] = mixed
    ffn_in = (
        mixed * lax.rsqrt(jnp.mean(mixed * mixed, axis=-1, keepdims=True) + 1e-05) * gain_ref[...]
    ).astype(BF16)
    start = 0
    for ref in out_refs:
        experts, rows, width = ref.shape
        count = experts * rows
        ref[...] = (
            jnp.dot(pick_ref[start : start + count], ffn_in, preferred_element_type=F32)
            .astype(BF16)
            .reshape(experts, rows, width)
        )
        start += count


def dispatch(heads, w_out, tokens, gain, pick, experts, cap):
    tok, width = tokens.shape
    return pl.pallas_call(
        dispatch_kernel,
        out_shape=[jax.ShapeDtypeStruct((tok, width), F32)]
        + [jax.ShapeDtypeStruct((experts, cap // CHUNKS, width), BF16)] * CHUNKS,
        in_specs=[vmem_spec()] * 5,
        out_specs=[vmem_spec()] * (1 + CHUNKS),
        compiler_params=pltpu.CompilerParams(vmem_limit_bytes=16 * MIB),
        cost_estimate=pl.CostEstimate(
            flops=600 * 10**6, bytes_accessed=5 * 10**6, transcendentals=0
        ),
        name="dispatch",
    )(heads, w_out, tokens, gain.reshape(1, width), pick)


def expert_kernel(rows_ref, up_ref, down_ref, out_ref):
    count, width = rows_ref.shape
    hidden = down_ref.shape[0]
    step = min(256, count)
    wide = 256

    def block(i, _):
        here = pl.ds(pl.multiple_of(i * step, step), step)
        rows = rows_ref[here, :]
        total = jnp.zeros((step, width), F32)
        for first in range(0, hidden, wide):
            last = min(first + wide, hidden)
            gate = jnp.dot(rows, up_ref[:, first:last], preferred_element_type=F32)
            value = jnp.dot(
                rows, up_ref[:, hidden + first : hidden + last], preferred_element_type=F32
            )
            active = (gate / (1.0 + jnp.exp(-gate)) * value).astype(BF16)
            total = total + jnp.dot(active, down_ref[first:last], preferred_element_type=F32)
        out_ref[here, :] = total.astype(BF16)
        return 0

    lax.fori_loop(0, count // step, block, 0)


def run_expert(rows, w_gateup, w_down):
    count, width = rows.shape
    hidden = w_down.shape[0]
    return pl.pallas_call(
        expert_kernel,
        out_shape=jax.ShapeDtypeStruct((count, width), BF16),
        in_specs=[vmem_spec()] * 3,
        out_specs=vmem_spec(),
        compiler_params=pltpu.CompilerParams(vmem_limit_bytes=24 * MIB),
        cost_estimate=pl.CostEstimate(
            flops=6 * count * width * hidden, bytes_accessed=9 * 10**6, transcendentals=count * hidden
        ),
        name="experts",
    )(rows, w_gateup, w_down)


def combine_kernel(mixed_ref, high_ref, low_ref, *refs):
    back, out_ref = refs[:-1], refs[-1]
    total = mixed_ref[...]
    start = 0
    for ref in back:
        count = ref.shape[0]
        rows = ref[...]
        total = total + jnp.dot(
            high_ref[:, start : start + count], rows, preferred_element_type=F32
        )
        total = total + jnp.dot(
            low_ref[:, start : start + count], rows, preferred_element_type=F32
        )
        start += count
    out_ref[...] = total.astype(BF16)


def combine(mixed, high, low, back):
    return pl.pallas_call(
        combine_kernel,
        out_shape=jax.ShapeDtypeStruct(mixed.shape, BF16),
        in_specs=[vmem_spec()] * (3 + len(back)),
        out_specs=vmem_spec(),
        compiler_params=pltpu.CompilerParams(vmem_limit_bytes=16 * MIB),
        cost_estimate=pl.CostEstimate(
            flops=540 * 10**6, bytes_accessed=4 * 10**6, transcendentals=0
        ),
        name="combine",
    )(mixed, high, low, *back)


def ring_gather(block, axis):
    size = lax.axis_size(axis)
    up = [(i, (i + 1) % size) for i in range(size)]
    down = [(i, (i - 1) % size) for i in range(size)]
    blocks, steps = [block], [0]
    forth = back = block
    for step in range(1, size // 2):
        forth = lax.ppermute(forth, axis, up)
        back = lax.ppermute(back, axis, down)
        blocks += [forth, back]
        steps += [-step, step]
    half = block.shape[0] // 2
    blocks += [lax.ppermute(forth[:half], axis, up), lax.ppermute(back[half:], axis, down)]
    steps += [size // 2]
    return blocks, steps


def per_device(
    tokens,
    chain_ids,
    route_ids,
    route_weights,
    attn_gain,
    ffn_gain,
    chain_bias,
    w_qkv,
    w_out,
    w_gateup,
    w_down,
):
    inputs = tokens[0]
    tok, width = inputs.shape
    ring = lax.axis_size("ctx")
    experts = lax.axis_size("expert")
    me = lax.axis_index("ctx").astype(jnp.int32).reshape(1)
    normed = rms_scale(inputs, attn_gain).astype(BF16)
    blocks, steps = ring_gather(normed, "ctx")

    small = jnp.concatenate([w_out.T, chain_ids.astype(BF16), jnp.zeros((7, tok), BF16)], axis=0)
    small = lax.all_gather(small, "ctx", axis=0)
    columns = w_out.shape[1]
    chains = small[:, columns : columns + 1].astype(F32)
    w_rows = small[:, :columns].transpose(1, 0, 2).reshape(columns, width)
    w_all = lax.all_gather(w_rows, "expert", axis=0, tiled=True)

    w_head = lax.all_to_all(
        jnp.broadcast_to(w_qkv[None], (experts,) + w_qkv.shape), "expert", 0, 0, tiled=True
    )
    pick, high, low = route_tables(route_ids[0], route_weights[0], experts, CAP)
    attended = attention(me, chain_bias, chains, w_head, blocks, steps)
    heads = lax.all_to_all(attended, "ctx", split_axis=0, concat_axis=0, tiled=True)
    mixed, *outgoing = dispatch(heads, w_all, inputs, ffn_gain, pick, experts, CAP)
    back = []
    for rows in outgoing:
        arrived = lax.all_to_all(rows, "expert", split_axis=0, concat_axis=0, tiled=True)
        result = run_expert(arrived.reshape(-1, width), w_gateup[0], w_down[0])
        back.append(
            lax.all_to_all(
                result.reshape(arrived.shape), "expert", split_axis=0, concat_axis=0, tiled=True
            ).reshape(-1, width)
        )
    return combine(mixed, high, low, back)[None]


def solution(mesh):
    placed = (
        P("expert", "ctx", None),
        P("expert", "ctx"),
        P("expert", "ctx", None),
        P("expert", "ctx", None),
        P(),
        P(),
        P(),
        P(None, "expert", "ctx"),
        P("ctx", "expert"),
        P("expert", None, None),
        P("expert", None, None),
    )
    return jax.shard_map(
        per_device, mesh=mesh, in_specs=placed, out_specs=P("expert", "ctx", None), check_vma=False
    )
```

time: 300 us -> 193 us (0.64)
  waiting for transfers between devices: 99.7 us -> 22.1 us
  matrix products: 24.9 us -> 0 us
  Pallas kernels: 0 us -> 21.9 us
  blocking collectives: 112 us -> 94.8 us
  local copies, waits for them, and re-layouts: 22.7 us -> 6.12 us
  starting transfers between devices: 15.9 us -> 30.3 us
  other arithmetic: 10.4 us -> 3.64 us
    all_gather x2 -> x1, waiting for transfers between devices: 64.2 us -> 0.01 us  [per_device(): w_all = lax.all_gather(w_rows, 'expert', axis=0, tiled=True)]
    all_gather x3 -> x1, blocking collectives: 74.7 us -> 22.9 us  [per_device(): small = lax.all_gather(small, 'ctx', axis=0)]
    all_to_all x1 -> x2, blocking collectives: 37.6 us -> 71.9 us  [the longest x1 39.9 us: per_device(): lax.all_to_all(rows, 'expert', split_axis=0, concat_axis=0, tiled=True)]
    all_to_all x3 -> x2, waiting for transfers between devices: 35.5 us -> 8.31 us  [the longest x1 8.31 us: per_device(): lax.all_to_all(attended, 'ctx', split_axis=0, concat_axis=0, tiled=True)]
    dot_general x9 -> x0, matrix products: 24.9 us -> none  [the longest x1 6.12 us: per_device(): jnp.einsum('sxcd,xdf->sxcf', grouped, w_gateup, preferred_element_type=jn...]
    pallas_call x0 -> x5, Pallas kernels: none -> 21.9 us  [the longest x1 12.5 us: run_expert(): pl.pallas_call(expert_kernel, out_shape=jax.ShapeDtypeStruct((count, widt...]
    ppermute x0 -> x8, waiting for transfers between devices: none -> 13.7 us  [the longest x3 11.5 us: ring_gather(): forth = lax.ppermute(forth, axis, up)]
    ppermute x0 -> x8, starting transfers between devices: none -> 11 us  [the longest x3 7.21 us: ring_gather(): back = lax.ppermute(back, axis, down)]
  transfers between devices with their start and end apart: 5 -> 11, of which waited for: 4 -> 4; matrix products, arithmetic and copies ran while one was open for 7% -> 2% of each run, Pallas kernels for 0% -> 3%
where the time goes in v1:
time: 193 us; the launch traced here: 192 us
  blocking collectives  94.8 us (49%)
  starting transfers between devices  30.3 us (16%)
  waiting for transfers between devices  22.1 us (11%)
  Pallas kernels  21.9 us (11%)
  between operations  13.5 us (7%)
  local copies, waits for them, and re-layouts  6.12 us (3%)
  other arithmetic  3.64 us (2%)
    all_to_all x1, blocking collectives, per_device(): lax.all_to_all(rows, 'expert', split_axis=0, concat_axis=0, tiled=True)  39.9 us
    all_to_all x1, blocking collectives, per_device(): lax.all_to_all(result.reshape(arrived.shape), 'expert', split_axis=0, con...  32 us
    all_gather x1, blocking collectives, per_device(): small = lax.all_gather(small, 'ctx', axis=0)  22.9 us
    all_to_all x1, starting transfers between devices, per_device(): lax.all_to_all(jnp.broadcast_to(w_qkv[None], (experts,) + w_qkv.shape), '...  14.4 us
    pallas_call x1, Pallas kernels, run_expert(): pl.pallas_call(expert_kernel, out_shape=jax.ShapeDtypeStruct((count, widt...  12.5 us
    ppermute x3, waiting for transfers between devices, ring_gather(): forth = lax.ppermute(forth, axis, up)  11.5 us
    all_to_all x1, waiting for transfers between devices, per_device(): lax.all_to_all(attended, 'ctx', split_axis=0, concat_axis=0, tiled=True)  8.31 us
    ppermute x3, starting transfers between devices, ring_gather(): back = lax.ppermute(back, axis, down)  7.21 us
  transfers between devices with their start and end apart: 11, of which 4 were waited for; matrix products, arithmetic and copies ran while one was open for 2% of the time, Pallas kernels for 3%

profile of v1, /device:TPU:1, one launch (start us, length us, event | category | flops | bytes accessed | tf_op | source)
XLA Modules:
  0.0 192.4 jit_solution(9578827217900794411)
XLA Ops:
  6.5 0.0 all-gather.3.cloned.1.call-start
  6.5 0.7 convert_element_type.12
  7.2 0.1 pad.2.clone
  7.3 0.8 maximum_maximum_fusion
  8.1 22.9 %all-gather = bf16[320,128]{1,0:T(8,128)(2,1)S(1)} all-gather(bf16[40,128]{1,0:T(8,128)(2,1)S(1)} %maximum_maximum_fusion), channel_id=2, replica_groups=mesh['ctx'=8,'expert'=32] {'ctx'}, dimensions={0}, use_global_device_ids=true | all-gather | bytes 92160 | tf_op jit(solution)/shard_map/all_gather | solution.py:325
  31.0 0.6 copy_bitcast_fusion
  31.6 0.0 all-gather.3.cloned.1.call-update
  31.6 1.1 fusion
  32.7 1.1 fusion.2.refs_0_
  33.9 0.9 collective-permute-start
  34.7 1.9 collective-permute-start.1
  36.6 1.7 broadcast_in_dim.7
  38.3 14.4 %all-to-all-start = ((bf16[32,3,32,128]{3,2,1,0:T(8,128)(2,1)}), bf16[32,3,32,128]{3,2,1,0:T(8,128)(2,1)S(1)}, u32[]{:S(2)}, u32[]{:S(2)}) async-start(bf16[32,3,32,128]{3,2,1,0:T(8,128)(2,1)} %broadcast_in_dim.7), calls=%async_computation | async-start | bytes 1572864 | tf_op jit(solution)/shard_map/all_to_all | solution.py:331
  52.8 0.0 collective-permute-done.refs_1_
  52.8 0.1 collective-permute-start.2
  52.9 0.0 collective-permute-done.1.refs_2_
  52.9 2.7 %collective-permute-start.3 = (bf16[128,1024]{1,0:T(8,128)(2,1)S(1)}, bf16[128,1024]{1,0:T(8,128)(2,1)S(1)}, u32[]{:S(2)}, u32[]{:S(2)}) collective-permute-start(bf16[128,1024]{1,0:T(8,128)(2,1)S(1)} %collective-permute-done.1.refs_2_), channel_id=1, source_target_pairs={{0,224},{32,0},{64,32},{96,64},{128,96},{160,128},{192,160},{224,1... | collective-permute-start | bytes 786440 | tf_op jit(solution)/shard_map/ppermute | solution.py:294
  55.5 6.2 %collective-permute-done.2.refs_3_ = bf16[128,1024]{1,0:T(8,128)(2,1)S(1)} collective-permute-done((bf16[128,1024]{1,0:T(8,128)(2,1)S(1)}, bf16[128,1024]{1,0:T(8,128)(2,1)S(1)}, u32[]{:S(2)}, u32[]{:S(2)}) %collective-permute-start.2) | collective-permute-done | bytes 262176 | tf_op jit(solution)/shard_map/ppermute | solution.py:293
  61.7 0.0 collective-permute-start.4
  61.7 0.0 collective-permute-done.3.refs_4_
  61.7 2.7 %collective-permute-start.5 = (bf16[128,1024]{1,0:T(8,128)(2,1)S(1)}, bf16[128,1024]{1,0:T(8,128)(2,1)S(1)}, u32[]{:S(2)}, u32[]{:S(2)}) collective-permute-start(bf16[128,1024]{1,0:T(8,128)(2,1)S(1)} %collective-permute-done.3.refs_4_), channel_id=1, source_target_pairs={{0,224},{32,0},{64,32},{96,64},{128,96},{160,128},{192,160},{224,1... | collective-permute-start | bytes 786440 | tf_op jit(solution)/shard_map/ppermute | solution.py:294
  64.4 5.3 %collective-permute-done.4.refs_5_ = bf16[128,1024]{1,0:T(8,128)(2,1)S(1)} collective-permute-done((bf16[128,1024]{1,0:T(8,128)(2,1)S(1)}, bf16[128,1024]{1,0:T(8,128)(2,1)S(1)}, u32[]{:S(2)}, u32[]{:S(2)}) %collective-permute-start.4) | collective-permute-done | bytes 262176 | tf_op jit(solution)/shard_map/ppermute | solution.py:293
  69.7 0.1 collective-permute-start.6
  69.8 0.0 collective-permute-done.5.refs_6_
  69.8 2.7 %collective-permute-start.7 = (bf16[64,1024]{1,0:T(8,128)(2,1)S(1)}, bf16[64,1024]{1,0:T(8,128)(2,1)S(1)}, u32[]{:S(2)}, u32[]{:S(2)}) collective-permute-start(bf16[64,1024]{1,0:T(8,128)(2,1)S(1)} %slice.18), channel_id=1, source_target_pairs={{0,224},{32,0},{64,32},{96,64},{128,96},{160,128},{192,160},{224,1... | collective-permute-start | bytes 393224 | tf_op jit(solution)/shard_map/ppermute | solution.py:298
  72.6 0.0 all-to-all-done.w_ref
  72.6 2.3 %collective-permute-done.6.refs_7_ = bf16[64,1024]{1,0:T(8,128)(2,1)S(1)} collective-permute-done((bf16[64,1024]{1,0:T(8,128)(2,1)S(1)}, bf16[64,1024]{1,0:T(8,128)(2,1)S(1)}, u32[]{:S(2)}, u32[]{:S(2)}) %collective-permute-start.6) | collective-permute-done | bytes 131104 | tf_op jit(solution)/shard_map/ppermute | solution.py:298
  74.8 0.0 collective-permute-done.7.refs_8_
  74.8 0.0 copy-start.7
  74.8 0.0 copy-start
  74.9 0.0 copy-start.2
  74.9 5.5 %attention.1 = bf16[8,128,128]{2,1,0:T(8,128)(2,1)} custom-call(s32[1]{0:T(128)} %bitcast.me_ref, f32[8]{0:T(128)S(1)} %copy-done.5, f32[8,1,128]{2,1,0:T(1,128)S(1)} %slice_convert_fusion.chain_ref, bf16[32,3,32,128]{3,2,1,0:T(8,128)(2,1)S(1)} %all-to-all-done.w_ref, bf16[128,1024]{1,0:T(8,128)(2,1)S(1)} %fusion.2.refs_0_, ...), custom_call_target="tpu_custom_call" | custom-call | flops 1400000000 | bytes 3000000 | tf_op jit(solution)/shard_map/attention/pallas_call | solution.py:159
  80.4 4.9 %all-to-all-start.1 = ((bf16[8,128,128]{2,1,0:T(8,128)(2,1)}), bf16[8,128,128]{2,1,0:T(8,128)(2,1)S(1)}, u32[]{:S(2)}, u32[]{:S(2)}) async-start(bf16[8,128,128]{2,1,0:T(8,128)(2,1)} %attention.1), calls=%async_computation.1 | async-start | bytes 524288 | tf_op jit(solution)/shard_map/all_to_all | solution.py:336
  85.3 0.0 copy-done.6
  85.3 0.1 copy.16
  85.4 0.0 copy-done.7
  85.5 0.1 copy.13
  85.6 0.9 route_tables.1
  86.5 8.3 %all-to-all-done.1.heads_ref = bf16[8,128,128]{2,1,0:T(8,128)(2,1)S(1)} async-done(((bf16[8,128,128]{2,1,0:T(8,128)(2,1)}), bf16[8,128,128]{2,1,0:T(8,128)(2,1)S(1)}, u32[]{:S(2)}, u32[]{:S(2)}) %all-to-all-start.1) | async-done | bytes 262176 | tf_op jit(solution)/shard_map/all_to_all | solution.py:336
  94.8 0.0 copy-done.2
  94.8 1.6 copy-done.1
  96.4 1.6 dispatch.1
  98.0 39.9 %all_to_all.20 = bf16[32,32,1024]{2,1,0:T(8,128)(2,1)S(1)} all-to-all(bf16[32,32,1024]{2,1,0:T(8,128)(2,1)S(1)} %get-tuple-element.14), channel_id=1, replica_groups=mesh['ctx'=8,'expert'=32] {'expert'}, dimensions={0} | all-to-all | bytes 4194304 | tf_op jit(solution)/shard_map/all_to_all | solution.py:340
  137.9 0.0 copy-done.3
  137.9 1.8 copy-done.4
  139.7 12.5 %experts.1 = bf16[1024,1024]{1,0:T(8,128)(2,1)S(1)} custom-call(bf16[1024,1024]{1,0:T(8,128)(2,1)S(1)} %bitcast.28, bf16[1024,2816]{1,0:T(8,128)(2,1)S(1)} %bitcast.34, bf16[1408,1024]{1,0:T(8,128)(2,1)S(1)} %bitcast.35), custom_call_target="tpu_custom_call" | custom-call | flops 8858370048 | bytes 9000000 | tf_op jit(solution)/shard_map/experts/pallas_call | solution.py:242
  152.2 32.0 %all_to_all.21 = bf16[32,32,1024]{2,1,0:T(8,128)(2,1)S(1)} all-to-all(bf16[32,32,1024]{2,1,0:T(8,128)(2,1)S(1)} %bitcast.29), channel_id=1, replica_groups=mesh['ctx'=8,'expert'=32] {'expert'}, dimensions={0} | all-to-all | bytes 4194304 | tf_op jit(solution)/shard_map/all_to_all | solution.py:343
  184.2 1.4 combine.1
  (14 shorter events, 0.1 us)
Async XLA Ops:
  6.5 68.3 %copy-start.5 = (f32[8]{0:T(128)S(1)}, f32[8]{0:T(128)}, u32[]{:S(2)}) copy-start(f32[8]{0:T(128)} %bias_ref.1) | copy-start | bytes 100
  6.5 88.3 %all-gather.3.cloned.1.call-start = ((), (), s32[]{:S(2)}) async-start(), calls=%async_computation.4 | async-start | bytes 2162688 | tf_op jit(solution)/shard_map/all_gather | solution.py:329
  33.9 18.9 %collective-permute-start = (bf16[128,1024]{1,0:T(8,128)(2,1)S(1)}, bf16[128,1024]{1,0:T(8,128)(2,1)S(1)}, u32[]{:S(2)}, u32[]{:S(2)}) collective-permute-start(bf16[128,1024]{1,0:T(8,128)(2,1)S(1)} %fusion.2.refs_0_), channel_id=1, source_target_pairs={{0,32},{32,64},{64,96},{96,128},{128,160},{160,192},{192,224},{224... | collective-permute-start | bytes 786440 | tf_op jit(solution)/shard_map/ppermute | solution.py:293
  34.7 18.1 %collective-permute-start.1 = (bf16[128,1024]{1,0:T(8,128)(2,1)S(1)}, bf16[128,1024]{1,0:T(8,128)(2,1)S(1)}, u32[]{:S(2)}, u32[]{:S(2)}) collective-permute-start(bf16[128,1024]{1,0:T(8,128)(2,1)S(1)} %fusion.2.refs_0_), channel_id=1, source_target_pairs={{0,224},{32,0},{64,32},{96,64},{128,96},{160,128},{192,160},{224,1... | collective-permute-start | bytes 786440 | tf_op jit(solution)/shard_map/ppermute | solution.py:294
  38.3 34.2 %all-to-all-start = ((bf16[32,3,32,128]{3,2,1,0:T(8,128)(2,1)}), bf16[32,3,32,128]{3,2,1,0:T(8,128)(2,1)S(1)}, u32[]{:S(2)}, u32[]{:S(2)}) async-start(bf16[32,3,32,128]{3,2,1,0:T(8,128)(2,1)} %broadcast_in_dim.7), calls=%async_computation | async-start | bytes 1572864 | tf_op jit(solution)/shard_map/all_to_all | solution.py:331
  52.8 9.0 %collective-permute-start.2 = (bf16[128,1024]{1,0:T(8,128)(2,1)S(1)}, bf16[128,1024]{1,0:T(8,128)(2,1)S(1)}, u32[]{:S(2)}, u32[]{:S(2)}) collective-permute-start(bf16[128,1024]{1,0:T(8,128)(2,1)S(1)} %collective-permute-done.refs_1_), channel_id=1, source_target_pairs={{0,32},{32,64},{64,96},{96,128},{128,160},{160,192},{192,224},{224... | collective-permute-start | bytes 786440 | tf_op jit(solution)/shard_map/ppermute | solution.py:293
  52.9 8.9 %collective-permute-start.3 = (bf16[128,1024]{1,0:T(8,128)(2,1)S(1)}, bf16[128,1024]{1,0:T(8,128)(2,1)S(1)}, u32[]{:S(2)}, u32[]{:S(2)}) collective-permute-start(bf16[128,1024]{1,0:T(8,128)(2,1)S(1)} %collective-permute-done.1.refs_2_), channel_id=1, source_target_pairs={{0,224},{32,0},{64,32},{96,64},{128,96},{160,128},{192,160},{224,1... | collective-permute-start | bytes 786440 | tf_op jit(solution)/shard_map/ppermute | solution.py:294
  61.7 8.0 %collective-permute-start.4 = (bf16[128,1024]{1,0:T(8,128)(2,1)S(1)}, bf16[128,1024]{1,0:T(8,128)(2,1)S(1)}, u32[]{:S(2)}, u32[]{:S(2)}) collective-permute-start(bf16[128,1024]{1,0:T(8,128)(2,1)S(1)} %collective-permute-done.2.refs_3_), channel_id=1, source_target_pairs={{0,32},{32,64},{64,96},{96,128},{128,160},{160,192},{192,224},{224... | collective-permute-start | bytes 786440 | tf_op jit(solution)/shard_map/ppermute | solution.py:293
  61.7 8.1 %collective-permute-start.5 = (bf16[128,1024]{1,0:T(8,128)(2,1)S(1)}, bf16[128,1024]{1,0:T(8,128)(2,1)S(1)}, u32[]{:S(2)}, u32[]{:S(2)}) collective-permute-start(bf16[128,1024]{1,0:T(8,128)(2,1)S(1)} %collective-permute-done.3.refs_4_), channel_id=1, source_target_pairs={{0,224},{32,0},{64,32},{96,64},{128,96},{160,128},{192,160},{224,1... | collective-permute-start | bytes 786440 | tf_op jit(solution)/shard_map/ppermute | solution.py:294
  69.7 5.1 %collective-permute-start.6 = (bf16[64,1024]{1,0:T(8,128)(2,1)S(1)}, bf16[64,1024]{1,0:T(8,128)(2,1)S(1)}, u32[]{:S(2)}, u32[]{:S(2)}) collective-permute-start(bf16[64,1024]{1,0:T(8,128)(2,1)S(1)} %slice.17), channel_id=1, source_target_pairs={{0,32},{32,64},{64,96},{96,128},{128,160},{160,192},{192,224},{224... | collective-permute-start | bytes 393224 | tf_op jit(solution)/shard_map/ppermute | solution.py:298
  69.8 5.0 %collective-permute-start.7 = (bf16[64,1024]{1,0:T(8,128)(2,1)S(1)}, bf16[64,1024]{1,0:T(8,128)(2,1)S(1)}, u32[]{:S(2)}, u32[]{:S(2)}) collective-permute-start(bf16[64,1024]{1,0:T(8,128)(2,1)S(1)} %slice.18), channel_id=1, source_target_pairs={{0,224},{32,0},{64,32},{96,64},{128,96},{160,128},{192,160},{224,1... | collective-permute-start | bytes 393224 | tf_op jit(solution)/shard_map/ppermute | solution.py:298
  74.8 10.5 %copy-start.6 = (s32[1,128,6]{1,0,2:T(1,128)S(1)}, s32[1,128,6]{1,0,2:T(1,128)}, u32[]{:S(2)}) copy-start(s32[1,128,6]{1,0,2:T(1,128)} %param.13) | copy-start | bytes 9220
  74.8 10.6 %copy-start.7 = (f32[1,128,6]{1,0,2:T(1,128)S(1)}, f32[1,128,6]{1,0,2:T(1,128)}, u32[]{:S(2)}) copy-start(f32[1,128,6]{1,0,2:T(1,128)} %param.14) | copy-start | bytes 9220
  74.8 20.0 %copy-start = (bf16[1,128,1024]{2,1,0:T(8,128)(2,1)S(1)}, bf16[1,128,1024]{2,1,0:T(8,128)(2,1)}, u32[]{:S(2)}) copy-start(bf16[1,128,1024]{2,1,0:T(8,128)(2,1)} %param.11) | copy-start | bytes 786436
  74.9 20.0 %copy-start.2 = (f32[1024]{0:T(1024)S(1)}, f32[1024]{0:T(1024)}, u32[]{:S(2)}) copy-start(f32[1024]{0:T(1024)} %param.16) | copy-start | bytes 12292
  80.4 14.4 %all-to-all-start.1 = ((bf16[8,128,128]{2,1,0:T(8,128)(2,1)}), bf16[8,128,128]{2,1,0:T(8,128)(2,1)S(1)}, u32[]{:S(2)}, u32[]{:S(2)}) async-start(bf16[8,128,128]{2,1,0:T(8,128)(2,1)} %attention.1), calls=%async_computation.1 | async-start | bytes 524288 | tf_op jit(solution)/shard_map/all_to_all | solution.py:336
  94.8 1.6 copy-start.1
  96.4 41.5 %copy-start.3 = (bf16[1,1024,2816]{2,1,0:T(8,128)(2,1)S(1)}, bf16[1,1024,2816]{2,1,0:T(8,128)(2,1)}, u32[]{:S(2)}) copy-start(bf16[1,1024,2816]{2,1,0:T(8,128)(2,1)} %param.20) | copy-start | bytes 17301508
  137.9 1.8 copy-start.4
Sparse Core Ops, SparseCore 0:
  31.8 57.5 all-gather.2

commit v2 on v1

v2 whole, which is shorter than its diff:
```python
import functools
import math

import jax
import jax.numpy as jnp
from jax import lax
from jax.experimental import pallas as pl
from jax.experimental.pallas import tpu as pltpu
from jax.sharding import PartitionSpec as P

F32 = jnp.float32
BF16 = jnp.bfloat16
MIB = 1 << 20
CAP = 32
EXTRA = 16
WIDE = 256


def vmem_spec():
    return pl.BlockSpec(memory_space=pltpu.VMEM)


def smem_spec():
    return pl.BlockSpec(memory_space=pltpu.SMEM)


def rms_scale(values, gain):
    wide = values.astype(F32)
    return wide * lax.rsqrt(jnp.mean(wide * wide, axis=-1, keepdims=True) + 1e-05) * gain


def slot_parts(shape, dim, cap):
    slot = lax.broadcasted_iota(jnp.int32, shape, dim)
    return slot // cap, lax.rem(slot, cap)


def pick_kernel(cap, ids_ref, pick_ref):
    topk, tok = ids_ref.shape
    slots = pick_ref.shape[0]
    experts = slots // cap
    named = jnp.zeros((experts, tok), F32)
    sub = lax.broadcasted_iota(jnp.int32, (experts, tok), 0)
    for route in range(topk):
        named = named + jnp.where(ids_ref[route : route + 1, :] == sub, 1.0, 0.0)
    row = lax.broadcasted_iota(jnp.int32, (tok, tok), 0)
    col = lax.broadcasted_iota(jnp.int32, (tok, tok), 1)
    before = jnp.where(row < col, 1.0, 0.0).astype(BF16)
    rank = jnp.dot(named.astype(BF16), before, preferred_element_type=F32)
    mine = jnp.where(named > 0.5, rank, -1.0).astype(BF16)
    expert_of, place_of = slot_parts((slots, experts), 0, cap)
    spread = jnp.where(
        lax.broadcasted_iota(jnp.int32, (slots, experts), 1) == expert_of, 1.0, 0.0
    ).astype(BF16)
    here = jnp.dot(spread, mine, preferred_element_type=F32) == place_of[:, 0:1].astype(F32)
    pick_ref[...] = jnp.where(here, 1.0, 0.0).astype(BF16)


def pick_table(ids, experts, cap):
    tok = ids.shape[0]
    return pl.pallas_call(
        functools.partial(pick_kernel, cap),
        out_shape=jax.ShapeDtypeStruct((experts * cap, tok), BF16),
        in_specs=[vmem_spec()],
        out_specs=vmem_spec(),
        compiler_params=pltpu.CompilerParams(vmem_limit_bytes=8 * MIB),
        cost_estimate=pl.CostEstimate(flops=10**8, bytes_accessed=10**6, transcendentals=0),
        name="pick_table",
    )(ids.T)


def gate_kernel(cap, ids_ref, weights_ref, high_ref, low_ref):
    tok, topk = ids_ref.shape
    slots = high_ref.shape[1]
    experts = slots // cap
    named = jnp.zeros((tok, experts), F32)
    gates = jnp.zeros((tok, experts), F32)
    lane = lax.broadcasted_iota(jnp.int32, (tok, experts), 1)
    for route in range(topk):
        hit = ids_ref[:, route : route + 1] == lane
        named = named + jnp.where(hit, 1.0, 0.0)
        gates = gates + jnp.where(hit, weights_ref[:, route : route + 1], 0.0)
    row = lax.broadcasted_iota(jnp.int32, (tok, tok), 0)
    col = lax.broadcasted_iota(jnp.int32, (tok, tok), 1)
    before = jnp.where(col < row, 1.0, 0.0).astype(BF16)
    rank = jnp.dot(before, named.astype(BF16), preferred_element_type=F32)
    expert_of, place_of = slot_parts((experts, slots), 1, cap)
    spread = jnp.where(
        lax.broadcasted_iota(jnp.int32, (experts, slots), 0) == expert_of, 1.0, 0.0
    ).astype(BF16)
    mine = jnp.where(named > 0.5, rank, -1.0).astype(BF16)
    here = jnp.dot(mine, spread, preferred_element_type=F32) == place_of[0:1, :].astype(F32)
    high = gates.astype(BF16)
    low = (gates - high.astype(F32)).astype(BF16)
    for part, ref in ((high, high_ref), (low, low_ref)):
        wide = jnp.dot(part, spread, preferred_element_type=F32)
        ref[...] = jnp.where(here, wide, 0.0).astype(BF16)


def gate_tables(ids, weights, experts, cap):
    tok = ids.shape[0]
    return pl.pallas_call(
        functools.partial(gate_kernel, cap),
        out_shape=[jax.ShapeDtypeStruct((tok, experts * cap), BF16)] * 2,
        in_specs=[vmem_spec()] * 2,
        out_specs=[vmem_spec()] * 2,
        compiler_params=pltpu.CompilerParams(vmem_limit_bytes=8 * MIB),
        cost_estimate=pl.CostEstimate(flops=10**8, bytes_accessed=10**6, transcendentals=0),
        name="gate_tables",
    )(ids, weights)


def attention_kernel(
    steps, me_ref, bias_ref, chain_ref, w_ref, *refs
):
    blocks, (out_ref, w_buf, q_buf, k_buf, v_buf) = refs[:-5], refs[-5:]
    me = me_ref[0]
    ring = len(steps)
    tok = out_ref.shape[1]
    head_dim = out_ref.shape[2]
    width = w_buf.shape[0]
    part = width // w_ref.shape[0]
    for i in range(3):
        w_buf[:, i * head_dim : (i + 1) * head_dim] = w_ref[:, i * part : (i + 1) * part].reshape(
            width, head_dim
        )
    start = 0
    for block in blocks:
        rows = block.shape[0]
        both = jnp.dot(block[...], w_buf[...], preferred_element_type=F32).astype(BF16)
        q_buf[start : start + rows] = both[:, :head_dim]
        k_buf[start : start + rows] = both[:, head_dim : 2 * head_dim]
        v_buf[start : start + rows] = both[:, 2 * head_dim :]
        start += rows
    owner = [lax.rem(me + (s + ring), ring) for s in steps]
    rows_of = [chain_ref[o] for o in owner]
    key_chain = jnp.concatenate(rows_of, axis=1)
    scale = 1.0 / math.sqrt(head_dim)
    bias = bias_ref[me]
    pair = 2
    for first in range(0, ring, pair):
        query_chain = jnp.concatenate(
            [
                jnp.broadcast_to(rows_of[first + j], (tok, tok)).T
                for j in range(pair)
            ],
            axis=0,
        )
        query_chain = jnp.concatenate([query_chain] * ring, axis=1)
        query = q_buf[first * tok : (first + pair) * tok]
        scores = (
            lax.dot_general(
                query, k_buf[...], (((1,), (1,)), ((), ())), preferred_element_type=F32
            )
            * scale
        )
        scores = scores + jnp.where(query_chain == key_chain, bias, 0.0)
        top = jnp.max(scores, axis=-1, keepdims=True)
        raised = jnp.exp(scores - top)
        probs = (raised * (1.0 / jnp.sum(raised, axis=-1, keepdims=True))).astype(BF16)
        mixed = jnp.dot(probs, v_buf[...], preferred_element_type=F32).astype(BF16)
        for j in range(pair):
            out_ref[owner[first + j]] = mixed[j * tok : (j + 1) * tok]


def attention(me, bias, chains, weights, blocks, steps):
    ring = len(steps)
    tok = chains.shape[2]
    head_dim = weights.shape[2]
    width = blocks[0].shape[1]
    length = ring * tok
    return pl.pallas_call(
        functools.partial(attention_kernel, steps),
        out_shape=jax.ShapeDtypeStruct((ring, tok, head_dim), BF16),
        in_specs=[smem_spec(), smem_spec()] + [vmem_spec()] * (2 + len(blocks)),
        out_specs=vmem_spec(),
        scratch_shapes=[
            pltpu.VMEM((width, 3 * head_dim), BF16),
            pltpu.VMEM((length, head_dim), BF16),
            pltpu.VMEM((length, head_dim), BF16),
            pltpu.VMEM((length, head_dim), BF16),
        ],
        compiler_params=pltpu.CompilerParams(vmem_limit_bytes=16 * MIB),
        cost_estimate=pl.CostEstimate(
            flops=1400 * 10**6, bytes_accessed=3 * 10**6, transcendentals=10**6
        ),
        name="attention",
    )(me, bias, chains, weights, *blocks)


def dispatch_kernel(
    core_ref, heads_ref, own_ref, other_ref, tokens_ref, gain_ref, pick_ref, mixed_ref, out_ref
):
    core = core_ref[0]
    half = heads_ref.shape[0] // 2
    width = tokens_ref.shape[1]
    mixed = tokens_ref[...].astype(F32)
    columns = own_ref.shape[1] // half
    for ref, side in ((own_ref, core), (other_ref, 1 - core)):
        local = jnp.concatenate([heads_ref[side * half + j] for j in range(half)], axis=1)
        w_out = jnp.concatenate(
            [
                ref[:, j * columns : (j + 1) * columns].reshape(width, heads_ref.shape[2])
                for j in range(half)
            ],
            axis=1,
        )
        mixed = mixed + lax.dot_general(
            local, w_out, (((1,), (1,)), ((), ())), preferred_element_type=F32
        )
    mixed_ref[...] = mixed
    ffn_in = (
        mixed * lax.rsqrt(jnp.mean(mixed * mixed, axis=-1, keepdims=True) + 1e-05) * gain_ref[...]
    ).astype(BF16)
    out_ref[...] = (
        jnp.dot(pick_ref[...], ffn_in, preferred_element_type=F32)
        .astype(BF16)
        .reshape(out_ref.shape)
    )


def dispatch(core, heads, own, other, tokens, gain, pick, experts, cap):
    tok, width = tokens.shape
    return pl.pallas_call(
        dispatch_kernel,
        out_shape=[
            jax.ShapeDtypeStruct((tok, width), F32),
            jax.ShapeDtypeStruct((experts, cap, width), BF16),
        ],
        in_specs=[smem_spec()] + [vmem_spec()] * 6,
        out_specs=[vmem_spec()] * 2,
        compiler_params=pltpu.CompilerParams(vmem_limit_bytes=16 * MIB),
        cost_estimate=pl.CostEstimate(
            flops=600 * 10**6, bytes_accessed=5 * 10**6, transcendentals=0
        ),
        name="dispatch",
    )(core, heads, own, other, tokens, gain.reshape(1, width), pick)


def expert_kernel(rows_ref, up_ref, down_ref, out_ref):
    hidden = down_ref.shape[0]
    rows = rows_ref[...]
    total = jnp.zeros(rows.shape, F32)
    for first in range(0, hidden, WIDE):
        last = min(first + WIDE, hidden)
        gate = jnp.dot(rows, up_ref[:, first:last], preferred_element_type=F32)
        value = jnp.dot(
            rows, up_ref[:, hidden + first : hidden + last], preferred_element_type=F32
        )
        active = (gate / (1.0 + jnp.exp(-gate)) * value).astype(BF16)
        total = total + jnp.dot(active, down_ref[first:last], preferred_element_type=F32)
    out_ref[...] = total.astype(BF16)


def run_expert(rows, w_gateup, w_down):
    count, width = rows.shape
    hidden = w_down.shape[0]
    return pl.pallas_call(
        expert_kernel,
        out_shape=jax.ShapeDtypeStruct((count, width), BF16),
        in_specs=[vmem_spec()] * 3,
        out_specs=vmem_spec(),
        compiler_params=pltpu.CompilerParams(vmem_limit_bytes=24 * MIB),
        cost_estimate=pl.CostEstimate(
            flops=6 * count * width * hidden, bytes_accessed=9 * 10**6, transcendentals=count * hidden
        ),
        name="experts",
    )(rows, w_gateup, w_down)


def combine_kernel(mixed_ref, high_ref, low_ref, back_ref, out_ref):
    rows = back_ref[...]
    total = mixed_ref[...] + jnp.dot(high_ref[...], rows, preferred_element_type=F32)
    total = total + jnp.dot(low_ref[...], rows, preferred_element_type=F32)
    out_ref[...] = total.astype(BF16)


def combine(mixed, high, low, back):
    return pl.pallas_call(
        combine_kernel,
        out_shape=jax.ShapeDtypeStruct(mixed.shape, BF16),
        in_specs=[vmem_spec()] * 4,
        out_specs=vmem_spec(),
        compiler_params=pltpu.CompilerParams(vmem_limit_bytes=16 * MIB),
        cost_estimate=pl.CostEstimate(
            flops=540 * 10**6, bytes_accessed=4 * 10**6, transcendentals=0
        ),
        name="combine",
    )(mixed, high, low, back)


def ring_gather(block, axis):
    size = lax.axis_size(axis)
    up = [(i, (i + 1) % size) for i in range(size)]
    down = [(i, (i - 1) % size) for i in range(size)]
    blocks, steps = [block], [0]
    forth = back = block
    for step in range(1, size // 2):
        forth = lax.ppermute(forth, axis, up)
        back = lax.ppermute(back, axis, down)
        blocks += [forth, back]
        steps += [-step, step]
    half = block.shape[0] // 2
    blocks += [lax.ppermute(forth[:half], axis, up), lax.ppermute(back[half:], axis, down)]
    steps += [size // 2]
    return blocks, steps


def per_device(
    tokens,
    chain_ids,
    route_ids,
    route_weights,
    attn_gain,
    ffn_gain,
    chain_bias,
    w_qkv,
    w_out,
    w_gateup,
    w_down,
):
    inputs = tokens[0]
    tok, width = inputs.shape
    ring = lax.axis_size("ctx")
    experts = lax.axis_size("expert")
    me = lax.axis_index("ctx").astype(jnp.int32).reshape(1)
    core = lax.rem(lax.axis_index("expert").astype(jnp.int32), 2).reshape(1)
    columns = w_out.shape[1]
    head_dim = tok

    normed = rms_scale(inputs, attn_gain).astype(BF16)
    small = jnp.concatenate(
        [w_out.T, chain_ids.astype(BF16), jnp.zeros((EXTRA - 1, tok), BF16)], axis=0
    )
    small, normed = lax.optimization_barrier((small, normed))
    small = lax.all_to_all(
        jnp.broadcast_to(small[None], (ring,) + small.shape), "ctx", 0, 0, tiled=True
    )
    chains = small[:, columns : columns + 1].astype(F32)

    blocks, steps = ring_gather(normed, "ctx")

    w_rows = small[:, :columns].reshape(2, -1, head_dim)
    mine = w_qkv.reshape(1, -1, head_dim)
    mine, blocks[1], blocks[2] = lax.optimization_barrier((mine, blocks[1], blocks[2]))
    both = jnp.concatenate([jnp.broadcast_to(mine, (2,) + mine.shape[1:]), w_rows], axis=1)
    plane = lax.all_to_all(
        jnp.broadcast_to(both[None], (experts // 2,) + both.shape).reshape(
            (experts,) + both.shape[1:]
        ),
        "expert",
        0,
        0,
        tiled=True,
    )
    plane, blocks[-2], blocks[-1] = lax.optimization_barrier((plane, blocks[-2], blocks[-1]))
    w_head = plane[:, : mine.shape[1]]

    pick = pick_table(route_ids[0], experts, CAP)
    high, low = gate_tables(route_ids[0], route_weights[0], experts, CAP)
    attended = attention(me, chain_bias, chains, w_head, blocks, steps)
    plane, attended = lax.optimization_barrier((plane, attended))
    own = plane[:, mine.shape[1] :]
    other = lax.ppermute(own, "expert", [(i, i ^ 1) for i in range(experts)])
    heads = lax.all_to_all(attended, "ctx", split_axis=0, concat_axis=0, tiled=True)
    pick, high, low = lax.optimization_barrier((pick, high, low))
    mixed, outgoing = dispatch(core, heads, own, other, inputs, ffn_gain, pick, experts, CAP)
    arrived = lax.all_to_all(outgoing, "expert", split_axis=0, concat_axis=0, tiled=True)
    result = run_expert(arrived.reshape(-1, width), w_gateup[0], w_down[0])
    back = lax.all_to_all(
        result.reshape(arrived.shape), "expert", split_axis=0, concat_axis=0, tiled=True
    )
    return combine(mixed, high, low, back.reshape(-1, width))[None]


def solution(mesh):
    placed = (
        P("expert", "ctx", None),
        P("expert", "ctx"),
        P("expert", "ctx", None),
        P("expert", "ctx", None),
        P(),
        P(),
        P(),
        P(None, "expert", "ctx"),
        P("ctx", "expert"),
        P("expert", None, None),
        P("expert", None, None),
    )
    return jax.shard_map(
        per_device, mesh=mesh, in_specs=placed, out_specs=P("expert", "ctx", None), check_vma=False
    )
```

time: 193 us -> 169 us (0.88)
  blocking collectives: 94.8 us -> 79.2 us
  between operations: 13.5 us -> 0.17 us
  waiting for transfers between devices: 22.1 us -> 27.6 us
  Pallas kernels: 21.9 us -> 19.6 us
    all_gather x1 -> x0, blocking collectives: 22.9 us -> none  [per_device(): small = lax.all_gather(small, 'ctx', axis=0)]
    all_to_all x1 -> x2, blocking collectives: 39.9 us -> 47.2 us  [the longest x1 34.7 us: per_device(): lax.all_to_all(outgoing, 'expert', split_axis=0, concat_axis=0, tiled=True)]
    all_to_all x1, starting transfers between devices: 14.4 us -> 9.93 us  [per_device(): lax.all_to_all(jnp.broadcast_to(both[None], (experts // 2,) + both.shape)...]
    all_to_all x1, waiting for transfers between devices: 8.31 us -> 11 us  [per_device(): lax.all_to_all(attended, 'ctx', split_axis=0, concat_axis=0, tiled=True)]
    all_to_all x1, waiting for transfers between devices: 0.01 us -> 2.64 us  [per_device(): lax.all_to_all(jnp.broadcast_to(both[None], (experts // 2,) + both.shape)...]
    slice x0 -> x3, local copies, waits for them, and re-layouts: none -> 2.54 us  [the longest x1 1.35 us: per_device(): own = plane[:, mine.shape[1]:]]
    pallas_call x1, Pallas kernels: 12.5 us -> 9.98 us  [run_expert(): pl.pallas_call(expert_kernel, out_shape=jax.ShapeDtypeStruct((count, widt...]
    ppermute x0 -> x1, starting transfers between devices: none -> 2.35 us  [per_device(): other = lax.ppermute(own, 'expert', [(i, i ^ 1) for i in range(experts)])]
  transfers between devices with their start and end apart: 11 -> 11, of which waited for: 4 -> 5; matrix products, arithmetic and copies ran while one was open for 2% -> 0% of each run, Pallas kernels for 3% -> 1%
where the time goes in v2:
time: 169 us
  blocking collectives  79.2 us (47%)
  starting transfers between devices  30.6 us (18%)
  waiting for transfers between devices  27.6 us (16%)
  Pallas kernels  19.6 us (12%)
  local copies, waits for them, and re-layouts  7.87 us (5%)
  other arithmetic  3.64 us (2%)
    all_to_all x1, blocking collectives, per_device(): lax.all_to_all(outgoing, 'expert', split_axis=0, concat_axis=0, tiled=True)  34.7 us
    all_to_all x1, blocking collectives, per_device(): lax.all_to_all(result.reshape(arrived.shape), 'expert', split_axis=0, con...  31.9 us
    all_to_all x1, blocking collectives, per_device(): lax.all_to_all(jnp.broadcast_to(small[None], (ring,) + small.shape), 'ctx...  12.6 us
    ppermute x3, waiting for transfers between devices, ring_gather(): forth = lax.ppermute(forth, axis, up)  11.6 us
    all_to_all x1, waiting for transfers between devices, per_device(): lax.all_to_all(attended, 'ctx', split_axis=0, concat_axis=0, tiled=True)  11 us
    pallas_call x1, Pallas kernels, run_expert(): pl.pallas_call(expert_kernel, out_shape=jax.ShapeDtypeStruct((count, widt...  9.98 us
    all_to_all x1, starting transfers between devices, per_device(): lax.all_to_all(jnp.broadcast_to(both[None], (experts // 2,) + both.shape)...  9.93 us
    ppermute x3, starting transfers between devices, ring_gather(): back = lax.ppermute(back, axis, down)  9.1 us
  transfers between devices with their start and end apart: 11, of which 5 were waited for; matrix products, arithmetic and copies ran while one was open for 0% of the time, Pallas kernels for 1%

profile of v2, /device:TPU:1, one launch (start us, length us, event | category | flops | bytes accessed | tf_op | source)
XLA Modules:
  0.0 168.7 jit_solution(2151095445007653907)
XLA Ops:
  0.0 1.1 fusion
  1.1 0.7 convert_element_type.12
  1.8 1.1 fusion.2.refs_0_
  2.9 0.1 pad.4.clone
  2.9 0.8 maximum_maximum_fusion
  3.7 2.5 %collective-permute-start = (bf16[128,1024]{1,0:T(8,128)(2,1)S(1)}, bf16[128,1024]{1,0:T(8,128)(2,1)S(1)}, u32[]{:S(2)}, u32[]{:S(2)}) collective-permute-start(bf16[128,1024]{1,0:T(8,128)(2,1)S(1)} %fusion.2.refs_0_), channel_id=1, source_target_pairs={{0,32},{32,64},{64,96},{96,128},{128,160},{160,192},{192,224},{224... | collective-permute-start | bytes 786440 | tf_op jit(solution)/shard_map/ppermute | solution.py:298
  6.2 4.0 %collective-permute-start.1 = (bf16[128,1024]{1,0:T(8,128)(2,1)S(1)}, bf16[128,1024]{1,0:T(8,128)(2,1)S(1)}, u32[]{:S(2)}, u32[]{:S(2)}) collective-permute-start(bf16[128,1024]{1,0:T(8,128)(2,1)S(1)} %fusion.2.refs_0_), channel_id=1, source_target_pairs={{0,224},{32,0},{64,32},{96,64},{128,96},{160,128},{192,160},{224,1... | collective-permute-start | bytes 786440 | tf_op jit(solution)/shard_map/ppermute | solution.py:299
  10.2 12.6 %all_to_all.25 = bf16[8,48,128]{2,1,0:T(8,128)(2,1)S(1)} all-to-all(bf16[8,48,128]{2,1,0:T(8,128)(2,1)S(1)} %broadcast_in_dim.30), channel_id=1, replica_groups=mesh['ctx'=8,'expert'=32] {'ctx'}, dimensions={0} | all-to-all | bytes 196608 | tf_op jit(solution)/shard_map/all_to_all | solution.py:335
  22.8 0.0 collective-permute-done.refs_1_
  22.8 0.0 collective-permute-done.1.refs_2_
  22.8 0.7 broadcast_in_dim.14
  23.6 1.6 broadcast_in_dim.31
  25.2 9.9 %all-to-all-start.1 = ((bf16[32,224,128]{2,1,0:T(8,128)(2,1)}), bf16[32,224,128]{2,1,0:T(8,128)(2,1)}, u32[]{:S(2)}, u32[]{:S(2)}) async-start(bf16[32,224,128]{2,1,0:T(8,128)(2,1)} %bitcast.6), calls=%async_computation.1 | async-start | bytes 3670016 | tf_op jit(solution)/shard_map/all_to_all | solution.py:346
  35.1 0.4 collective-permute-start.2
  35.5 2.4 %collective-permute-start.5 = (bf16[128,1024]{1,0:T(8,128)(2,1)S(1)}, bf16[128,1024]{1,0:T(8,128)(2,1)S(1)}, u32[]{:S(2)}, u32[]{:S(2)}) collective-permute-start(bf16[128,1024]{1,0:T(8,128)(2,1)S(1)} %collective-permute-done.1.refs_2_), channel_id=1, source_target_pairs={{0,224},{32,0},{64,32},{96,64},{128,96},{160,128},{192,160},{224,1... | collective-permute-start | bytes 786440 | tf_op jit(solution)/shard_map/ppermute | solution.py:299
  37.9 6.2 %collective-permute-done.2.refs_3_ = bf16[128,1024]{1,0:T(8,128)(2,1)S(1)} collective-permute-done((bf16[128,1024]{1,0:T(8,128)(2,1)S(1)}, bf16[128,1024]{1,0:T(8,128)(2,1)S(1)}, u32[]{:S(2)}, u32[]{:S(2)}) %collective-permute-start.2) | collective-permute-done | bytes 262176 | tf_op jit(solution)/shard_map/ppermute | solution.py:298
  44.1 0.0 collective-permute-start.3
  44.1 0.0 collective-permute-done.5.refs_4_
  44.1 2.7 %collective-permute-start.6 = (bf16[128,1024]{1,0:T(8,128)(2,1)S(1)}, bf16[128,1024]{1,0:T(8,128)(2,1)S(1)}, u32[]{:S(2)}, u32[]{:S(2)}) collective-permute-start(bf16[128,1024]{1,0:T(8,128)(2,1)S(1)} %collective-permute-done.5.refs_4_), channel_id=1, source_target_pairs={{0,224},{32,0},{64,32},{96,64},{128,96},{160,128},{192,160},{224,1... | collective-permute-start | bytes 786440 | tf_op jit(solution)/shard_map/ppermute | solution.py:299
  46.8 5.3 %collective-permute-done.3.refs_5_ = bf16[128,1024]{1,0:T(8,128)(2,1)S(1)} collective-permute-done((bf16[128,1024]{1,0:T(8,128)(2,1)S(1)}, bf16[128,1024]{1,0:T(8,128)(2,1)S(1)}, u32[]{:S(2)}, u32[]{:S(2)}) %collective-permute-start.3) | collective-permute-done | bytes 262176 | tf_op jit(solution)/shard_map/ppermute | solution.py:298
  52.1 0.1 collective-permute-start.4
  52.2 0.0 collective-permute-done.6.refs_6_
  52.3 2.7 %collective-permute-start.7 = (bf16[64,1024]{1,0:T(8,128)(2,1)S(1)}, bf16[64,1024]{1,0:T(8,128)(2,1)S(1)}, u32[]{:S(2)}, u32[]{:S(2)}) collective-permute-start(bf16[64,1024]{1,0:T(8,128)(2,1)S(1)} %slice.26), channel_id=1, source_target_pairs={{0,224},{32,0},{64,32},{96,64},{128,96},{160,128},{192,160},{224,1... | collective-permute-start | bytes 393224 | tf_op jit(solution)/shard_map/ppermute | solution.py:303
  55.0 2.4 %collective-permute-done.4.refs_7_ = bf16[64,1024]{1,0:T(8,128)(2,1)S(1)} collective-permute-done((bf16[64,1024]{1,0:T(8,128)(2,1)S(1)}, bf16[64,1024]{1,0:T(8,128)(2,1)S(1)}, u32[]{:S(2)}, u32[]{:S(2)}) %collective-permute-start.4) | collective-permute-done | bytes 131104 | tf_op jit(solution)/shard_map/ppermute | solution.py:303
  57.4 0.0 collective-permute-done.7.refs_8_
  57.4 2.6 %all-to-all-done.1 = bf16[32,224,128]{2,1,0:T(8,128)(2,1)} async-done(((bf16[32,224,128]{2,1,0:T(8,128)(2,1)}), bf16[32,224,128]{2,1,0:T(8,128)(2,1)}, u32[]{:S(2)}, u32[]{:S(2)}) %all-to-all-start.1) | async-done | bytes 1835040 | tf_op jit(solution)/shard_map/all_to_all | solution.py:346
  60.1 1.2 slice.22.w_ref
  61.3 0.0 copy-done.4
  61.3 5.5 %attention.1 = bf16[8,128,128]{2,1,0:T(8,128)(2,1)} custom-call(s32[1]{0:T(128)} %bitcast.7.me_ref, f32[8]{0:T(128)S(1)} %copy-done.4, f32[8,1,128]{2,1,0:T(1,128)S(1)} %slice_convert_fusion.chain_ref, bf16[32,96,128]{2,1,0:T(8,128)(2,1)S(1)} %slice.22.w_ref, bf16[128,1024]{1,0:T(8,128)(2,1)S(1)} %fusion.2.refs_0_, ...), custom_call_target="tpu_custom_call" | custom-call | flops 1400000000 | bytes 3000000 | tf_op jit(solution)/shard_map/attention/pallas_call | solution.py:171
  66.8 1.3 slice.23.own_ref
  68.2 2.3 %collective-permute-start.8 = (bf16[32,128,128]{2,1,0:T(8,128)(2,1)S(1)}, bf16[32,128,128]{2,1,0:T(8,128)(2,1)S(1)}, u32[]{:S(2)}, u32[]{:S(2)}) collective-permute-start(bf16[32,128,128]{2,1,0:T(8,128)(2,1)S(1)} %slice.23.own_ref), channel_id=1, source_target_pairs={{0,1},{1,0},{2,3},{3,2},{4,5},{5,4},{6,7},{7,6},{8,9},{9,8},{10,11... | collective-permute-start | bytes 3145736 | tf_op jit(solution)/shard_map/ppermute | solution.py:363
  70.5 3.6 %all-to-all-start.2 = ((bf16[8,128,128]{2,1,0:T(8,128)(2,1)}), bf16[8,128,128]{2,1,0:T(8,128)(2,1)S(1)}, u32[]{:S(2)}, u32[]{:S(2)}) async-start(bf16[8,128,128]{2,1,0:T(8,128)(2,1)} %attention.1), calls=%async_computation.2 | async-start | bytes 524288 | tf_op jit(solution)/shard_map/all_to_all | solution.py:364
  74.1 0.0 copy-done.5
  74.1 0.1 copy.12
  74.3 0.0 copy-done.6
  74.3 0.1 copy.14
  74.4 0.4 pick_table.1.pick_ref
  74.7 0.7 gate_tables.1
  75.5 11.0 %all-to-all-done.2.heads_ref = bf16[8,128,128]{2,1,0:T(8,128)(2,1)S(1)} async-done(((bf16[8,128,128]{2,1,0:T(8,128)(2,1)}), bf16[8,128,128]{2,1,0:T(8,128)(2,1)S(1)}, u32[]{:S(2)}, u32[]{:S(2)}) %all-to-all-start.2) | async-done | bytes 262176 | tf_op jit(solution)/shard_map/all_to_all | solution.py:364
  86.4 0.0 collective-permute-done.8.other_ref
  86.4 0.0 copy-done
  86.4 1.6 dispatch.1
  88.0 0.0 copy-start.3
  88.0 34.7 %all_to_all.26 = bf16[32,32,1024]{2,1,0:T(8,128)(2,1)S(1)} all-to-all(bf16[32,32,1024]{2,1,0:T(8,128)(2,1)S(1)} %get-tuple-element.38), channel_id=1, replica_groups=mesh['ctx'=8,'expert'=32] {'expert'}, dimensions={0} | all-to-all | bytes 4194304 | tf_op jit(solution)/shard_map/all_to_all | solution.py:367
  122.7 2.6 %copy-done.2 = bf16[1,1024,2816]{2,1,0:T(8,128)(2,1)S(1)} copy-done((bf16[1,1024,2816]{2,1,0:T(8,128)(2,1)S(1)}, bf16[1,1024,2816]{2,1,0:T(8,128)(2,1)}, u32[]{:S(2)}) %copy-start.2) | copy-done | bytes 5767192
  125.3 10.0 %experts.1 = bf16[1024,1024]{1,0:T(8,128)(2,1)S(1)} custom-call(bf16[1024,1024]{1,0:T(8,128)(2,1)S(1)} %bitcast.25, bf16[1024,2816]{1,0:T(8,128)(2,1)S(1)} %bitcast.31, bf16[1408,1024]{1,0:T(8,128)(2,1)S(1)} %bitcast.32), custom_call_target="tpu_custom_call" | custom-call | flops 8858370048 | bytes 9000000 | tf_op jit(solution)/shard_map/experts/pallas_call | solution.py:257
  135.3 31.9 %all_to_all.27 = bf16[32,32,1024]{2,1,0:T(8,128)(2,1)S(1)} all-to-all(bf16[32,32,1024]{2,1,0:T(8,128)(2,1)S(1)} %bitcast.26), channel_id=1, replica_groups=mesh['ctx'=8,'expert'=32] {'expert'}, dimensions={0} | all-to-all | bytes 4194304 | tf_op jit(solution)/shard_map/all_to_all | solution.py:369
  167.2 1.4 combine.1
  (17 shorter events, 0.1 us)
Async XLA Ops:
  3.7 19.1 %collective-permute-start = (bf16[128,1024]{1,0:T(8,128)(2,1)S(1)}, bf16[128,1024]{1,0:T(8,128)(2,1)S(1)}, u32[]{:S(2)}, u32[]{:S(2)}) collective-permute-start(bf16[128,1024]{1,0:T(8,128)(2,1)S(1)} %fusion.2.refs_0_), channel_id=1, source_target_pairs={{0,32},{32,64},{64,96},{96,128},{128,160},{160,192},{192,224},{224... | collective-permute-start | bytes 786440 | tf_op jit(solution)/shard_map/ppermute | solution.py:298
  6.2 16.6 %collective-permute-start.1 = (bf16[128,1024]{1,0:T(8,128)(2,1)S(1)}, bf16[128,1024]{1,0:T(8,128)(2,1)S(1)}, u32[]{:S(2)}, u32[]{:S(2)}) collective-permute-start(bf16[128,1024]{1,0:T(8,128)(2,1)S(1)} %fusion.2.refs_0_), channel_id=1, source_target_pairs={{0,224},{32,0},{64,32},{96,64},{128,96},{160,128},{192,160},{224,1... | collective-permute-start | bytes 786440 | tf_op jit(solution)/shard_map/ppermute | solution.py:299
  25.2 36.1 %copy-start.4 = (f32[8]{0:T(128)S(1)}, f32[8]{0:T(128)}, u32[]{:S(2)}) copy-start(f32[8]{0:T(128)} %bias_ref.1) | copy-start | bytes 100
  25.2 34.9 %all-to-all-start.1 = ((bf16[32,224,128]{2,1,0:T(8,128)(2,1)}), bf16[32,224,128]{2,1,0:T(8,128)(2,1)}, u32[]{:S(2)}, u32[]{:S(2)}) async-start(bf16[32,224,128]{2,1,0:T(8,128)(2,1)} %bitcast.6), calls=%async_computation.1 | async-start | bytes 3670016 | tf_op jit(solution)/shard_map/all_to_all | solution.py:346
  35.1 9.0 %collective-permute-start.2 = (bf16[128,1024]{1,0:T(8,128)(2,1)S(1)}, bf16[128,1024]{1,0:T(8,128)(2,1)S(1)}, u32[]{:S(2)}, u32[]{:S(2)}) collective-permute-start(bf16[128,1024]{1,0:T(8,128)(2,1)S(1)} %collective-permute-done.refs_1_), channel_id=1, source_target_pairs={{0,32},{32,64},{64,96},{96,128},{128,160},{160,192},{192,224},{224... | collective-permute-start | bytes 786440 | tf_op jit(solution)/shard_map/ppermute | solution.py:298
  35.5 8.6 %collective-permute-start.5 = (bf16[128,1024]{1,0:T(8,128)(2,1)S(1)}, bf16[128,1024]{1,0:T(8,128)(2,1)S(1)}, u32[]{:S(2)}, u32[]{:S(2)}) collective-permute-start(bf16[128,1024]{1,0:T(8,128)(2,1)S(1)} %collective-permute-done.1.refs_2_), channel_id=1, source_target_pairs={{0,224},{32,0},{64,32},{96,64},{128,96},{160,128},{192,160},{224,1... | collective-permute-start | bytes 786440 | tf_op jit(solution)/shard_map/ppermute | solution.py:299
  44.1 8.0 %collective-permute-start.3 = (bf16[128,1024]{1,0:T(8,128)(2,1)S(1)}, bf16[128,1024]{1,0:T(8,128)(2,1)S(1)}, u32[]{:S(2)}, u32[]{:S(2)}) collective-permute-start(bf16[128,1024]{1,0:T(8,128)(2,1)S(1)} %collective-permute-done.2.refs_3_), channel_id=1, source_target_pairs={{0,32},{32,64},{64,96},{96,128},{128,160},{160,192},{192,224},{224... | collective-permute-start | bytes 786440 | tf_op jit(solution)/shard_map/ppermute | solution.py:298
  44.1 8.1 %collective-permute-start.6 = (bf16[128,1024]{1,0:T(8,128)(2,1)S(1)}, bf16[128,1024]{1,0:T(8,128)(2,1)S(1)}, u32[]{:S(2)}, u32[]{:S(2)}) collective-permute-start(bf16[128,1024]{1,0:T(8,128)(2,1)S(1)} %collective-permute-done.5.refs_4_), channel_id=1, source_target_pairs={{0,224},{32,0},{64,32},{96,64},{128,96},{160,128},{192,160},{224,1... | collective-permute-start | bytes 786440 | tf_op jit(solution)/shard_map/ppermute | solution.py:299
  52.1 5.3 %collective-permute-start.4 = (bf16[64,1024]{1,0:T(8,128)(2,1)S(1)}, bf16[64,1024]{1,0:T(8,128)(2,1)S(1)}, u32[]{:S(2)}, u32[]{:S(2)}) collective-permute-start(bf16[64,1024]{1,0:T(8,128)(2,1)S(1)} %slice.25), channel_id=1, source_target_pairs={{0,32},{32,64},{64,96},{96,128},{128,160},{160,192},{192,224},{224... | collective-permute-start | bytes 393224 | tf_op jit(solution)/shard_map/ppermute | solution.py:303
  52.3 5.2 %collective-permute-start.7 = (bf16[64,1024]{1,0:T(8,128)(2,1)S(1)}, bf16[64,1024]{1,0:T(8,128)(2,1)S(1)}, u32[]{:S(2)}, u32[]{:S(2)}) collective-permute-start(bf16[64,1024]{1,0:T(8,128)(2,1)S(1)} %slice.26), channel_id=1, source_target_pairs={{0,224},{32,0},{64,32},{96,64},{128,96},{160,128},{192,160},{224,1... | collective-permute-start | bytes 393224 | tf_op jit(solution)/shard_map/ppermute | solution.py:303
  66.8 7.3 %copy-start.5 = (s32[1,128,6]{1,0,2:T(1,128)S(1)}, s32[1,128,6]{1,0,2:T(1,128)}, u32[]{:S(2)}) copy-start(s32[1,128,6]{1,0,2:T(1,128)} %param.13) | copy-start | bytes 9220
  66.8 7.4 %copy-start.6 = (f32[1,128,6]{1,0,2:T(1,128)S(1)}, f32[1,128,6]{1,0,2:T(1,128)}, u32[]{:S(2)}) copy-start(f32[1,128,6]{1,0,2:T(1,128)} %param.14) | copy-start | bytes 9220
  66.8 19.6 %copy-start = (bf16[1,128,1024]{2,1,0:T(8,128)(2,1)S(1)}, bf16[1,128,1024]{2,1,0:T(8,128)(2,1)}, u32[]{:S(2)}) copy-start(bf16[1,128,1024]{2,1,0:T(8,128)(2,1)} %param.11) | copy-start | bytes 786436
  66.8 19.6 %copy-start.1 = (f32[1024]{0:T(1024)S(1)}, f32[1024]{0:T(1024)}, u32[]{:S(2)}) copy-start(f32[1024]{0:T(1024)} %param.16) | copy-start | bytes 12292
  68.2 18.3 %collective-permute-start.8 = (bf16[32,128,128]{2,1,0:T(8,128)(2,1)S(1)}, bf16[32,128,128]{2,1,0:T(8,128)(2,1)S(1)}, u32[]{:S(2)}, u32[]{:S(2)}) collective-permute-start(bf16[32,128,128]{2,1,0:T(8,128)(2,1)S(1)} %slice.23.own_ref), channel_id=1, source_target_pairs={{0,1},{1,0},{2,3},{3,2},{4,5},{5,4},{6,7},{7,6},{8,9},{9,8},{10,11... | collective-permute-start | bytes 3145736 | tf_op jit(solution)/shard_map/ppermute | solution.py:363
  70.5 15.9 %all-to-all-start.2 = ((bf16[8,128,128]{2,1,0:T(8,128)(2,1)}), bf16[8,128,128]{2,1,0:T(8,128)(2,1)S(1)}, u32[]{:S(2)}, u32[]{:S(2)}) async-start(bf16[8,128,128]{2,1,0:T(8,128)(2,1)} %attention.1), calls=%async_computation.2 | async-start | bytes 524288 | tf_op jit(solution)/shard_map/all_to_all | solution.py:364
  88.0 34.7 %copy-start.3 = (bf16[1,1408,1024]{2,1,0:T(8,128)(2,1)S(1)}, bf16[1,1408,1024]{2,1,0:T(8,128)(2,1)}, u32[]{:S(2)}) copy-start(bf16[1,1408,1024]{2,1,0:T(8,128)(2,1)} %param.21) | copy-start | bytes 8650756
  122.7 2.6 %copy-start.2 = (bf16[1,1024,2816]{2,1,0:T(8,128)(2,1)S(1)}, bf16[1,1024,2816]{2,1,0:T(8,128)(2,1)}, u32[]{:S(2)}) copy-start(bf16[1,1024,2816]{2,1,0:T(8,128)(2,1)} %param.20) | copy-start | bytes 17301508

commit v3 on v2

--- a/solution.py
+++ b/solution.py
@@ -13,6 +13,7 @@
 MIB = 1 << 20
 CAP = 32
 EXTRA = 16
+CHAINS = 8
 WIDE = 256
 
 
@@ -24,9 +25,69 @@
     return pl.BlockSpec(memory_space=pltpu.SMEM)
 
 
-def rms_scale(values, gain):
-    wide = values.astype(F32)
-    return wide * lax.rsqrt(jnp.mean(wide * wide, axis=-1, keepdims=True) + 1e-05) * gain
+def start_kernel(tokens_ref, gain_ref, w_ref, chain_ref, normed_ref, small_ref):
+    wide = tokens_ref[...].astype(F32)
+    normed_ref[...] = (
+        wide * lax.rsqrt(jnp.mean(wide * wide, axis=-1, keepdims=True) + 1e-05) * gain_ref[...]
+    ).astype(BF16)
+    columns = w_ref.shape[0]
+    chains = jnp.broadcast_to(chain_ref[...].astype(F32), (EXTRA, w_ref.shape[1])).astype(BF16)
+    for i in range(small_ref.shape[0]):
+        small_ref[i, :columns] = w_ref[...]
+        small_ref[i, columns:] = chains
+
+
+def start(tokens, gain, w_out, chain_ids, ring):
+    tok, width = tokens.shape
+    columns = w_out.shape[1]
+    return pl.pallas_call(
+        start_kernel,
+        out_shape=[
+            jax.ShapeDtypeStruct((tok, width), BF16),
+            jax.ShapeDtypeStruct((ring, columns + EXTRA, tok), BF16),
+        ],
+        in_specs=[vmem_spec()] * 4,
+        out_specs=[vmem_spec()] * 2,
+        compiler_params=pltpu.CompilerParams(vmem_limit_bytes=60 * MIB),
+        cost_estimate=pl.CostEstimate(flops=10**6, bytes_accessed=10**6, transcendentals=0),
+        name="start",
+    )(tokens, gain.reshape(1, width), w_out.T, chain_ids)
+
+
+def plane_kernel(small_ref, w_ref, plane_ref, chain_ref, parts, left):
+    ring, rows, _ = small_ref.shape
+    columns = rows - EXTRA
+    own, half = w_ref.shape[0], ring // 2
+    chain_ref[...] = small_ref[:, columns:].astype(F32)[:, 0:1]
+    copies = []
+    for core in range(2):
+        parts[core, :own] = w_ref[...]
+        for j in range(half):
+            first = own + j * columns
+            parts[core, first : first + columns] = small_ref[core * half + j, :columns]
+        for i in range(core, plane_ref.shape[0], 2):
+            copies.append(pltpu.make_async_copy(parts.at[core], plane_ref.at[i], left.at[i]))
+            copies[-1].start()
+    for copy in copies:
+        copy.wait()
+
+
+def plane_parts(small, w_head, experts):
+    ring, rows, lanes = small.shape
+    count = w_head.shape[0] + ring // 2 * (rows - EXTRA)
+    return pl.pallas_call(
+        plane_kernel,
+        out_shape=[
+            jax.ShapeDtypeStruct((experts, count, lanes), BF16),
+            jax.ShapeDtypeStruct((ring, 1, lanes), F32),
+        ],
+        in_specs=[vmem_spec()] * 2,
+        out_specs=[pl.BlockSpec(memory_space=pltpu.HBM), vmem_spec()],
+        scratch_shapes=[pltpu.VMEM((2, count, lanes), BF16), pltpu.SemaphoreType.DMA((experts,))],
+        compiler_params=pltpu.CompilerParams(vmem_limit_bytes=60 * MIB),
+        cost_estimate=pl.CostEstimate(flops=10**6, bytes_accessed=2 * 10**6, transcendentals=0),
+        name="plane_parts",
+    )(small, w_head)
 
 
 def slot_parts(shape, dim, cap):
@@ -68,9 +129,9 @@
     )(ids.T)
 
 
-def gate_kernel(cap, ids_ref, weights_ref, high_ref, low_ref):
+def gate_kernel(cap, ids_ref, weights_ref, gate_ref):
     tok, topk = ids_ref.shape
-    slots = high_ref.shape[1]
+    slots = gate_ref.shape[1]
     experts = slots // cap
     named = jnp.zeros((tok, experts), F32)
     gates = jnp.zeros((tok, experts), F32)
@@ -91,27 +152,25 @@
     here = jnp.dot(mine, spread, preferred_element_type=F32) == place_of[0:1, :].astype(F32)
     high = gates.astype(BF16)
     low = (gates - high.astype(F32)).astype(BF16)
-    for part, ref in ((high, high_ref), (low, low_ref)):
+    for i, part in enumerate((high, low)):
         wide = jnp.dot(part, spread, preferred_element_type=F32)
-        ref[...] = jnp.where(here, wide, 0.0).astype(BF16)
+        gate_ref[i * tok : (i + 1) * tok] = jnp.where(here, wide, 0.0).astype(BF16)
 
 
 def gate_tables(ids, weights, experts, cap):
     tok = ids.shape[0]
     return pl.pallas_call(
         functools.partial(gate_kernel, cap),
-        out_shape=[jax.ShapeDtypeStruct((tok, experts * cap), BF16)] * 2,
+        out_shape=jax.ShapeDtypeStruct((2 * tok, experts * cap), BF16),
         in_specs=[vmem_spec()] * 2,
-        out_specs=[vmem_spec()] * 2,
+        out_specs=vmem_spec(),
         compiler_params=pltpu.CompilerParams(vmem_limit_bytes=8 * MIB),
         cost_estimate=pl.CostEstimate(flops=10**8, bytes_accessed=10**6, transcendentals=0),
         name="gate_tables",
     )(ids, weights)
 
 
-def attention_kernel(
-    steps, me_ref, bias_ref, chain_ref, w_ref, *refs
-):
+def attention_kernel(steps, me_ref, bias_ref, chain_ref, w_ref, *refs):
     blocks, (out_ref, w_buf, q_buf, k_buf, v_buf) = refs[:-5], refs[-5:]
     me = me_ref[0]
     ring = len(steps)
@@ -125,41 +184,40 @@
         )
     start = 0
     for block in blocks:
-        rows = block.shape[0]
+        here = slice(start, start + block.shape[0])
         both = jnp.dot(block[...], w_buf[...], preferred_element_type=F32).astype(BF16)
-        q_buf[start : start + rows] = both[:, :head_dim]
-        k_buf[start : start + rows] = both[:, head_dim : 2 * head_dim]
-        v_buf[start : start + rows] = both[:, 2 * head_dim :]
-        start += rows
+        q_buf[here, :head_dim] = both[:, :head_dim]
+        k_buf[here, :head_dim] = both[:, head_dim : 2 * head_dim]
+        v_buf[here] = both[:, 2 * head_dim :]
+        start += block.shape[0]
+    scale = 1.0 / math.sqrt(head_dim)
+    lane = lax.broadcasted_iota(jnp.int32, (tok, tok), 1)
+    named = jnp.where(lane < 3 * CHAINS, lax.rem(lane, CHAINS), -1).astype(F32)
+    whole = jnp.full((tok, tok), bias_ref[me] * math.sqrt(head_dim), F32)
+    first = whole.astype(BF16).astype(F32)
+    second = (whole - first).astype(BF16).astype(F32)
+    third = whole - first - second
+    bias = jnp.where(lane < CHAINS, first, jnp.where(lane < 2 * CHAINS, second, third))
     owner = [lax.rem(me + (s + ring), ring) for s in steps]
-    rows_of = [chain_ref[o] for o in owner]
-    key_chain = jnp.concatenate(rows_of, axis=1)
-    scale = 1.0 / math.sqrt(head_dim)
-    bias = bias_ref[me]
-    pair = 2
-    for first in range(0, ring, pair):
-        query_chain = jnp.concatenate(
-            [
-                jnp.broadcast_to(rows_of[first + j], (tok, tok)).T
-                for j in range(pair)
-            ],
-            axis=0,
+    for i in range(ring):
+        same = jnp.broadcast_to(chain_ref[owner[i]], (tok, tok)).T == named
+        here = slice(i * tok, (i + 1) * tok)
+        k_buf[here, head_dim:] = jnp.where(same, 1.0, 0.0).astype(BF16)
+        q_buf[here, head_dim:] = jnp.where(same, bias, 0.0).astype(BF16)
+    count = 4
+    for start in range(0, ring, count):
+        scores = lax.dot_general(
+            q_buf[start * tok : (start + count) * tok],
+            k_buf[...],
+            (((1,), (1,)), ((), ())),
+            preferred_element_type=F32,
         )
-        query_chain = jnp.concatenate([query_chain] * ring, axis=1)
-        query = q_buf[first * tok : (first + pair) * tok]
-        scores = (
-            lax.dot_general(
-                query, k_buf[...], (((1,), (1,)), ((), ())), preferred_element_type=F32
-            )
-            * scale
-        )
-        scores = scores + jnp.where(query_chain == key_chain, bias, 0.0)
         top = jnp.max(scores, axis=-1, keepdims=True)
-        raised = jnp.exp(scores - top)
+        raised = jnp.exp2((scores - top) * (scale * math.log2(math.e)))
         probs = (raised * (1.0 / jnp.sum(raised, axis=-1, keepdims=True))).astype(BF16)
         mixed = jnp.dot(probs, v_buf[...], preferred_element_type=F32).astype(BF16)
-        for j in range(pair):
-            out_ref[owner[first + j]] = mixed[j * tok : (j + 1) * tok]
+        for j in range(count):
+            out_ref[owner[start + j]] = mixed[j * tok : (j + 1) * tok]
 
 
 def attention(me, bias, chains, weights, blocks, steps):
@@ -175,8 +233,8 @@
         out_specs=vmem_spec(),
         scratch_shapes=[
             pltpu.VMEM((width, 3 * head_dim), BF16),
-            pltpu.VMEM((length, head_dim), BF16),
-            pltpu.VMEM((length, head_dim), BF16),
+            pltpu.VMEM((length, head_dim + tok), BF16),
+            pltpu.VMEM((length, head_dim + tok), BF16),
             pltpu.VMEM((length, head_dim), BF16),
         ],
         compiler_params=pltpu.CompilerParams(vmem_limit_bytes=16 * MIB),
@@ -187,22 +245,16 @@
     )(me, bias, chains, weights, *blocks)
 
 
-def dispatch_kernel(
-    core_ref, heads_ref, own_ref, other_ref, tokens_ref, gain_ref, pick_ref, mixed_ref, out_ref
-):
+def dispatch_kernel(core_ref, heads_ref, *refs):
+    parts, (tokens_ref, gain_ref, pick_ref, mixed_ref, out_ref) = refs[:-5], refs[-5:]
     core = core_ref[0]
     half = heads_ref.shape[0] // 2
     width = tokens_ref.shape[1]
     mixed = tokens_ref[...].astype(F32)
-    columns = own_ref.shape[1] // half
-    for ref, side in ((own_ref, core), (other_ref, 1 - core)):
+    for own, side in ((0, core), (half, 1 - core)):
         local = jnp.concatenate([heads_ref[side * half + j] for j in range(half)], axis=1)
         w_out = jnp.concatenate(
-            [
-                ref[:, j * columns : (j + 1) * columns].reshape(width, heads_ref.shape[2])
-                for j in range(half)
-            ],
-            axis=1,
+            [parts[own + j][...].reshape(width, heads_ref.shape[2]) for j in range(half)], axis=1
         )
         mixed = mixed + lax.dot_general(
             local, w_out, (((1,), (1,)), ((), ())), preferred_element_type=F32
@@ -218,7 +270,7 @@
     )
 
 
-def dispatch(core, heads, own, other, tokens, gain, pick, experts, cap):
+def dispatch(core, heads, parts, tokens, gain, pick, experts, cap):
     tok, width = tokens.shape
     return pl.pallas_call(
         dispatch_kernel,
@@ -226,14 +278,14 @@
             jax.ShapeDtypeStruct((tok, width), F32),
             jax.ShapeDtypeStruct((experts, cap, width), BF16),
         ],
-        in_specs=[smem_spec()] + [vmem_spec()] * 6,
+        in_specs=[smem_spec()] + [vmem_spec()] * (4 + len(parts)),
         out_specs=[vmem_spec()] * 2,
         compiler_params=pltpu.CompilerParams(vmem_limit_bytes=16 * MIB),
         cost_estimate=pl.CostEstimate(
             flops=600 * 10**6, bytes_accessed=5 * 10**6, transcendentals=0
         ),
         name="dispatch",
-    )(core, heads, own, other, tokens, gain.reshape(1, width), pick)
+    )(core, heads, *parts, tokens, gain.reshape(1, width), pick)
 
 
 def expert_kernel(rows_ref, up_ref, down_ref, out_ref):
@@ -267,25 +319,24 @@
     )(rows, w_gateup, w_down)
 
 
-def combine_kernel(mixed_ref, high_ref, low_ref, back_ref, out_ref):
-    rows = back_ref[...]
-    total = mixed_ref[...] + jnp.dot(high_ref[...], rows, preferred_element_type=F32)
-    total = total + jnp.dot(low_ref[...], rows, preferred_element_type=F32)
-    out_ref[...] = total.astype(BF16)
-
-
-def combine(mixed, high, low, back):
+def combine_kernel(mixed_ref, gate_ref, back_ref, out_ref):
+    tok = mixed_ref.shape[0]
+    both = jnp.dot(gate_ref[...], back_ref[...], preferred_element_type=F32)
+    out_ref[...] = (mixed_ref[...] + (both[:tok] + both[tok:])).astype(BF16)
+
+
+def combine(mixed, gates, back):
     return pl.pallas_call(
         combine_kernel,
         out_shape=jax.ShapeDtypeStruct(mixed.shape, BF16),
-        in_specs=[vmem_spec()] * 4,
+        in_specs=[vmem_spec()] * 3,
         out_specs=vmem_spec(),
         compiler_params=pltpu.CompilerParams(vmem_limit_bytes=16 * MIB),
         cost_estimate=pl.CostEstimate(
             flops=540 * 10**6, bytes_accessed=4 * 10**6, transcendentals=0
         ),
         name="combine",
-    )(mixed, high, low, back)
+    )(mixed, gates, back)
 
 
 def ring_gather(block, axis):
@@ -324,52 +375,34 @@
     experts = lax.axis_size("expert")
     me = lax.axis_index("ctx").astype(jnp.int32).reshape(1)
     core = lax.rem(lax.axis_index("expert").astype(jnp.int32), 2).reshape(1)
-    columns = w_out.shape[1]
-    head_dim = tok
-
-    normed = rms_scale(inputs, attn_gain).astype(BF16)
-    small = jnp.concatenate(
-        [w_out.T, chain_ids.astype(BF16), jnp.zeros((EXTRA - 1, tok), BF16)], axis=0
-    )
-    small, normed = lax.optimization_barrier((small, normed))
-    small = lax.all_to_all(
-        jnp.broadcast_to(small[None], (ring,) + small.shape), "ctx", 0, 0, tiled=True
-    )
-    chains = small[:, columns : columns + 1].astype(F32)
-
+    normed, small = start(inputs, attn_gain, w_out, chain_ids, ring)
     blocks, steps = ring_gather(normed, "ctx")
 
-    w_rows = small[:, :columns].reshape(2, -1, head_dim)
-    mine = w_qkv.reshape(1, -1, head_dim)
-    mine, blocks[1], blocks[2] = lax.optimization_barrier((mine, blocks[1], blocks[2]))
-    both = jnp.concatenate([jnp.broadcast_to(mine, (2,) + mine.shape[1:]), w_rows], axis=1)
-    plane = lax.all_to_all(
-        jnp.broadcast_to(both[None], (experts // 2,) + both.shape).reshape(
-            (experts,) + both.shape[1:]
-        ),
-        "expert",
-        0,
-        0,
-        tiled=True,
-    )
+    small = lax.all_to_all(small, "ctx", 0, 0, tiled=True)
+    w_head = w_qkv.reshape(-1, w_qkv.shape[2])
+    w_head, blocks[1], blocks[2] = lax.optimization_barrier((w_head, blocks[1], blocks[2]))
+    parts, chains = plane_parts(small, w_head, experts)
+    plane = lax.all_to_all(parts, "expert", 0, 0, tiled=True)
     plane, blocks[-2], blocks[-1] = lax.optimization_barrier((plane, blocks[-2], blocks[-1]))
-    w_head = plane[:, : mine.shape[1]]
-
+
+    mine = w_head.shape[0]
+    attended = attention(me, chain_bias, chains, plane[:, :mine], blocks, steps)
+    plane, attended = lax.optimization_barrier((plane, attended))
+    swap = [(i, i ^ 1) for i in range(experts)]
+    rest = plane.shape[1] - mine
+    own = [plane[:, mine + i * rest // 4 : mine + (i + 1) * rest // 4] for i in range(4)]
+    other = [lax.ppermute(part, "expert", swap) for part in own]
+    heads = lax.all_to_all(attended, "ctx", split_axis=0, concat_axis=0, tiled=True)
     pick = pick_table(route_ids[0], experts, CAP)
-    high, low = gate_tables(route_ids[0], route_weights[0], experts, CAP)
-    attended = attention(me, chain_bias, chains, w_head, blocks, steps)
-    plane, attended = lax.optimization_barrier((plane, attended))
-    own = plane[:, mine.shape[1] :]
-    other = lax.ppermute(own, "expert", [(i, i ^ 1) for i in range(experts)])
-    heads = lax.all_to_all(attended, "ctx", split_axis=0, concat_axis=0, tiled=True)
-    pick, high, low = lax.optimization_barrier((pick, high, low))
-    mixed, outgoing = dispatch(core, heads, own, other, inputs, ffn_gain, pick, experts, CAP)
+    gates = gate_tables(route_ids[0], route_weights[0], experts, CAP)
+    pick, gates = lax.optimization_barrier((pick, gates))
+    mixed, outgoing = dispatch(core, heads, own + other, inputs, ffn_gain, pick, experts, CAP)
     arrived = lax.all_to_all(outgoing, "expert", split_axis=0, concat_axis=0, tiled=True)
     result = run_expert(arrived.reshape(-1, width), w_gateup[0], w_down[0])
     back = lax.all_to_all(
         result.reshape(arrived.shape), "expert", split_axis=0, concat_axis=0, tiled=True
     )
-    return combine(mixed, high, low, back.reshape(-1, width))[None]
+    return combine(mixed, gates, back.reshape(-1, width))[None]
 
 
 def solution(mesh):

time: 169 us -> 165 us (0.976)
  blocking collectives: 79.2 us -> 69.9 us
  starting transfers between devices: 30.6 us -> 36.4 us
  Pallas kernels: 19.6 us -> 23.5 us
  other arithmetic: 3.64 us -> 0 us
  local copies, waits for them, and re-layouts: 7.87 us -> 6.03 us
    all_to_all x1 -> x0, blocking collectives: 12.6 us -> none  [per_device(): lax.all_to_all(jnp.broadcast_to(small[None], (ring,) + small.shape), 'ctx...]
    all_to_all x1, waiting for transfers between devices: 11 us -> 3.47 us  [per_device(): lax.all_to_all(attended, 'ctx', split_axis=0, concat_axis=0, tiled=True)]
    all_to_all x1 -> x2, waiting for transfers between devices: 2.64 us -> 9.26 us  [the longest x1 6.62 us: per_device(): small = lax.all_to_all(small, 'ctx', 0, 0, tiled=True)]
    all_to_all x1 -> x2, starting transfers between devices: 9.93 us -> 15.2 us  [the longest x1 9.94 us: per_device(): plane = lax.all_to_all(parts, 'expert', 0, 0, tiled=True)]
    pallas_call x1 -> x3, Pallas kernels: 0.7 us -> 5.54 us  [the longest x1 3.01 us: plane_parts(): pl.pallas_call(plane_kernel, out_shape=[jax.ShapeDtypeStruct((experts, co...]
    all_to_all x1, blocking collectives: 34.7 us -> 37.9 us  [per_device(): lax.all_to_all(outgoing, 'expert', split_axis=0, concat_axis=0, tiled=True)]
    broadcast_in_dim x4 -> x0, local copies, waits for them, and re-layouts: 2.34 us -> none  [the longest x1 1.58 us: per_device(): jnp.broadcast_to(both[None], (experts // 2,) + both.shape)]
    convert_element_type x3 -> x0, other arithmetic: 1.77 us -> none  [the longest x1 1.1 us: per_device(): normed = rms_scale(inputs, attn_gain).astype(BF16)]
  transfers between devices with their start and end apart: 11 -> 15, of which waited for: 5 -> 8; matrix products, arithmetic and copies ran while one was open for 0% -> 1% of each run, Pallas kernels for 1% -> 1%
where the time goes in v3:
time: 165 us; the launch traced here: 164 us
  blocking collectives  69.9 us (42%)
  starting transfers between devices  36.4 us (22%)
  waiting for transfers between devices  28 us (17%)
  Pallas kernels  23.5 us (14%)
  local copies, waits for them, and re-layouts  6.03 us (4%)
    all_to_all x1, blocking collectives, per_device(): lax.all_to_all(outgoing, 'expert', split_axis=0, concat_axis=0, tiled=True)  37.9 us
    all_to_all x1, blocking collectives, per_device(): lax.all_to_all(result.reshape(arrived.shape), 'expert', split_axis=0, con...  31.9 us
    ppermute x3, waiting for transfers between devices, ring_gather(): forth = lax.ppermute(forth, axis, up)  12.5 us
    pallas_call x1, Pallas kernels, run_expert(): pl.pallas_call(expert_kernel, out_shape=jax.ShapeDtypeStruct((count, widt...  9.98 us
    all_to_all x1, starting transfers between devices, per_device(): plane = lax.all_to_all(parts, 'expert', 0, 0, tiled=True)  9.94 us
    ppermute x3, starting transfers between devices, ring_gather(): back = lax.ppermute(back, axis, down)  9.01 us
    all_to_all x1, waiting for transfers between devices, per_device(): small = lax.all_to_all(small, 'ctx', 0, 0, tiled=True)  6.62 us
    all_to_all x1, starting transfers between devices, per_device(): small = lax.all_to_all(small, 'ctx', 0, 0, tiled=True)  5.28 us
  transfers between devices with their start and end apart: 15, of which 8 were waited for; matrix products, arithmetic and copies ran while one was open for 1% of the time, Pallas kernels for 1%

profile of v3, /device:TPU:1, one launch (start us, length us, event | category | flops | bytes accessed | tf_op | source)
XLA Modules:
  0.0 164.0 jit_solution(13857928012689819645)
XLA Ops:
  0.0 1.8 %start.1 = (bf16[128,1024]{1,0:T(8,128)(2,1)}, bf16[8,48,128]{2,1,0:T(8,128)(2,1)}) custom-call(bf16[128,1024]{1,0:T(8,128)(2,1)} %bitcast.22, f32[1,1024]{1,0:T(1,128)} %bitcast.32, bf16[32,128]{1,0:T(8,128)(2,1)} %bitcast.31, s32[1,128]{1,0:T(1,128)} %chain_ref.1), custom_call_target="tpu_custom_call" | custom-call | flops 1000000 | bytes 1000000 | tf_op jit(solution)/shard_map/start/pallas_call | solution.py:43
  1.8 2.5 %collective-permute-start = (bf16[128,1024]{1,0:T(8,128)(2,1)}, bf16[128,1024]{1,0:T(8,128)(2,1)S(1)}, u32[]{:S(2)}, u32[]{:S(2)}) collective-permute-start(bf16[128,1024]{1,0:T(8,128)(2,1)} %get-tuple-element.22.refs_0_), channel_id=1, source_target_pairs={{0,32},{32,64},{64,96},{96,128},{128,160},{160,192},{192,224},{224... | collective-permute-start | bytes 786440 | tf_op jit(solution)/shard_map/ppermute | solution.py:349
  4.3 3.9 %collective-permute-start.1 = (bf16[128,1024]{1,0:T(8,128)(2,1)}, bf16[128,1024]{1,0:T(8,128)(2,1)S(1)}, u32[]{:S(2)}, u32[]{:S(2)}) collective-permute-start(bf16[128,1024]{1,0:T(8,128)(2,1)} %get-tuple-element.22.refs_0_), channel_id=1, source_target_pairs={{0,224},{32,0},{64,32},{96,64},{128,96},{160,128},{192,160},{224,1... | collective-permute-start | bytes 786440 | tf_op jit(solution)/shard_map/ppermute | solution.py:350
  8.2 5.3 %all-to-all-start = ((bf16[8,48,128]{2,1,0:T(8,128)(2,1)}), bf16[8,48,128]{2,1,0:T(8,128)(2,1)S(1)}, u32[]{:S(2)}, u32[]{:S(2)}) async-start(bf16[8,48,128]{2,1,0:T(8,128)(2,1)} %get-tuple-element.21), calls=%async_computation | async-start | bytes 196608 | tf_op jit(solution)/shard_map/all_to_all | solution.py:381
  13.5 1.0 collective-permute-done.refs_1_
  14.5 0.0 collective-permute-done.1.refs_2_
  14.5 6.6 %all-to-all-done.small_ref = bf16[8,48,128]{2,1,0:T(8,128)(2,1)S(1)} async-done(((bf16[8,48,128]{2,1,0:T(8,128)(2,1)}), bf16[8,48,128]{2,1,0:T(8,128)(2,1)S(1)}, u32[]{:S(2)}, u32[]{:S(2)}) %all-to-all-start) | async-done | bytes 98336 | tf_op jit(solution)/shard_map/all_to_all | solution.py:381
  21.1 0.6 copy-done.7
  21.7 3.0 %plane_parts.1 = (bf16[32,224,128]{2,1,0:T(8,128)(2,1)}, f32[8,1,128]{2,1,0:T(1,128)}) custom-call(bf16[8,48,128]{2,1,0:T(8,128)(2,1)} %copy-done.7, bf16[96,128]{1,0:T(8,128)(2,1)} %bitcast.30), custom_call_target="tpu_custom_call" | custom-call | flops 1000000 | bytes 2000000 | tf_op jit(solution)/shard_map/plane_parts/pallas_call | solution.py:78
  24.8 0.0 copy-start.4
  24.8 0.0 copy-start.6
  24.8 9.9 %all-to-all-start.1 = ((bf16[32,224,128]{2,1,0:T(8,128)(2,1)}), bf16[32,224,128]{2,1,0:T(8,128)(2,1)}, u32[]{:S(2)}, u32[]{:S(2)}) async-start(bf16[32,224,128]{2,1,0:T(8,128)(2,1)} %get-tuple-element.24), calls=%async_computation.1 | async-start | bytes 3670016 | tf_op jit(solution)/shard_map/all_to_all | solution.py:385
  34.7 0.4 collective-permute-start.2
  35.1 2.4 %collective-permute-start.5 = (bf16[128,1024]{1,0:T(8,128)(2,1)S(1)}, bf16[128,1024]{1,0:T(8,128)(2,1)S(1)}, u32[]{:S(2)}, u32[]{:S(2)}) collective-permute-start(bf16[128,1024]{1,0:T(8,128)(2,1)S(1)} %collective-permute-done.1.refs_2_), channel_id=1, source_target_pairs={{0,224},{32,0},{64,32},{96,64},{128,96},{160,128},{192,160},{224,1... | collective-permute-start | bytes 786440 | tf_op jit(solution)/shard_map/ppermute | solution.py:350
  37.5 6.2 %collective-permute-done.2.refs_3_ = bf16[128,1024]{1,0:T(8,128)(2,1)S(1)} collective-permute-done((bf16[128,1024]{1,0:T(8,128)(2,1)S(1)}, bf16[128,1024]{1,0:T(8,128)(2,1)S(1)}, u32[]{:S(2)}, u32[]{:S(2)}) %collective-permute-start.2) | collective-permute-done | bytes 262176 | tf_op jit(solution)/shard_map/ppermute | solution.py:349
  43.7 0.0 collective-permute-start.3
  43.7 0.0 collective-permute-done.5.refs_4_
  43.7 2.7 %collective-permute-start.6 = (bf16[128,1024]{1,0:T(8,128)(2,1)S(1)}, bf16[128,1024]{1,0:T(8,128)(2,1)S(1)}, u32[]{:S(2)}, u32[]{:S(2)}) collective-permute-start(bf16[128,1024]{1,0:T(8,128)(2,1)S(1)} %collective-permute-done.5.refs_4_), channel_id=1, source_target_pairs={{0,224},{32,0},{64,32},{96,64},{128,96},{160,128},{192,160},{224,1... | collective-permute-start | bytes 786440 | tf_op jit(solution)/shard_map/ppermute | solution.py:350
  46.4 5.3 %collective-permute-done.3.refs_5_ = bf16[128,1024]{1,0:T(8,128)(2,1)S(1)} collective-permute-done((bf16[128,1024]{1,0:T(8,128)(2,1)S(1)}, bf16[128,1024]{1,0:T(8,128)(2,1)S(1)}, u32[]{:S(2)}, u32[]{:S(2)}) %collective-permute-start.3) | collective-permute-done | bytes 262176 | tf_op jit(solution)/shard_map/ppermute | solution.py:349
  51.8 0.1 collective-permute-start.4
  51.9 0.0 collective-permute-done.6.refs_6_
  51.9 2.7 %collective-permute-start.7 = (bf16[64,1024]{1,0:T(8,128)(2,1)S(1)}, bf16[64,1024]{1,0:T(8,128)(2,1)S(1)}, u32[]{:S(2)}, u32[]{:S(2)}) collective-permute-start(bf16[64,1024]{1,0:T(8,128)(2,1)S(1)} %slice.29), channel_id=1, source_target_pairs={{0,224},{32,0},{64,32},{96,64},{128,96},{160,128},{192,160},{224,1... | collective-permute-start | bytes 393224 | tf_op jit(solution)/shard_map/ppermute | solution.py:354
  54.6 2.4 %collective-permute-done.4.refs_7_ = bf16[64,1024]{1,0:T(8,128)(2,1)S(1)} collective-permute-done((bf16[64,1024]{1,0:T(8,128)(2,1)S(1)}, bf16[64,1024]{1,0:T(8,128)(2,1)S(1)}, u32[]{:S(2)}, u32[]{:S(2)}) %collective-permute-start.4) | collective-permute-done | bytes 131104 | tf_op jit(solution)/shard_map/ppermute | solution.py:354
  57.1 0.0 collective-permute-done.7.refs_8_
  57.1 2.6 %all-to-all-done.1 = bf16[32,224,128]{2,1,0:T(8,128)(2,1)} async-done(((bf16[32,224,128]{2,1,0:T(8,128)(2,1)}), bf16[32,224,128]{2,1,0:T(8,128)(2,1)}, u32[]{:S(2)}, u32[]{:S(2)}) %all-to-all-start.1) | async-done | bytes 1835040 | tf_op jit(solution)/shard_map/all_to_all | solution.py:385
  59.7 1.2 slice.23.w_ref
  60.9 4.6 %attention.1 = bf16[8,128,128]{2,1,0:T(8,128)(2,1)} custom-call(s32[1]{0:T(128)} %bitcast.5.me_ref, f32[8]{0:T(128)S(1)} %copy-done.6, f32[8,1,128]{2,1,0:T(1,128)S(1)} %copy-done.5, bf16[32,96,128]{2,1,0:T(8,128)(2,1)S(1)} %slice.23.w_ref, bf16[128,1024]{1,0:T(8,128)(2,1)S(1)} %copy-done.4, bf16[128,1024]{1,0:T(8,128)(2,1)S(1)} %collective-permute-done.refs_1_, ...), custom_call_target="tpu_custom_call" | custom-call | flops 1400000000 | bytes 3000000 | tf_op jit(solution)/shard_map/attention/pallas_call | solution.py:229
  65.5 3.6 %all-to-all-start.2 = ((bf16[8,128,128]{2,1,0:T(8,128)(2,1)}), bf16[8,128,128]{2,1,0:T(8,128)(2,1)S(1)}, u32[]{:S(2)}, u32[]{:S(2)}) async-start(bf16[8,128,128]{2,1,0:T(8,128)(2,1)} %attention.1), calls=%async_computation.2 | async-start | bytes 524288 | tf_op jit(solution)/shard_map/all_to_all | solution.py:395
  69.1 1.3 fusion
  70.4 2.3 %collective-permute-start.10 = (bf16[32,32,128]{2,1,0:T(8,128)(2,1)S(1)}, bf16[32,32,128]{2,1,0:T(8,128)(2,1)S(1)}, u32[]{:S(2)}, u32[]{:S(2)}) collective-permute-start(bf16[32,32,128]{2,1,0:T(8,128)(2,1)S(1)} %get-tuple-element.38.refs_2_), channel_id=1, source_target_pairs={{0,1},{1,0},{2,3},{3,2},{4,5},{5,4},{6,7},{7,6},{8,9},{9,8},{10,11... | collective-permute-start | bytes 786440 | tf_op jit(solution)/shard_map/ppermute | solution.py:394
  72.7 0.1 collective-permute-start.11
  72.8 0.4 collective-permute-start.8
  73.2 0.1 collective-permute-start.9
  73.4 0.1 copy.12
  73.5 0.1 copy.14
  73.6 0.4 pick_table.1.refs_10_
  74.0 0.7 gate_tables.1.gate_ref
  74.7 0.0 collective-permute-done.11.refs_7_
  74.7 0.0 collective-permute-done.8.refs_4_
  74.7 0.3 collective-permute-done.9.refs_5_
  75.0 3.5 %all-to-all-done.2.heads_ref = bf16[8,128,128]{2,1,0:T(8,128)(2,1)S(1)} async-done(((bf16[8,128,128]{2,1,0:T(8,128)(2,1)}), bf16[8,128,128]{2,1,0:T(8,128)(2,1)S(1)}, u32[]{:S(2)}, u32[]{:S(2)}) %all-to-all-start.2) | async-done | bytes 262176 | tf_op jit(solution)/shard_map/all_to_all | solution.py:395
  78.5 1.6 dispatch.1
  80.1 0.0 copy-start.3
  80.1 37.9 %all_to_all.25 = bf16[32,32,1024]{2,1,0:T(8,128)(2,1)S(1)} all-to-all(bf16[32,32,1024]{2,1,0:T(8,128)(2,1)S(1)} %get-tuple-element.36), channel_id=1, replica_groups=mesh['ctx'=8,'expert'=32] {'expert'}, dimensions={0} | all-to-all | bytes 4194304 | tf_op jit(solution)/shard_map/all_to_all | solution.py:400
  118.0 2.6 %copy-done.2 = bf16[1,1024,2816]{2,1,0:T(8,128)(2,1)S(1)} copy-done((bf16[1,1024,2816]{2,1,0:T(8,128)(2,1)S(1)}, bf16[1,1024,2816]{2,1,0:T(8,128)(2,1)}, u32[]{:S(2)}) %copy-start.2) | copy-done | bytes 5767192
  120.7 10.0 %experts.1 = bf16[1024,1024]{1,0:T(8,128)(2,1)S(1)} custom-call(bf16[1024,1024]{1,0:T(8,128)(2,1)S(1)} %bitcast.20, bf16[1024,2816]{1,0:T(8,128)(2,1)S(1)} %bitcast.28, bf16[1408,1024]{1,0:T(8,128)(2,1)S(1)} %bitcast.29), custom_call_target="tpu_custom_call" | custom-call | flops 8858370048 | bytes 9000000 | tf_op jit(solution)/shard_map/experts/pallas_call | solution.py:309
  130.7 31.9 %all_to_all.26 = bf16[32,32,1024]{2,1,0:T(8,128)(2,1)S(1)} all-to-all(bf16[32,32,1024]{2,1,0:T(8,128)(2,1)S(1)} %bitcast.21), channel_id=1, replica_groups=mesh['ctx'=8,'expert'=32] {'expert'}, dimensions={0} | all-to-all | bytes 4194304 | tf_op jit(solution)/shard_map/all_to_all | solution.py:402
  162.6 1.4 combine.1
  (19 shorter events, 0.1 us)
Async XLA Ops:
  1.8 12.6 %collective-permute-start = (bf16[128,1024]{1,0:T(8,128)(2,1)}, bf16[128,1024]{1,0:T(8,128)(2,1)S(1)}, u32[]{:S(2)}, u32[]{:S(2)}) collective-permute-start(bf16[128,1024]{1,0:T(8,128)(2,1)} %get-tuple-element.22.refs_0_), channel_id=1, source_target_pairs={{0,32},{32,64},{64,96},{96,128},{128,160},{160,192},{192,224},{224... | collective-permute-start | bytes 786440 | tf_op jit(solution)/shard_map/ppermute | solution.py:349
  4.3 10.2 %collective-permute-start.1 = (bf16[128,1024]{1,0:T(8,128)(2,1)}, bf16[128,1024]{1,0:T(8,128)(2,1)S(1)}, u32[]{:S(2)}, u32[]{:S(2)}) collective-permute-start(bf16[128,1024]{1,0:T(8,128)(2,1)} %get-tuple-element.22.refs_0_), channel_id=1, source_target_pairs={{0,224},{32,0},{64,32},{96,64},{128,96},{160,128},{192,160},{224,1... | collective-permute-start | bytes 786440 | tf_op jit(solution)/shard_map/ppermute | solution.py:350
  8.2 12.9 %all-to-all-start = ((bf16[8,48,128]{2,1,0:T(8,128)(2,1)}), bf16[8,48,128]{2,1,0:T(8,128)(2,1)S(1)}, u32[]{:S(2)}, u32[]{:S(2)}) async-start(bf16[8,48,128]{2,1,0:T(8,128)(2,1)} %get-tuple-element.21), calls=%async_computation | async-start | bytes 196608 | tf_op jit(solution)/shard_map/all_to_all | solution.py:381
  21.1 0.6 copy-start.7
  24.8 36.1 %copy-start.4 = (bf16[128,1024]{1,0:T(8,128)(2,1)S(1)}, bf16[128,1024]{1,0:T(8,128)(2,1)}, u32[]{:S(2)}) copy-start(bf16[128,1024]{1,0:T(8,128)(2,1)} %get-tuple-element.22.refs_0_) | copy-start | bytes 786436
  24.8 36.1 %copy-start.5 = (f32[8,1,128]{2,1,0:T(1,128)S(1)}, f32[8,1,128]{2,1,0:T(1,128)}, u32[]{:S(2)}) copy-start(f32[8,1,128]{2,1,0:T(1,128)} %get-tuple-element.26.chain_ref) | copy-start | bytes 12292
  24.8 36.1 %copy-start.6 = (f32[8]{0:T(128)S(1)}, f32[8]{0:T(128)}, u32[]{:S(2)}) copy-start(f32[8]{0:T(128)} %bias_ref.1) | copy-start | bytes 100
  24.8 34.9 %all-to-all-start.1 = ((bf16[32,224,128]{2,1,0:T(8,128)(2,1)}), bf16[32,224,128]{2,1,0:T(8,128)(2,1)}, u32[]{:S(2)}, u32[]{:S(2)}) async-start(bf16[32,224,128]{2,1,0:T(8,128)(2,1)} %get-tuple-element.24), calls=%async_computation.1 | async-start | bytes 3670016 | tf_op jit(solution)/shard_map/all_to_all | solution.py:385
  34.7 9.0 %collective-permute-start.2 = (bf16[128,1024]{1,0:T(8,128)(2,1)S(1)}, bf16[128,1024]{1,0:T(8,128)(2,1)S(1)}, u32[]{:S(2)}, u32[]{:S(2)}) collective-permute-start(bf16[128,1024]{1,0:T(8,128)(2,1)S(1)} %collective-permute-done.refs_1_), channel_id=1, source_target_pairs={{0,32},{32,64},{64,96},{96,128},{128,160},{160,192},{192,224},{224... | collective-permute-start | bytes 786440 | tf_op jit(solution)/shard_map/ppermute | solution.py:349
  35.1 8.6 %collective-permute-start.5 = (bf16[128,1024]{1,0:T(8,128)(2,1)S(1)}, bf16[128,1024]{1,0:T(8,128)(2,1)S(1)}, u32[]{:S(2)}, u32[]{:S(2)}) collective-permute-start(bf16[128,1024]{1,0:T(8,128)(2,1)S(1)} %collective-permute-done.1.refs_2_), channel_id=1, source_target_pairs={{0,224},{32,0},{64,32},{96,64},{128,96},{160,128},{192,160},{224,1... | collective-permute-start | bytes 786440 | tf_op jit(solution)/shard_map/ppermute | solution.py:350
  43.7 8.0 %collective-permute-start.3 = (bf16[128,1024]{1,0:T(8,128)(2,1)S(1)}, bf16[128,1024]{1,0:T(8,128)(2,1)S(1)}, u32[]{:S(2)}, u32[]{:S(2)}) collective-permute-start(bf16[128,1024]{1,0:T(8,128)(2,1)S(1)} %collective-permute-done.2.refs_3_), channel_id=1, source_target_pairs={{0,32},{32,64},{64,96},{96,128},{128,160},{160,192},{192,224},{224... | collective-permute-start | bytes 786440 | tf_op jit(solution)/shard_map/ppermute | solution.py:349
  43.7 8.1 %collective-permute-start.6 = (bf16[128,1024]{1,0:T(8,128)(2,1)S(1)}, bf16[128,1024]{1,0:T(8,128)(2,1)S(1)}, u32[]{:S(2)}, u32[]{:S(2)}) collective-permute-start(bf16[128,1024]{1,0:T(8,128)(2,1)S(1)} %collective-permute-done.5.refs_4_), channel_id=1, source_target_pairs={{0,224},{32,0},{64,32},{96,64},{128,96},{160,128},{192,160},{224,1... | collective-permute-start | bytes 786440 | tf_op jit(solution)/shard_map/ppermute | solution.py:350
  51.8 5.3 %collective-permute-start.4 = (bf16[64,1024]{1,0:T(8,128)(2,1)S(1)}, bf16[64,1024]{1,0:T(8,128)(2,1)S(1)}, u32[]{:S(2)}, u32[]{:S(2)}) collective-permute-start(bf16[64,1024]{1,0:T(8,128)(2,1)S(1)} %slice.28), channel_id=1, source_target_pairs={{0,32},{32,64},{64,96},{96,128},{128,160},{160,192},{192,224},{224... | collective-permute-start | bytes 393224 | tf_op jit(solution)/shard_map/ppermute | solution.py:354
  51.9 5.2 %collective-permute-start.7 = (bf16[64,1024]{1,0:T(8,128)(2,1)S(1)}, bf16[64,1024]{1,0:T(8,128)(2,1)S(1)}, u32[]{:S(2)}, u32[]{:S(2)}) collective-permute-start(bf16[64,1024]{1,0:T(8,128)(2,1)S(1)} %slice.29), channel_id=1, source_target_pairs={{0,224},{32,0},{64,32},{96,64},{128,96},{160,128},{192,160},{224,1... | collective-permute-start | bytes 393224 | tf_op jit(solution)/shard_map/ppermute | solution.py:354
  65.5 7.8 %copy-start.8 = (s32[1,128,6]{1,0,2:T(1,128)S(1)}, s32[1,128,6]{1,0,2:T(1,128)}, u32[]{:S(2)}) copy-start(s32[1,128,6]{1,0,2:T(1,128)} %param.13) | copy-start | bytes 9220
  65.5 7.9 %copy-start.9 = (f32[1,128,6]{1,0,2:T(1,128)S(1)}, f32[1,128,6]{1,0,2:T(1,128)}, u32[]{:S(2)}) copy-start(f32[1,128,6]{1,0,2:T(1,128)} %param.14) | copy-start | bytes 9220
  65.5 13.0 %copy-start = (bf16[1,128,1024]{2,1,0:T(8,128)(2,1)S(1)}, bf16[1,128,1024]{2,1,0:T(8,128)(2,1)}, u32[]{:S(2)}) copy-start(bf16[1,128,1024]{2,1,0:T(8,128)(2,1)} %param.11) | copy-start | bytes 786436
  65.5 13.0 %copy-start.1 = (f32[1024]{0:T(1024)S(1)}, f32[1024]{0:T(1024)}, u32[]{:S(2)}) copy-start(f32[1024]{0:T(1024)} %param.16) | copy-start | bytes 12292
  65.5 13.0 %all-to-all-start.2 = ((bf16[8,128,128]{2,1,0:T(8,128)(2,1)}), bf16[8,128,128]{2,1,0:T(8,128)(2,1)S(1)}, u32[]{:S(2)}, u32[]{:S(2)}) async-start(bf16[8,128,128]{2,1,0:T(8,128)(2,1)} %attention.1), calls=%async_computation.2 | async-start | bytes 524288 | tf_op jit(solution)/shard_map/all_to_all | solution.py:395
  70.4 4.3 %collective-permute-start.10 = (bf16[32,32,128]{2,1,0:T(8,128)(2,1)S(1)}, bf16[32,32,128]{2,1,0:T(8,128)(2,1)S(1)}, u32[]{:S(2)}, u32[]{:S(2)}) collective-permute-start(bf16[32,32,128]{2,1,0:T(8,128)(2,1)S(1)} %get-tuple-element.38.refs_2_), channel_id=1, source_target_pairs={{0,1},{1,0},{2,3},{3,2},{4,5},{5,4},{6,7},{7,6},{8,9},{9,8},{10,11... | collective-permute-start | bytes 786440 | tf_op jit(solution)/shard_map/ppermute | solution.py:394
  72.7 2.0 %collective-permute-start.11 = (bf16[32,32,128]{2,1,0:T(8,128)(2,1)S(1)}, bf16[32,32,128]{2,1,0:T(8,128)(2,1)S(1)}, u32[]{:S(2)}, u32[]{:S(2)}) collective-permute-start(bf16[32,32,128]{2,1,0:T(8,128)(2,1)S(1)} %get-tuple-element.37.refs_3_), channel_id=1, source_target_pairs={{0,1},{1,0},{2,3},{3,2},{4,5},{5,4},{6,7},{7,6},{8,9},{9,8},{10,11... | collective-permute-start | bytes 786440 | tf_op jit(solution)/shard_map/ppermute | solution.py:394
  72.8 1.9 %collective-permute-start.8 = (bf16[32,32,128]{2,1,0:T(8,128)(2,1)S(1)}, bf16[32,32,128]{2,1,0:T(8,128)(2,1)S(1)}, u32[]{:S(2)}, u32[]{:S(2)}) collective-permute-start(bf16[32,32,128]{2,1,0:T(8,128)(2,1)S(1)} %get-tuple-element.40.refs_0_), channel_id=1, source_target_pairs={{0,1},{1,0},{2,3},{3,2},{4,5},{5,4},{6,7},{7,6},{8,9},{9,8},{10,11... | collective-permute-start | bytes 786440 | tf_op jit(solution)/shard_map/ppermute | solution.py:394
  73.2 1.8 %collective-permute-start.9 = (bf16[32,32,128]{2,1,0:T(8,128)(2,1)S(1)}, bf16[32,32,128]{2,1,0:T(8,128)(2,1)S(1)}, u32[]{:S(2)}, u32[]{:S(2)}) collective-permute-start(bf16[32,32,128]{2,1,0:T(8,128)(2,1)S(1)} %get-tuple-element.39.refs_1_), channel_id=1, source_target_pairs={{0,1},{1,0},{2,3},{3,2},{4,5},{5,4},{6,7},{7,6},{8,9},{9,8},{10,11... | collective-permute-start | bytes 786440 | tf_op jit(solution)/shard_map/ppermute | solution.py:394
  80.1 38.0 %copy-start.3 = (bf16[1,1408,1024]{2,1,0:T(8,128)(2,1)S(1)}, bf16[1,1408,1024]{2,1,0:T(8,128)(2,1)}, u32[]{:S(2)}) copy-start(bf16[1,1408,1024]{2,1,0:T(8,128)(2,1)} %param.21) | copy-start | bytes 8650756
  118.0 2.6 %copy-start.2 = (bf16[1,1024,2816]{2,1,0:T(8,128)(2,1)S(1)}, bf16[1,1024,2816]{2,1,0:T(8,128)(2,1)}, u32[]{:S(2)}) copy-start(bf16[1,1024,2816]{2,1,0:T(8,128)(2,1)} %param.20) | copy-start | bytes 17301508

commit v4 on v3

--- a/solution.py
+++ b/solution.py
@@ -54,22 +54,16 @@
     )(tokens, gain.reshape(1, width), w_out.T, chain_ids)
 
 
-def plane_kernel(small_ref, w_ref, plane_ref, chain_ref, parts, left):
+def plane_kernel(small_ref, w_ref, plane_ref, chain_ref):
     ring, rows, _ = small_ref.shape
     columns = rows - EXTRA
     own, half = w_ref.shape[0], ring // 2
     chain_ref[...] = small_ref[:, columns:].astype(F32)[:, 0:1]
-    copies = []
-    for core in range(2):
-        parts[core, :own] = w_ref[...]
+    for i in range(plane_ref.shape[0]):
+        plane_ref[i, :own] = w_ref[...]
         for j in range(half):
             first = own + j * columns
-            parts[core, first : first + columns] = small_ref[core * half + j, :columns]
-        for i in range(core, plane_ref.shape[0], 2):
-            copies.append(pltpu.make_async_copy(parts.at[core], plane_ref.at[i], left.at[i]))
-            copies[-1].start()
-    for copy in copies:
-        copy.wait()
+            plane_ref[i, first : first + columns] = small_ref[(i % 2) * half + j, :columns]
 
 
 def plane_parts(small, w_head, experts):
@@ -82,8 +76,7 @@
             jax.ShapeDtypeStruct((ring, 1, lanes), F32),
         ],
         in_specs=[vmem_spec()] * 2,
-        out_specs=[pl.BlockSpec(memory_space=pltpu.HBM), vmem_spec()],
-        scratch_shapes=[pltpu.VMEM((2, count, lanes), BF16), pltpu.SemaphoreType.DMA((experts,))],
+        out_specs=[vmem_spec()] * 2,
         compiler_params=pltpu.CompilerParams(vmem_limit_bytes=60 * MIB),
         cost_estimate=pl.CostEstimate(flops=10**6, bytes_accessed=2 * 10**6, transcendentals=0),
         name="plane_parts",
@@ -246,7 +239,10 @@
 
 
 def dispatch_kernel(core_ref, heads_ref, *refs):
-    parts, (tokens_ref, gain_ref, pick_ref, mixed_ref, out_ref) = refs[:-5], refs[-5:]
+    parts, refs = refs[:-8], refs[-8:]
+    tokens_ref, gain_ref, pick_ref, up_hbm, mixed_ref, out_ref, up_ref, arrived = refs
+    copy = pltpu.make_async_copy(up_hbm, up_ref, arrived)
+    copy.start()
     core = core_ref[0]
     half = heads_ref.shape[0] // 2
     width = tokens_ref.shape[1]
@@ -268,24 +264,29 @@
         .astype(BF16)
         .reshape(out_ref.shape)
     )
-
-
-def dispatch(core, heads, parts, tokens, gain, pick, experts, cap):
+    copy.wait()
+
+
+def dispatch(core, heads, parts, tokens, gain, pick, w_gateup, experts, cap):
     tok, width = tokens.shape
     return pl.pallas_call(
         dispatch_kernel,
         out_shape=[
             jax.ShapeDtypeStruct((tok, width), F32),
             jax.ShapeDtypeStruct((experts, cap, width), BF16),
+            jax.ShapeDtypeStruct(w_gateup.shape, BF16),
         ],
-        in_specs=[smem_spec()] + [vmem_spec()] * (4 + len(parts)),
-        out_specs=[vmem_spec()] * 2,
-        compiler_params=pltpu.CompilerParams(vmem_limit_bytes=16 * MIB),
+        in_specs=[smem_spec()]
+        + [vmem_spec()] * (4 + len(parts))
+        + [pl.BlockSpec(memory_space=pltpu.HBM)],
+        out_specs=[vmem_spec()] * 3,
+        scratch_shapes=[pltpu.SemaphoreType.DMA],
+        compiler_params=pltpu.CompilerParams(vmem_limit_bytes=40 * MIB),
         cost_estimate=pl.CostEstimate(
             flops=600 * 10**6, bytes_accessed=5 * 10**6, transcendentals=0
         ),
         name="dispatch",
-    )(core, heads, *parts, tokens, gain.reshape(1, width), pick)
+    )(core, heads, *parts, tokens, gain.reshape(1, width), pick, w_gateup)
 
 
 def expert_kernel(rows_ref, up_ref, down_ref, out_ref):
@@ -396,9 +397,11 @@
     pick = pick_table(route_ids[0], experts, CAP)
     gates = gate_tables(route_ids[0], route_weights[0], experts, CAP)
     pick, gates = lax.optimization_barrier((pick, gates))
-    mixed, outgoing = dispatch(core, heads, own + other, inputs, ffn_gain, pick, experts, CAP)
+    mixed, outgoing, w_up = dispatch(
+        core, heads, own + other, inputs, ffn_gain, pick, w_gateup[0], experts, CAP
+    )
     arrived = lax.all_to_all(outgoing, "expert", split_axis=0, concat_axis=0, tiled=True)
-    result = run_expert(arrived.reshape(-1, width), w_gateup[0], w_down[0])
+    result = run_expert(arrived.reshape(-1, width), w_up, w_down[0])
     back = lax.all_to_all(
         result.reshape(arrived.shape), "expert", split_axis=0, concat_axis=0, tiled=True
     )

time: 165 us -> 161 us (0.976)
  starting transfers between devices: 36.4 us -> 32.5 us
  waiting for transfers between devices: 28 us -> 30.8 us
  local copies, waits for them, and re-layouts: 6.03 us -> 3.39 us
    ppermute x3, waiting for transfers between devices: 0.01 us -> 12.9 us  [ring_gather(): back = lax.ppermute(back, axis, down)]
    ppermute x3, waiting for transfers between devices: 12.5 us -> 2.99 us  [ring_gather(): forth = lax.ppermute(forth, axis, up)]
    all_to_all x1, waiting for transfers between devices: 6.62 us -> 3.38 us  [per_device(): small = lax.all_to_all(small, 'ctx', 0, 0, tiled=True)]
    unnamed x22 -> x20, local copies, waits for them, and re-layouts: 3.54 us -> 0.9 us
    ppermute x1, waiting for transfers between devices: 0.01 us -> 1.83 us  [ring_gather(): lax.ppermute(back[half:], axis, down)]
  transfers between devices with their start and end apart: 15 -> 15, of which waited for: 8 -> 10; matrix products, arithmetic and copies ran while one was open for 1% -> 1% of each run, Pallas kernels for 1% -> 1%
where the time goes in v4:
time: 161 us; the launch traced here: 160 us
  blocking collectives  69.7 us (43%)
  starting transfers between devices  32.5 us (20%)
  waiting for transfers between devices  30.8 us (19%)
  Pallas kernels  23.9 us (15%)
  local copies, waits for them, and re-layouts  3.39 us (2%)
    all_to_all x1, blocking collectives, per_device(): lax.all_to_all(outgoing, 'expert', split_axis=0, concat_axis=0, tiled=True)  37.8 us
    all_to_all x1, blocking collectives, per_device(): lax.all_to_all(result.reshape(arrived.shape), 'expert', split_axis=0, con...  31.9 us
    ppermute x3, waiting for transfers between devices, ring_gather(): back = lax.ppermute(back, axis, down)  12.9 us
    pallas_call x1, Pallas kernels, run_expert(): pl.pallas_call(expert_kernel, out_shape=jax.ShapeDtypeStruct((count, widt...  9.99 us
    all_to_all x1, starting transfers between devices, per_device(): plane = lax.all_to_all(parts, 'expert', 0, 0, tiled=True)  9.94 us
    ppermute x3, starting transfers between devices, ring_gather(): back = lax.ppermute(back, axis, down)  7.74 us
    pallas_call x1, Pallas kernels, attention(): pl.pallas_call(functools.partial(attention_kernel, steps), out_shape=jax....  4.6 us
    all_to_all x1, starting transfers between devices, per_device(): small = lax.all_to_all(small, 'ctx', 0, 0, tiled=True)  4.07 us
  transfers between devices with their start and end apart: 15, of which 10 were waited for; matrix products, arithmetic and copies ran while one was open for 1% of the time, Pallas kernels for 1%

profile of v4, /device:TPU:1, one launch (start us, length us, event | category | flops | bytes accessed | tf_op | source)
XLA Modules:
  0.0 160.4 jit_solution(5020684891265664055)
XLA Ops:
  0.0 1.8 %start.1 = (bf16[128,1024]{1,0:T(8,128)(2,1)}, bf16[8,48,128]{2,1,0:T(8,128)(2,1)}) custom-call(bf16[128,1024]{1,0:T(8,128)(2,1)} %bitcast.22, f32[1,1024]{1,0:T(1,128)} %bitcast.32, bf16[32,128]{1,0:T(8,128)(2,1)} %bitcast.31, s32[1,128]{1,0:T(1,128)} %chain_ref.1), custom_call_target="tpu_custom_call" | custom-call | flops 1000000 | bytes 1000000 | tf_op jit(solution)/shard_map/start/pallas_call | solution.py:43
  1.8 6.4 %collective-permute-start.1 = (bf16[128,1024]{1,0:T(8,128)(2,1)}, bf16[128,1024]{1,0:T(8,128)(2,1)S(1)}, u32[]{:S(2)}, u32[]{:S(2)}) collective-permute-start(bf16[128,1024]{1,0:T(8,128)(2,1)} %get-tuple-element.23.refs_0_), channel_id=1, source_target_pairs={{0,224},{32,0},{64,32},{96,64},{128,96},{160,128},{192,160},{224,1... | collective-permute-start | bytes 786440 | tf_op jit(solution)/shard_map/ppermute | solution.py:351
  8.2 0.0 collective-permute-start
  8.2 4.1 %all-to-all-start = ((bf16[8,48,128]{2,1,0:T(8,128)(2,1)}), bf16[8,48,128]{2,1,0:T(8,128)(2,1)S(1)}, u32[]{:S(2)}, u32[]{:S(2)}) async-start(bf16[8,48,128]{2,1,0:T(8,128)(2,1)} %get-tuple-element.22), calls=%async_computation | async-start | bytes 196608 | tf_op jit(solution)/shard_map/all_to_all | solution.py:382
  12.3 1.2 collective-permute-done.1.refs_2_
  13.5 3.0 %collective-permute-done.refs_1_ = bf16[128,1024]{1,0:T(8,128)(2,1)S(1)} collective-permute-done((bf16[128,1024]{1,0:T(8,128)(2,1)}, bf16[128,1024]{1,0:T(8,128)(2,1)S(1)}, u32[]{:S(2)}, u32[]{:S(2)}) %collective-permute-start) | collective-permute-done | bytes 262176 | tf_op jit(solution)/shard_map/ppermute | solution.py:350
  16.5 3.4 %all-to-all-done.small_ref = bf16[8,48,128]{2,1,0:T(8,128)(2,1)S(1)} async-done(((bf16[8,48,128]{2,1,0:T(8,128)(2,1)}), bf16[8,48,128]{2,1,0:T(8,128)(2,1)S(1)}, u32[]{:S(2)}, u32[]{:S(2)}) %all-to-all-start) | async-done | bytes 98336 | tf_op jit(solution)/shard_map/all_to_all | solution.py:382
  19.9 0.6 copy-done.6
  20.5 2.3 %plane_parts.1 = (bf16[32,224,128]{2,1,0:T(8,128)(2,1)}, f32[8,1,128]{2,1,0:T(1,128)}) custom-call(bf16[8,48,128]{2,1,0:T(8,128)(2,1)} %copy-done.6, bf16[96,128]{1,0:T(8,128)(2,1)} %bitcast.30), custom_call_target="tpu_custom_call" | custom-call | flops 1000000 | bytes 2000000 | tf_op jit(solution)/shard_map/plane_parts/pallas_call | solution.py:72
  22.9 9.9 %all-to-all-start.1 = ((bf16[32,224,128]{2,1,0:T(8,128)(2,1)}), bf16[32,224,128]{2,1,0:T(8,128)(2,1)}, u32[]{:S(2)}, u32[]{:S(2)}) async-start(bf16[32,224,128]{2,1,0:T(8,128)(2,1)} %get-tuple-element.25), calls=%async_computation.1 | async-start | bytes 3670016 | tf_op jit(solution)/shard_map/all_to_all | solution.py:386
  32.8 0.1 collective-permute-start.5
  32.9 1.4 collective-permute-start.2
  34.4 6.2 %collective-permute-done.5.refs_4_ = bf16[128,1024]{1,0:T(8,128)(2,1)S(1)} collective-permute-done((bf16[128,1024]{1,0:T(8,128)(2,1)S(1)}, bf16[128,1024]{1,0:T(8,128)(2,1)S(1)}, u32[]{:S(2)}, u32[]{:S(2)}) %collective-permute-start.5) | collective-permute-done | bytes 262176 | tf_op jit(solution)/shard_map/ppermute | solution.py:351
  40.6 1.2 collective-permute-start.6
  41.9 0.0 collective-permute-done.2.refs_3_
  41.9 0.2 collective-permute-start.3
  42.1 5.4 %collective-permute-done.6.refs_6_ = bf16[128,1024]{1,0:T(8,128)(2,1)S(1)} collective-permute-done((bf16[128,1024]{1,0:T(8,128)(2,1)S(1)}, bf16[128,1024]{1,0:T(8,128)(2,1)S(1)}, u32[]{:S(2)}, u32[]{:S(2)}) %collective-permute-start.6) | collective-permute-done | bytes 262176 | tf_op jit(solution)/shard_map/ppermute | solution.py:351
  47.5 2.4 %collective-permute-start.7 = (bf16[64,1024]{1,0:T(8,128)(2,1)S(1)}, bf16[64,1024]{1,0:T(8,128)(2,1)S(1)}, u32[]{:S(2)}, u32[]{:S(2)}) collective-permute-start(bf16[64,1024]{1,0:T(8,128)(2,1)S(1)} %slice.29), channel_id=1, source_target_pairs={{0,224},{32,0},{64,32},{96,64},{128,96},{160,128},{192,160},{224,1... | collective-permute-start | bytes 393224 | tf_op jit(solution)/shard_map/ppermute | solution.py:355
  50.0 0.0 collective-permute-done.3.refs_5_
  50.0 0.1 collective-permute-start.4
  50.1 1.8 %collective-permute-done.7.refs_8_ = bf16[64,1024]{1,0:T(8,128)(2,1)S(1)} collective-permute-done((bf16[64,1024]{1,0:T(8,128)(2,1)S(1)}, bf16[64,1024]{1,0:T(8,128)(2,1)S(1)}, u32[]{:S(2)}, u32[]{:S(2)}) %collective-permute-start.7) | collective-permute-done | bytes 131104 | tf_op jit(solution)/shard_map/ppermute | solution.py:355
  51.9 3.2 %collective-permute-done.4.refs_7_ = bf16[64,1024]{1,0:T(8,128)(2,1)S(1)} collective-permute-done((bf16[64,1024]{1,0:T(8,128)(2,1)S(1)}, bf16[64,1024]{1,0:T(8,128)(2,1)S(1)}, u32[]{:S(2)}, u32[]{:S(2)}) %collective-permute-start.4) | collective-permute-done | bytes 131104 | tf_op jit(solution)/shard_map/ppermute | solution.py:355
  55.2 2.6 %all-to-all-done.1 = bf16[32,224,128]{2,1,0:T(8,128)(2,1)} async-done(((bf16[32,224,128]{2,1,0:T(8,128)(2,1)}), bf16[32,224,128]{2,1,0:T(8,128)(2,1)}, u32[]{:S(2)}, u32[]{:S(2)}) %all-to-all-start.1) | async-done | bytes 1835040 | tf_op jit(solution)/shard_map/all_to_all | solution.py:386
  57.8 1.2 slice.23.w_ref
  59.0 0.0 copy-done.3
  59.0 4.6 %attention.1 = bf16[8,128,128]{2,1,0:T(8,128)(2,1)} custom-call(s32[1]{0:T(128)} %bitcast.5.me_ref, f32[8]{0:T(128)S(1)} %copy-done.5, f32[8,1,128]{2,1,0:T(1,128)S(1)} %copy-done.4, bf16[32,96,128]{2,1,0:T(8,128)(2,1)S(1)} %slice.23.w_ref, bf16[128,1024]{1,0:T(8,128)(2,1)S(1)} %copy-done.3, bf16[128,1024]{1,0:T(8,128)(2,1)S(1)} %collective-permute-done.refs_1_, ...), custom_call_target="tpu_custom_call" | custom-call | flops 1400000000 | bytes 3000000 | tf_op jit(solution)/shard_map/attention/pallas_call | solution.py:222
  63.6 3.6 %all-to-all-start.2 = ((bf16[8,128,128]{2,1,0:T(8,128)(2,1)}), bf16[8,128,128]{2,1,0:T(8,128)(2,1)S(1)}, u32[]{:S(2)}, u32[]{:S(2)}) async-start(bf16[8,128,128]{2,1,0:T(8,128)(2,1)} %attention.1), calls=%async_computation.2 | async-start | bytes 524288 | tf_op jit(solution)/shard_map/all_to_all | solution.py:396
  67.2 1.3 fusion
  68.5 2.4 %collective-permute-start.11 = (bf16[32,32,128]{2,1,0:T(8,128)(2,1)S(1)}, bf16[32,32,128]{2,1,0:T(8,128)(2,1)S(1)}, u32[]{:S(2)}, u32[]{:S(2)}) collective-permute-start(bf16[32,32,128]{2,1,0:T(8,128)(2,1)S(1)} %get-tuple-element.39.refs_3_), channel_id=1, source_target_pairs={{0,1},{1,0},{2,3},{3,2},{4,5},{5,4},{6,7},{7,6},{8,9},{9,8},{10,11... | collective-permute-start | bytes 786440 | tf_op jit(solution)/shard_map/ppermute | solution.py:395
  70.8 0.1 collective-permute-start.10
  70.9 0.4 collective-permute-start.9
  71.4 0.1 collective-permute-start.8
  71.5 0.0 copy-done.7
  71.5 0.1 copy.12
  71.6 0.1 copy.14
  71.7 0.4 pick_table.1.refs_10_
  72.1 0.7 gate_tables.1.gate_ref
  72.8 0.0 collective-permute-done.11.refs_7_
  72.8 0.0 collective-permute-done.10.refs_6_
  72.8 0.0 collective-permute-done.9.refs_5_
  72.8 0.3 collective-permute-done.8.refs_4_
  73.1 3.5 %all-to-all-done.2.heads_ref = bf16[8,128,128]{2,1,0:T(8,128)(2,1)S(1)} async-done(((bf16[8,128,128]{2,1,0:T(8,128)(2,1)}), bf16[8,128,128]{2,1,0:T(8,128)(2,1)S(1)}, u32[]{:S(2)}, u32[]{:S(2)}) %all-to-all-start.2) | async-done | bytes 262176 | tf_op jit(solution)/shard_map/all_to_all | solution.py:396
  76.6 2.6 %dispatch.1 = (f32[128,1024]{1,0:T(8,128)S(1)}, bf16[32,32,1024]{2,1,0:T(8,128)(2,1)S(1)}, bf16[1024,2816]{1,0:T(8,128)(2,1)S(1)}) custom-call(s32[1]{0:T(128)} %bitcast.core_ref, bf16[8,128,128]{2,1,0:T(8,128)(2,1)S(1)} %all-to-all-done.2.heads_ref, bf16[32,32,128]{2,1,0:T(8,128)(2,1)S(1)} %get-tuple-element.42.refs_0_, ...), custom_call_target="tpu_custom_call" | custom-call | flops 600000000 | bytes 5000000 | tf_op jit(solution)/shard_map/dispatch/pallas_call | solution.py:272
  79.3 0.0 copy-start.2
  79.3 37.8 %all_to_all.25 = bf16[32,32,1024]{2,1,0:T(8,128)(2,1)S(1)} all-to-all(bf16[32,32,1024]{2,1,0:T(8,128)(2,1)S(1)} %get-tuple-element.37), channel_id=1, replica_groups=mesh['ctx'=8,'expert'=32] {'expert'}, dimensions={0} | all-to-all | bytes 4194304 | tf_op jit(solution)/shard_map/all_to_all | solution.py:403
  117.1 10.0 %experts.1 = bf16[1024,1024]{1,0:T(8,128)(2,1)S(1)} custom-call(bf16[1024,1024]{1,0:T(8,128)(2,1)S(1)} %bitcast.20, bf16[1024,2816]{1,0:T(8,128)(2,1)S(1)} %get-tuple-element.38.up_ref, bf16[1408,1024]{1,0:T(8,128)(2,1)S(1)} %bitcast.28), custom_call_target="tpu_custom_call" | custom-call | flops 8858370048 | bytes 9000000 | tf_op jit(solution)/shard_map/experts/pallas_call | solution.py:310
  127.1 31.9 %all_to_all.26 = bf16[32,32,1024]{2,1,0:T(8,128)(2,1)S(1)} all-to-all(bf16[32,32,1024]{2,1,0:T(8,128)(2,1)S(1)} %bitcast.21), channel_id=1, replica_groups=mesh['ctx'=8,'expert'=32] {'expert'}, dimensions={0} | all-to-all | bytes 4194304 | tf_op jit(solution)/shard_map/all_to_all | solution.py:405
  159.0 1.4 combine.1
  (17 shorter events, 0.0 us)
Async XLA Ops:
  1.8 11.7 %collective-permute-start.1 = (bf16[128,1024]{1,0:T(8,128)(2,1)}, bf16[128,1024]{1,0:T(8,128)(2,1)S(1)}, u32[]{:S(2)}, u32[]{:S(2)}) collective-permute-start(bf16[128,1024]{1,0:T(8,128)(2,1)} %get-tuple-element.23.refs_0_), channel_id=1, source_target_pairs={{0,224},{32,0},{64,32},{96,64},{128,96},{160,128},{192,160},{224,1... | collective-permute-start | bytes 786440 | tf_op jit(solution)/shard_map/ppermute | solution.py:351
  8.2 8.3 %collective-permute-start = (bf16[128,1024]{1,0:T(8,128)(2,1)}, bf16[128,1024]{1,0:T(8,128)(2,1)S(1)}, u32[]{:S(2)}, u32[]{:S(2)}) collective-permute-start(bf16[128,1024]{1,0:T(8,128)(2,1)} %get-tuple-element.23.refs_0_), channel_id=1, source_target_pairs={{0,32},{32,64},{64,96},{96,128},{128,160},{160,192},{192,224},{224... | collective-permute-start | bytes 786440 | tf_op jit(solution)/shard_map/ppermute | solution.py:350
  8.2 11.7 %all-to-all-start = ((bf16[8,48,128]{2,1,0:T(8,128)(2,1)}), bf16[8,48,128]{2,1,0:T(8,128)(2,1)S(1)}, u32[]{:S(2)}, u32[]{:S(2)}) async-start(bf16[8,48,128]{2,1,0:T(8,128)(2,1)} %get-tuple-element.22), calls=%async_computation | async-start | bytes 196608 | tf_op jit(solution)/shard_map/all_to_all | solution.py:382
  19.9 0.6 copy-start.6
  22.9 36.1 %copy-start.3 = (bf16[128,1024]{1,0:T(8,128)(2,1)S(1)}, bf16[128,1024]{1,0:T(8,128)(2,1)}, u32[]{:S(2)}) copy-start(bf16[128,1024]{1,0:T(8,128)(2,1)} %get-tuple-element.23.refs_0_) | copy-start | bytes 786436
  22.9 36.1 %copy-start.4 = (f32[8,1,128]{2,1,0:T(1,128)S(1)}, f32[8,1,128]{2,1,0:T(1,128)}, u32[]{:S(2)}) copy-start(f32[8,1,128]{2,1,0:T(1,128)} %get-tuple-element.27.chain_ref) | copy-start | bytes 12292
  22.9 36.1 %copy-start.5 = (f32[8]{0:T(128)S(1)}, f32[8]{0:T(128)}, u32[]{:S(2)}) copy-start(f32[8]{0:T(128)} %bias_ref.1) | copy-start | bytes 100
  22.9 34.9 %all-to-all-start.1 = ((bf16[32,224,128]{2,1,0:T(8,128)(2,1)}), bf16[32,224,128]{2,1,0:T(8,128)(2,1)}, u32[]{:S(2)}, u32[]{:S(2)}) async-start(bf16[32,224,128]{2,1,0:T(8,128)(2,1)} %get-tuple-element.25), calls=%async_computation.1 | async-start | bytes 3670016 | tf_op jit(solution)/shard_map/all_to_all | solution.py:386
  32.8 7.8 %collective-permute-start.5 = (bf16[128,1024]{1,0:T(8,128)(2,1)S(1)}, bf16[128,1024]{1,0:T(8,128)(2,1)S(1)}, u32[]{:S(2)}, u32[]{:S(2)}) collective-permute-start(bf16[128,1024]{1,0:T(8,128)(2,1)S(1)} %collective-permute-done.1.refs_2_), channel_id=1, source_target_pairs={{0,224},{32,0},{64,32},{96,64},{128,96},{160,128},{192,160},{224,1... | collective-permute-start | bytes 786440 | tf_op jit(solution)/shard_map/ppermute | solution.py:351
  32.9 8.9 %collective-permute-start.2 = (bf16[128,1024]{1,0:T(8,128)(2,1)S(1)}, bf16[128,1024]{1,0:T(8,128)(2,1)S(1)}, u32[]{:S(2)}, u32[]{:S(2)}) collective-permute-start(bf16[128,1024]{1,0:T(8,128)(2,1)S(1)} %collective-permute-done.refs_1_), channel_id=1, source_target_pairs={{0,32},{32,64},{64,96},{96,128},{128,160},{160,192},{192,224},{224... | collective-permute-start | bytes 786440 | tf_op jit(solution)/shard_map/ppermute | solution.py:350
  40.6 6.9 %collective-permute-start.6 = (bf16[128,1024]{1,0:T(8,128)(2,1)S(1)}, bf16[128,1024]{1,0:T(8,128)(2,1)S(1)}, u32[]{:S(2)}, u32[]{:S(2)}) collective-permute-start(bf16[128,1024]{1,0:T(8,128)(2,1)S(1)} %collective-permute-done.5.refs_4_), channel_id=1, source_target_pairs={{0,224},{32,0},{64,32},{96,64},{128,96},{160,128},{192,160},{224,1... | collective-permute-start | bytes 786440 | tf_op jit(solution)/shard_map/ppermute | solution.py:351
  41.9 8.1 %collective-permute-start.3 = (bf16[128,1024]{1,0:T(8,128)(2,1)S(1)}, bf16[128,1024]{1,0:T(8,128)(2,1)S(1)}, u32[]{:S(2)}, u32[]{:S(2)}) collective-permute-start(bf16[128,1024]{1,0:T(8,128)(2,1)S(1)} %collective-permute-done.2.refs_3_), channel_id=1, source_target_pairs={{0,32},{32,64},{64,96},{96,128},{128,160},{160,192},{192,224},{224... | collective-permute-start | bytes 786440 | tf_op jit(solution)/shard_map/ppermute | solution.py:350
  47.5 4.4 %collective-permute-start.7 = (bf16[64,1024]{1,0:T(8,128)(2,1)S(1)}, bf16[64,1024]{1,0:T(8,128)(2,1)S(1)}, u32[]{:S(2)}, u32[]{:S(2)}) collective-permute-start(bf16[64,1024]{1,0:T(8,128)(2,1)S(1)} %slice.29), channel_id=1, source_target_pairs={{0,224},{32,0},{64,32},{96,64},{128,96},{160,128},{192,160},{224,1... | collective-permute-start | bytes 393224 | tf_op jit(solution)/shard_map/ppermute | solution.py:355
  50.0 5.2 %collective-permute-start.4 = (bf16[64,1024]{1,0:T(8,128)(2,1)S(1)}, bf16[64,1024]{1,0:T(8,128)(2,1)S(1)}, u32[]{:S(2)}, u32[]{:S(2)}) collective-permute-start(bf16[64,1024]{1,0:T(8,128)(2,1)S(1)} %slice.28), channel_id=1, source_target_pairs={{0,32},{32,64},{64,96},{96,128},{128,160},{160,192},{192,224},{224... | collective-permute-start | bytes 393224 | tf_op jit(solution)/shard_map/ppermute | solution.py:355
  63.6 7.8 %copy-start.7 = (s32[1,128,6]{1,0,2:T(1,128)S(1)}, s32[1,128,6]{1,0,2:T(1,128)}, u32[]{:S(2)}) copy-start(s32[1,128,6]{1,0,2:T(1,128)} %param.13) | copy-start | bytes 9220
  63.6 7.9 %copy-start.8 = (f32[1,128,6]{1,0,2:T(1,128)S(1)}, f32[1,128,6]{1,0,2:T(1,128)}, u32[]{:S(2)}) copy-start(f32[1,128,6]{1,0,2:T(1,128)} %param.14) | copy-start | bytes 9220
  63.6 13.0 %copy-start = (bf16[1,128,1024]{2,1,0:T(8,128)(2,1)S(1)}, bf16[1,128,1024]{2,1,0:T(8,128)(2,1)}, u32[]{:S(2)}) copy-start(bf16[1,128,1024]{2,1,0:T(8,128)(2,1)} %param.11) | copy-start | bytes 786436
  63.6 13.0 %copy-start.1 = (f32[1024]{0:T(1024)S(1)}, f32[1024]{0:T(1024)}, u32[]{:S(2)}) copy-start(f32[1024]{0:T(1024)} %param.16) | copy-start | bytes 12292
  63.6 13.0 %all-to-all-start.2 = ((bf16[8,128,128]{2,1,0:T(8,128)(2,1)}), bf16[8,128,128]{2,1,0:T(8,128)(2,1)S(1)}, u32[]{:S(2)}, u32[]{:S(2)}) async-start(bf16[8,128,128]{2,1,0:T(8,128)(2,1)} %attention.1), calls=%async_computation.2 | async-start | bytes 524288 | tf_op jit(solution)/shard_map/all_to_all | solution.py:396
  68.5 4.3 %collective-permute-start.11 = (bf16[32,32,128]{2,1,0:T(8,128)(2,1)S(1)}, bf16[32,32,128]{2,1,0:T(8,128)(2,1)S(1)}, u32[]{:S(2)}, u32[]{:S(2)}) collective-permute-start(bf16[32,32,128]{2,1,0:T(8,128)(2,1)S(1)} %get-tuple-element.39.refs_3_), channel_id=1, source_target_pairs={{0,1},{1,0},{2,3},{3,2},{4,5},{5,4},{6,7},{7,6},{8,9},{9,8},{10,11... | collective-permute-start | bytes 786440 | tf_op jit(solution)/shard_map/ppermute | solution.py:395
  70.8 1.9 %collective-permute-start.10 = (bf16[32,32,128]{2,1,0:T(8,128)(2,1)S(1)}, bf16[32,32,128]{2,1,0:T(8,128)(2,1)S(1)}, u32[]{:S(2)}, u32[]{:S(2)}) collective-permute-start(bf16[32,32,128]{2,1,0:T(8,128)(2,1)S(1)} %get-tuple-element.40.refs_2_), channel_id=1, source_target_pairs={{0,1},{1,0},{2,3},{3,2},{4,5},{5,4},{6,7},{7,6},{8,9},{9,8},{10,11... | collective-permute-start | bytes 786440 | tf_op jit(solution)/shard_map/ppermute | solution.py:395
  70.9 1.9 %collective-permute-start.9 = (bf16[32,32,128]{2,1,0:T(8,128)(2,1)S(1)}, bf16[32,32,128]{2,1,0:T(8,128)(2,1)S(1)}, u32[]{:S(2)}, u32[]{:S(2)}) collective-permute-start(bf16[32,32,128]{2,1,0:T(8,128)(2,1)S(1)} %get-tuple-element.41.refs_1_), channel_id=1, source_target_pairs={{0,1},{1,0},{2,3},{3,2},{4,5},{5,4},{6,7},{7,6},{8,9},{9,8},{10,11... | collective-permute-start | bytes 786440 | tf_op jit(solution)/shard_map/ppermute | solution.py:395
  71.4 1.8 %collective-permute-start.8 = (bf16[32,32,128]{2,1,0:T(8,128)(2,1)S(1)}, bf16[32,32,128]{2,1,0:T(8,128)(2,1)S(1)}, u32[]{:S(2)}, u32[]{:S(2)}) collective-permute-start(bf16[32,32,128]{2,1,0:T(8,128)(2,1)S(1)} %get-tuple-element.42.refs_0_), channel_id=1, source_target_pairs={{0,1},{1,0},{2,3},{3,2},{4,5},{5,4},{6,7},{7,6},{8,9},{9,8},{10,11... | collective-permute-start | bytes 786440 | tf_op jit(solution)/shard_map/ppermute | solution.py:395
  79.3 37.8 %copy-start.2 = (bf16[1,1408,1024]{2,1,0:T(8,128)(2,1)S(1)}, bf16[1,1408,1024]{2,1,0:T(8,128)(2,1)}, u32[]{:S(2)}) copy-start(bf16[1,1408,1024]{2,1,0:T(8,128)(2,1)} %param.21) | copy-start | bytes 8650756

commit v5 on v4

--- a/solution.py
+++ b/solution.py
@@ -12,9 +12,10 @@
 BF16 = jnp.bfloat16
 MIB = 1 << 20
 CAP = 32
-EXTRA = 16
+EXTRA = 48
 CHAINS = 8
 WIDE = 256
+PIECES = 4
 
 
 def vmem_spec():
@@ -77,7 +78,7 @@
         ],
         in_specs=[vmem_spec()] * 2,
         out_specs=[vmem_spec()] * 2,
-        compiler_params=pltpu.CompilerParams(vmem_limit_bytes=60 * MIB),
+        compiler_params=pltpu.CompilerParams(vmem_limit_bytes=40 * MIB),
         cost_estimate=pl.CostEstimate(flops=10**6, bytes_accessed=2 * 10**6, transcendentals=0),
         name="plane_parts",
     )(small, w_head)
@@ -241,8 +242,12 @@
 def dispatch_kernel(core_ref, heads_ref, *refs):
     parts, refs = refs[:-8], refs[-8:]
     tokens_ref, gain_ref, pick_ref, up_hbm, mixed_ref, out_ref, up_ref, arrived = refs
-    copy = pltpu.make_async_copy(up_hbm, up_ref, arrived)
-    copy.start()
+    rows = up_hbm.shape[0] // PIECES
+    copies = []
+    for i in range(PIECES):
+        here = pl.ds(i * rows, rows)
+        copies.append(pltpu.make_async_copy(up_hbm.at[here], up_ref.at[here], arrived.at[i]))
+        copies[-1].start()
     core = core_ref[0]
     half = heads_ref.shape[0] // 2
     width = tokens_ref.shape[1]
@@ -264,7 +269,8 @@
         .astype(BF16)
         .reshape(out_ref.shape)
     )
-    copy.wait()
+    for copy in copies:
+        copy.wait()
 
 
 def dispatch(core, heads, parts, tokens, gain, pick, w_gateup, experts, cap):
@@ -280,7 +286,7 @@
         + [vmem_spec()] * (4 + len(parts))
         + [pl.BlockSpec(memory_space=pltpu.HBM)],
         out_specs=[vmem_spec()] * 3,
-        scratch_shapes=[pltpu.SemaphoreType.DMA],
+        scratch_shapes=[pltpu.SemaphoreType.DMA((PIECES,))],
         compiler_params=pltpu.CompilerParams(vmem_limit_bytes=40 * MIB),
         cost_estimate=pl.CostEstimate(
             flops=600 * 10**6, bytes_accessed=5 * 10**6, transcendentals=0

time: 161 us -> 166 us (1.031)
  starting transfers between devices: 32.5 us -> 35.9 us
  blocking collectives: 69.7 us -> 71.7 us
    ppermute x3, waiting for transfers between devices: 12.9 us -> 19 us  [ring_gather(): back = lax.ppermute(back, axis, down)]
    all_to_all x1, starting transfers between devices: 4.07 us -> 9.02 us  [per_device(): small = lax.all_to_all(small, 'ctx', 0, 0, tiled=True)]
    all_to_all x1, waiting for transfers between devices: 3.38 us -> 0.01 us  [per_device(): small = lax.all_to_all(small, 'ctx', 0, 0, tiled=True)]
    all_to_all x1, blocking collectives: 37.8 us -> 39.8 us  [per_device(): lax.all_to_all(outgoing, 'expert', split_axis=0, concat_axis=0, tiled=True)]
    ppermute x3, starting transfers between devices: 7.74 us -> 5.88 us  [ring_gather(): back = lax.ppermute(back, axis, down)]
  transfers between devices with their start and end apart: 15 -> 15, of which waited for: 10 -> 9; matrix products, arithmetic and copies ran while one was open for 1% -> 1% of each run, Pallas kernels for 1% -> 1%
where the time goes in v5:
time: 166 us; the launch traced here: 165 us
  blocking collectives  71.7 us (43%)
  starting transfers between devices  35.9 us (22%)
  waiting for transfers between devices  30.2 us (18%)
  Pallas kernels  23.8 us (14%)
  local copies, waits for them, and re-layouts  3.47 us (2%)
    all_to_all x1, blocking collectives, per_device(): lax.all_to_all(outgoing, 'expert', split_axis=0, concat_axis=0, tiled=True)  39.8 us
    all_to_all x1, blocking collectives, per_device(): lax.all_to_all(result.reshape(arrived.shape), 'expert', split_axis=0, con...  31.9 us
    ppermute x3, waiting for transfers between devices, ring_gather(): back = lax.ppermute(back, axis, down)  19 us
    pallas_call x1, Pallas kernels, run_expert(): pl.pallas_call(expert_kernel, out_shape=jax.ShapeDtypeStruct((count, widt...  9.99 us
    all_to_all x1, starting transfers between devices, per_device(): small = lax.all_to_all(small, 'ctx', 0, 0, tiled=True)  9.02 us
    all_to_all x1, starting transfers between devices, per_device(): plane = lax.all_to_all(parts, 'expert', 0, 0, tiled=True)  8.93 us
    ppermute x3, starting transfers between devices, ring_gather(): back = lax.ppermute(back, axis, down)  5.88 us
    pallas_call x1, Pallas kernels, attention(): pl.pallas_call(functools.partial(attention_kernel, steps), out_shape=jax....  4.62 us
  transfers between devices with their start and end apart: 15, of which 9 were waited for; matrix products, arithmetic and copies ran while one was open for 1% of the time, Pallas kernels for 1%

profile of v5, /device:TPU:1, one launch (start us, length us, event | category | flops | bytes accessed | tf_op | source)
XLA Modules:
  0.0 165.1 jit_solution(16122114521147838741)
XLA Ops:
  0.0 1.8 %start.1 = (bf16[128,1024]{1,0:T(8,128)(2,1)}, bf16[8,80,128]{2,1,0:T(8,128)(2,1)}) custom-call(bf16[128,1024]{1,0:T(8,128)(2,1)} %bitcast.22, f32[1,1024]{1,0:T(1,128)} %bitcast.32, bf16[32,128]{1,0:T(8,128)(2,1)} %bitcast.31, s32[1,128]{1,0:T(1,128)} %chain_ref.1), custom_call_target="tpu_custom_call" | custom-call | flops 1000000 | bytes 1000000 | tf_op jit(solution)/shard_map/start/pallas_call | solution.py:44
  1.8 9.0 %all-to-all-start = ((bf16[8,80,128]{2,1,0:T(8,128)(2,1)}), bf16[8,80,128]{2,1,0:T(8,128)(2,1)S(1)}, u32[]{:S(2)}, u32[]{:S(2)}) async-start(bf16[8,80,128]{2,1,0:T(8,128)(2,1)} %get-tuple-element.22), calls=%async_computation | async-start | bytes 327680 | tf_op jit(solution)/shard_map/all_to_all | solution.py:388
  10.8 2.7 %collective-permute-start.1 = (bf16[128,1024]{1,0:T(8,128)(2,1)}, bf16[128,1024]{1,0:T(8,128)(2,1)S(1)}, u32[]{:S(2)}, u32[]{:S(2)}) collective-permute-start(bf16[128,1024]{1,0:T(8,128)(2,1)} %get-tuple-element.23.refs_0_), channel_id=1, source_target_pairs={{0,224},{32,0},{64,32},{96,64},{128,96},{160,128},{192,160},{224,1... | collective-permute-start | bytes 786440 | tf_op jit(solution)/shard_map/ppermute | solution.py:357
  13.5 0.0 collective-permute-start
  13.5 8.1 %collective-permute-done.1.refs_2_ = bf16[128,1024]{1,0:T(8,128)(2,1)S(1)} collective-permute-done((bf16[128,1024]{1,0:T(8,128)(2,1)}, bf16[128,1024]{1,0:T(8,128)(2,1)S(1)}, u32[]{:S(2)}, u32[]{:S(2)}) %collective-permute-start.1) | collective-permute-done | bytes 262176 | tf_op jit(solution)/shard_map/ppermute | solution.py:357
  21.6 1.5 collective-permute-done.refs_1_
  23.1 0.0 all-to-all-done.small_ref
  23.2 0.7 copy-done.1
  23.9 1.4 plane_parts.1
  25.3 8.9 %all-to-all-start.1 = ((bf16[32,224,128]{2,1,0:T(8,128)(2,1)}), bf16[32,224,128]{2,1,0:T(8,128)(2,1)}, u32[]{:S(2)}, u32[]{:S(2)}) async-start(bf16[32,224,128]{2,1,0:T(8,128)(2,1)} %get-tuple-element.25), calls=%async_computation.1 | async-start | bytes 3670016 | tf_op jit(solution)/shard_map/all_to_all | solution.py:392
  34.3 1.0 collective-permute-start.5
  35.3 0.5 collective-permute-start.2
  35.8 6.2 %collective-permute-done.5.refs_4_ = bf16[128,1024]{1,0:T(8,128)(2,1)S(1)} collective-permute-done((bf16[128,1024]{1,0:T(8,128)(2,1)S(1)}, bf16[128,1024]{1,0:T(8,128)(2,1)S(1)}, u32[]{:S(2)}, u32[]{:S(2)}) %collective-permute-start.5) | collective-permute-done | bytes 262176 | tf_op jit(solution)/shard_map/ppermute | solution.py:357
  42.1 2.2 %collective-permute-start.6 = (bf16[128,1024]{1,0:T(8,128)(2,1)S(1)}, bf16[128,1024]{1,0:T(8,128)(2,1)S(1)}, u32[]{:S(2)}, u32[]{:S(2)}) collective-permute-start(bf16[128,1024]{1,0:T(8,128)(2,1)S(1)} %collective-permute-done.5.refs_4_), channel_id=1, source_target_pairs={{0,224},{32,0},{64,32},{96,64},{128,96},{160,128},{192,160},{224,1... | collective-permute-start | bytes 786440 | tf_op jit(solution)/shard_map/ppermute | solution.py:357
  44.2 0.0 collective-permute-done.2.refs_3_
  44.2 0.0 collective-permute-start.3
  44.2 4.7 %collective-permute-done.6.refs_6_ = bf16[128,1024]{1,0:T(8,128)(2,1)S(1)} collective-permute-done((bf16[128,1024]{1,0:T(8,128)(2,1)S(1)}, bf16[128,1024]{1,0:T(8,128)(2,1)S(1)}, u32[]{:S(2)}, u32[]{:S(2)}) %collective-permute-start.6) | collective-permute-done | bytes 262176 | tf_op jit(solution)/shard_map/ppermute | solution.py:357
  49.0 3.4 %collective-permute-start.7 = (bf16[64,1024]{1,0:T(8,128)(2,1)S(1)}, bf16[64,1024]{1,0:T(8,128)(2,1)S(1)}, u32[]{:S(2)}, u32[]{:S(2)}) collective-permute-start(bf16[64,1024]{1,0:T(8,128)(2,1)S(1)} %slice.29), channel_id=1, source_target_pairs={{0,224},{32,0},{64,32},{96,64},{128,96},{160,128},{192,160},{224,1... | collective-permute-start | bytes 393224 | tf_op jit(solution)/shard_map/ppermute | solution.py:361
  52.4 0.0 collective-permute-done.3.refs_5_
  52.4 0.1 collective-permute-start.4
  52.5 1.8 %collective-permute-done.7.refs_8_ = bf16[64,1024]{1,0:T(8,128)(2,1)S(1)} collective-permute-done((bf16[64,1024]{1,0:T(8,128)(2,1)S(1)}, bf16[64,1024]{1,0:T(8,128)(2,1)S(1)}, u32[]{:S(2)}, u32[]{:S(2)}) %collective-permute-start.7) | collective-permute-done | bytes 131104 | tf_op jit(solution)/shard_map/ppermute | solution.py:361
  54.3 3.2 %collective-permute-done.4.refs_7_ = bf16[64,1024]{1,0:T(8,128)(2,1)S(1)} collective-permute-done((bf16[64,1024]{1,0:T(8,128)(2,1)S(1)}, bf16[64,1024]{1,0:T(8,128)(2,1)S(1)}, u32[]{:S(2)}, u32[]{:S(2)}) %collective-permute-start.4) | collective-permute-done | bytes 131104 | tf_op jit(solution)/shard_map/ppermute | solution.py:361
  57.5 1.8 %all-to-all-done.1 = bf16[32,224,128]{2,1,0:T(8,128)(2,1)} async-done(((bf16[32,224,128]{2,1,0:T(8,128)(2,1)}), bf16[32,224,128]{2,1,0:T(8,128)(2,1)}, u32[]{:S(2)}, u32[]{:S(2)}) %all-to-all-start.1) | async-done | bytes 1835040 | tf_op jit(solution)/shard_map/all_to_all | solution.py:392
  59.2 1.2 slice.23.w_ref
  60.4 0.0 copy-done.4
  60.5 4.6 %attention.1 = bf16[8,128,128]{2,1,0:T(8,128)(2,1)} custom-call(s32[1]{0:T(128)} %bitcast.5.me_ref, f32[8]{0:T(128)S(1)} %copy-done.5, f32[8,1,128]{2,1,0:T(1,128)S(1)} %get-tuple-element.27.chain_ref, bf16[32,96,128]{2,1,0:T(8,128)(2,1)S(1)} %slice.23.w_ref, bf16[128,1024]{1,0:T(8,128)(2,1)S(1)} %copy-done.4, ...), custom_call_target="tpu_custom_call" | custom-call | flops 1400000000 | bytes 3000000 | tf_op jit(solution)/shard_map/attention/pallas_call | solution.py:223
  65.1 4.1 %all-to-all-start.2 = ((bf16[8,128,128]{2,1,0:T(8,128)(2,1)}), bf16[8,128,128]{2,1,0:T(8,128)(2,1)S(1)}, u32[]{:S(2)}, u32[]{:S(2)}) async-start(bf16[8,128,128]{2,1,0:T(8,128)(2,1)} %attention.1), calls=%async_computation.2 | async-start | bytes 524288 | tf_op jit(solution)/shard_map/all_to_all | solution.py:402
  69.2 1.3 fusion
  70.4 3.4 %collective-permute-start.11 = (bf16[32,32,128]{2,1,0:T(8,128)(2,1)S(1)}, bf16[32,32,128]{2,1,0:T(8,128)(2,1)S(1)}, u32[]{:S(2)}, u32[]{:S(2)}) collective-permute-start(bf16[32,32,128]{2,1,0:T(8,128)(2,1)S(1)} %get-tuple-element.39.refs_3_), channel_id=1, source_target_pairs={{0,1},{1,0},{2,3},{3,2},{4,5},{5,4},{6,7},{7,6},{8,9},{9,8},{10,11... | collective-permute-start | bytes 786440 | tf_op jit(solution)/shard_map/ppermute | solution.py:401
  73.8 0.1 collective-permute-start.10
  73.9 0.4 collective-permute-start.9
  74.3 0.1 collective-permute-start.8
  74.4 0.1 copy.12
  74.6 0.1 copy.14
  74.7 0.4 pick_table.1.refs_10_
  75.0 0.7 gate_tables.1.gate_ref
  75.8 0.0 collective-permute-done.11.refs_7_
  75.8 0.0 collective-permute-done.10.refs_6_
  75.8 0.0 collective-permute-done.9.refs_5_
  75.8 0.3 collective-permute-done.8.refs_4_
  76.1 2.5 %all-to-all-done.2.heads_ref = bf16[8,128,128]{2,1,0:T(8,128)(2,1)S(1)} async-done(((bf16[8,128,128]{2,1,0:T(8,128)(2,1)}), bf16[8,128,128]{2,1,0:T(8,128)(2,1)S(1)}, u32[]{:S(2)}, u32[]{:S(2)}) %all-to-all-start.2) | async-done | bytes 262176 | tf_op jit(solution)/shard_map/all_to_all | solution.py:402
  78.6 0.0 copy-done.2
  78.6 3.4 %dispatch.1 = (f32[128,1024]{1,0:T(8,128)S(1)}, bf16[32,32,1024]{2,1,0:T(8,128)(2,1)S(1)}, bf16[1024,2816]{1,0:T(8,128)(2,1)S(1)}) custom-call(s32[1]{0:T(128)} %bitcast.core_ref, bf16[8,128,128]{2,1,0:T(8,128)(2,1)S(1)} %all-to-all-done.2.heads_ref, bf16[32,32,128]{2,1,0:T(8,128)(2,1)S(1)} %get-tuple-element.42.refs_0_, ...), custom_call_target="tpu_custom_call" | custom-call | flops 600000000 | bytes 5000000 | tf_op jit(solution)/shard_map/dispatch/pallas_call | solution.py:278
  82.0 0.0 copy-start.3
  82.0 39.8 %all_to_all.25 = bf16[32,32,1024]{2,1,0:T(8,128)(2,1)S(1)} all-to-all(bf16[32,32,1024]{2,1,0:T(8,128)(2,1)S(1)} %get-tuple-element.37), channel_id=1, replica_groups=mesh['ctx'=8,'expert'=32] {'expert'}, dimensions={0} | all-to-all | bytes 4194304 | tf_op jit(solution)/shard_map/all_to_all | solution.py:409
  121.8 10.0 %experts.1 = bf16[1024,1024]{1,0:T(8,128)(2,1)S(1)} custom-call(bf16[1024,1024]{1,0:T(8,128)(2,1)S(1)} %bitcast.20, bf16[1024,2816]{1,0:T(8,128)(2,1)S(1)} %get-tuple-element.38.up_ref, bf16[1408,1024]{1,0:T(8,128)(2,1)S(1)} %bitcast.29), custom_call_target="tpu_custom_call" | custom-call | flops 8858370048 | bytes 9000000 | tf_op jit(solution)/shard_map/experts/pallas_call | solution.py:316
  131.8 31.9 %all_to_all.26 = bf16[32,32,1024]{2,1,0:T(8,128)(2,1)S(1)} all-to-all(bf16[32,32,1024]{2,1,0:T(8,128)(2,1)S(1)} %bitcast.21), channel_id=1, replica_groups=mesh['ctx'=8,'expert'=32] {'expert'}, dimensions={0} | all-to-all | bytes 4194304 | tf_op jit(solution)/shard_map/all_to_all | solution.py:411
  163.7 1.4 combine.1
  (15 shorter events, 0.0 us)
Async XLA Ops:
  1.8 21.3 %all-to-all-start = ((bf16[8,80,128]{2,1,0:T(8,128)(2,1)}), bf16[8,80,128]{2,1,0:T(8,128)(2,1)S(1)}, u32[]{:S(2)}, u32[]{:S(2)}) async-start(bf16[8,80,128]{2,1,0:T(8,128)(2,1)} %get-tuple-element.22), calls=%async_computation | async-start | bytes 327680 | tf_op jit(solution)/shard_map/all_to_all | solution.py:388
  10.8 10.8 %collective-permute-start.1 = (bf16[128,1024]{1,0:T(8,128)(2,1)}, bf16[128,1024]{1,0:T(8,128)(2,1)S(1)}, u32[]{:S(2)}, u32[]{:S(2)}) collective-permute-start(bf16[128,1024]{1,0:T(8,128)(2,1)} %get-tuple-element.23.refs_0_), channel_id=1, source_target_pairs={{0,224},{32,0},{64,32},{96,64},{128,96},{160,128},{192,160},{224,1... | collective-permute-start | bytes 786440 | tf_op jit(solution)/shard_map/ppermute | solution.py:357
  13.5 9.6 %collective-permute-start = (bf16[128,1024]{1,0:T(8,128)(2,1)}, bf16[128,1024]{1,0:T(8,128)(2,1)S(1)}, u32[]{:S(2)}, u32[]{:S(2)}) collective-permute-start(bf16[128,1024]{1,0:T(8,128)(2,1)} %get-tuple-element.23.refs_0_), channel_id=1, source_target_pairs={{0,32},{32,64},{64,96},{96,128},{128,160},{160,192},{192,224},{224... | collective-permute-start | bytes 786440 | tf_op jit(solution)/shard_map/ppermute | solution.py:356
  23.2 0.7 copy-start.1
  25.3 35.1 %copy-start.4 = (bf16[128,1024]{1,0:T(8,128)(2,1)S(1)}, bf16[128,1024]{1,0:T(8,128)(2,1)}, u32[]{:S(2)}) copy-start(bf16[128,1024]{1,0:T(8,128)(2,1)} %get-tuple-element.23.refs_0_) | copy-start | bytes 786436
  25.3 35.1 %copy-start.5 = (f32[8]{0:T(128)S(1)}, f32[8]{0:T(128)}, u32[]{:S(2)}) copy-start(f32[8]{0:T(128)} %bias_ref.1) | copy-start | bytes 100
  25.3 33.9 %all-to-all-start.1 = ((bf16[32,224,128]{2,1,0:T(8,128)(2,1)}), bf16[32,224,128]{2,1,0:T(8,128)(2,1)}, u32[]{:S(2)}, u32[]{:S(2)}) async-start(bf16[32,224,128]{2,1,0:T(8,128)(2,1)} %get-tuple-element.25), calls=%async_computation.1 | async-start | bytes 3670016 | tf_op jit(solution)/shard_map/all_to_all | solution.py:392
  34.3 7.8 %collective-permute-start.5 = (bf16[128,1024]{1,0:T(8,128)(2,1)S(1)}, bf16[128,1024]{1,0:T(8,128)(2,1)S(1)}, u32[]{:S(2)}, u32[]{:S(2)}) collective-permute-start(bf16[128,1024]{1,0:T(8,128)(2,1)S(1)} %collective-permute-done.1.refs_2_), channel_id=1, source_target_pairs={{0,224},{32,0},{64,32},{96,64},{128,96},{160,128},{192,160},{224,1... | collective-permute-start | bytes 786440 | tf_op jit(solution)/shard_map/ppermute | solution.py:357
  35.3 8.9 %collective-permute-start.2 = (bf16[128,1024]{1,0:T(8,128)(2,1)S(1)}, bf16[128,1024]{1,0:T(8,128)(2,1)S(1)}, u32[]{:S(2)}, u32[]{:S(2)}) collective-permute-start(bf16[128,1024]{1,0:T(8,128)(2,1)S(1)} %collective-permute-done.refs_1_), channel_id=1, source_target_pairs={{0,32},{32,64},{64,96},{96,128},{128,160},{160,192},{192,224},{224... | collective-permute-start | bytes 786440 | tf_op jit(solution)/shard_map/ppermute | solution.py:356
  42.1 6.9 %collective-permute-start.6 = (bf16[128,1024]{1,0:T(8,128)(2,1)S(1)}, bf16[128,1024]{1,0:T(8,128)(2,1)S(1)}, u32[]{:S(2)}, u32[]{:S(2)}) collective-permute-start(bf16[128,1024]{1,0:T(8,128)(2,1)S(1)} %collective-permute-done.5.refs_4_), channel_id=1, source_target_pairs={{0,224},{32,0},{64,32},{96,64},{128,96},{160,128},{192,160},{224,1... | collective-permute-start | bytes 786440 | tf_op jit(solution)/shard_map/ppermute | solution.py:357
  44.2 8.1 %collective-permute-start.3 = (bf16[128,1024]{1,0:T(8,128)(2,1)S(1)}, bf16[128,1024]{1,0:T(8,128)(2,1)S(1)}, u32[]{:S(2)}, u32[]{:S(2)}) collective-permute-start(bf16[128,1024]{1,0:T(8,128)(2,1)S(1)} %collective-permute-done.2.refs_3_), channel_id=1, source_target_pairs={{0,32},{32,64},{64,96},{96,128},{128,160},{160,192},{192,224},{224... | collective-permute-start | bytes 786440 | tf_op jit(solution)/shard_map/ppermute | solution.py:356
  49.0 5.3 %collective-permute-start.7 = (bf16[64,1024]{1,0:T(8,128)(2,1)S(1)}, bf16[64,1024]{1,0:T(8,128)(2,1)S(1)}, u32[]{:S(2)}, u32[]{:S(2)}) collective-permute-start(bf16[64,1024]{1,0:T(8,128)(2,1)S(1)} %slice.29), channel_id=1, source_target_pairs={{0,224},{32,0},{64,32},{96,64},{128,96},{160,128},{192,160},{224,1... | collective-permute-start | bytes 393224 | tf_op jit(solution)/shard_map/ppermute | solution.py:361
  52.4 5.1 %collective-permute-start.4 = (bf16[64,1024]{1,0:T(8,128)(2,1)S(1)}, bf16[64,1024]{1,0:T(8,128)(2,1)S(1)}, u32[]{:S(2)}, u32[]{:S(2)}) collective-permute-start(bf16[64,1024]{1,0:T(8,128)(2,1)S(1)} %slice.28), channel_id=1, source_target_pairs={{0,32},{32,64},{64,96},{96,128},{128,160},{160,192},{192,224},{224... | collective-permute-start | bytes 393224 | tf_op jit(solution)/shard_map/ppermute | solution.py:361
  65.1 9.4 %copy-start.6 = (s32[1,128,6]{1,0,2:T(1,128)S(1)}, s32[1,128,6]{1,0,2:T(1,128)}, u32[]{:S(2)}) copy-start(s32[1,128,6]{1,0,2:T(1,128)} %param.13) | copy-start | bytes 9220
  65.1 9.5 %copy-start.7 = (f32[1,128,6]{1,0,2:T(1,128)S(1)}, f32[1,128,6]{1,0,2:T(1,128)}, u32[]{:S(2)}) copy-start(f32[1,128,6]{1,0,2:T(1,128)} %param.14) | copy-start | bytes 9220
  65.1 13.5 %copy-start = (bf16[1,128,1024]{2,1,0:T(8,128)(2,1)S(1)}, bf16[1,128,1024]{2,1,0:T(8,128)(2,1)}, u32[]{:S(2)}) copy-start(bf16[1,128,1024]{2,1,0:T(8,128)(2,1)} %param.11) | copy-start | bytes 786436
  65.1 13.5 %copy-start.2 = (f32[1024]{0:T(1024)S(1)}, f32[1024]{0:T(1024)}, u32[]{:S(2)}) copy-start(f32[1024]{0:T(1024)} %param.16) | copy-start | bytes 12292
  65.1 13.5 %all-to-all-start.2 = ((bf16[8,128,128]{2,1,0:T(8,128)(2,1)}), bf16[8,128,128]{2,1,0:T(8,128)(2,1)S(1)}, u32[]{:S(2)}, u32[]{:S(2)}) async-start(bf16[8,128,128]{2,1,0:T(8,128)(2,1)} %attention.1), calls=%async_computation.2 | async-start | bytes 524288 | tf_op jit(solution)/shard_map/all_to_all | solution.py:402
  70.4 5.3 %collective-permute-start.11 = (bf16[32,32,128]{2,1,0:T(8,128)(2,1)S(1)}, bf16[32,32,128]{2,1,0:T(8,128)(2,1)S(1)}, u32[]{:S(2)}, u32[]{:S(2)}) collective-permute-start(bf16[32,32,128]{2,1,0:T(8,128)(2,1)S(1)} %get-tuple-element.39.refs_3_), channel_id=1, source_target_pairs={{0,1},{1,0},{2,3},{3,2},{4,5},{5,4},{6,7},{7,6},{8,9},{9,8},{10,11... | collective-permute-start | bytes 786440 | tf_op jit(solution)/shard_map/ppermute | solution.py:401
  73.8 1.9 %collective-permute-start.10 = (bf16[32,32,128]{2,1,0:T(8,128)(2,1)S(1)}, bf16[32,32,128]{2,1,0:T(8,128)(2,1)S(1)}, u32[]{:S(2)}, u32[]{:S(2)}) collective-permute-start(bf16[32,32,128]{2,1,0:T(8,128)(2,1)S(1)} %get-tuple-element.40.refs_2_), channel_id=1, source_target_pairs={{0,1},{1,0},{2,3},{3,2},{4,5},{5,4},{6,7},{7,6},{8,9},{9,8},{10,11... | collective-permute-start | bytes 786440 | tf_op jit(solution)/shard_map/ppermute | solution.py:401
  73.9 1.9 %collective-permute-start.9 = (bf16[32,32,128]{2,1,0:T(8,128)(2,1)S(1)}, bf16[32,32,128]{2,1,0:T(8,128)(2,1)S(1)}, u32[]{:S(2)}, u32[]{:S(2)}) collective-permute-start(bf16[32,32,128]{2,1,0:T(8,128)(2,1)S(1)} %get-tuple-element.41.refs_1_), channel_id=1, source_target_pairs={{0,1},{1,0},{2,3},{3,2},{4,5},{5,4},{6,7},{7,6},{8,9},{9,8},{10,11... | collective-permute-start | bytes 786440 | tf_op jit(solution)/shard_map/ppermute | solution.py:401
  74.3 1.8 %collective-permute-start.8 = (bf16[32,32,128]{2,1,0:T(8,128)(2,1)S(1)}, bf16[32,32,128]{2,1,0:T(8,128)(2,1)S(1)}, u32[]{:S(2)}, u32[]{:S(2)}) collective-permute-start(bf16[32,32,128]{2,1,0:T(8,128)(2,1)S(1)} %get-tuple-element.42.refs_0_), channel_id=1, source_target_pairs={{0,1},{1,0},{2,3},{3,2},{4,5},{5,4},{6,7},{7,6},{8,9},{9,8},{10,11... | collective-permute-start | bytes 786440 | tf_op jit(solution)/shard_map/ppermute | solution.py:401
  82.0 39.8 %copy-start.3 = (bf16[1,1408,1024]{2,1,0:T(8,128)(2,1)S(1)}, bf16[1,1408,1024]{2,1,0:T(8,128)(2,1)}, u32[]{:S(2)}) copy-start(bf16[1,1408,1024]{2,1,0:T(8,128)(2,1)} %param.21) | copy-start | bytes 8650756

commit v6 on v4

--- a/solution.py
+++ b/solution.py
@@ -77,7 +77,7 @@
         ],
         in_specs=[vmem_spec()] * 2,
         out_specs=[vmem_spec()] * 2,
-        compiler_params=pltpu.CompilerParams(vmem_limit_bytes=60 * MIB),
+        compiler_params=pltpu.CompilerParams(vmem_limit_bytes=40 * MIB),
         cost_estimate=pl.CostEstimate(flops=10**6, bytes_accessed=2 * 10**6, transcendentals=0),
         name="plane_parts",
     )(small, w_head)

time: 161 us -> 160 us (level)
  no operation moved by 1% of the time
where the time goes in v6:
time: 160 us
  blocking collectives  69.7 us (44%)
  starting transfers between devices  32.5 us (20%)
  waiting for transfers between devices  30.8 us (19%)
  Pallas kernels  23 us (14%)
  local copies, waits for them, and re-layouts  3.48 us (2%)
    all_to_all x1, blocking collectives, per_device(): lax.all_to_all(outgoing, 'expert', split_axis=0, concat_axis=0, tiled=True)  37.8 us
    all_to_all x1, blocking collectives, per_device(): lax.all_to_all(result.reshape(arrived.shape), 'expert', split_axis=0, con...  31.9 us
    ppermute x3, waiting for transfers between devices, ring_gather(): back = lax.ppermute(back, axis, down)  12.9 us
    pallas_call x1, Pallas kernels, run_expert(): pl.pallas_call(expert_kernel, out_shape=jax.ShapeDtypeStruct((count, widt...  9.99 us
    all_to_all x1, starting transfers between devices, per_device(): plane = lax.all_to_all(parts, 'expert', 0, 0, tiled=True)  9.93 us
    ppermute x3, starting transfers between devices, ring_gather(): back = lax.ppermute(back, axis, down)  7.74 us
    pallas_call x1, Pallas kernels, attention(): pl.pallas_call(functools.partial(attention_kernel, steps), out_shape=jax....  4.62 us
    all_to_all x1, starting transfers between devices, per_device(): small = lax.all_to_all(small, 'ctx', 0, 0, tiled=True)  4.07 us
  transfers between devices with their start and end apart: 15, of which 10 were waited for; matrix products, arithmetic and copies ran while one was open for 1% of the time, Pallas kernels for 1%

profile of v6, /device:TPU:1, one launch (start us, length us, event | category | flops | bytes accessed | tf_op | source)
XLA Modules:
  0.0 159.6 jit_solution(9785819105105742747)
XLA Ops:
  0.0 1.8 %start.1 = (bf16[128,1024]{1,0:T(8,128)(2,1)}, bf16[8,48,128]{2,1,0:T(8,128)(2,1)}) custom-call(bf16[128,1024]{1,0:T(8,128)(2,1)} %bitcast.22, f32[1,1024]{1,0:T(1,128)} %bitcast.32, bf16[32,128]{1,0:T(8,128)(2,1)} %bitcast.31, s32[1,128]{1,0:T(1,128)} %chain_ref.1), custom_call_target="tpu_custom_call" | custom-call | flops 1000000 | bytes 1000000 | tf_op jit(solution)/shard_map/start/pallas_call | solution.py:43
  1.8 6.4 %collective-permute-start.1 = (bf16[128,1024]{1,0:T(8,128)(2,1)}, bf16[128,1024]{1,0:T(8,128)(2,1)S(1)}, u32[]{:S(2)}, u32[]{:S(2)}) collective-permute-start(bf16[128,1024]{1,0:T(8,128)(2,1)} %get-tuple-element.23.refs_0_), channel_id=1, source_target_pairs={{0,224},{32,0},{64,32},{96,64},{128,96},{160,128},{192,160},{224,1... | collective-permute-start | bytes 786440 | tf_op jit(solution)/shard_map/ppermute | solution.py:351
  8.2 0.0 collective-permute-start
  8.2 4.1 %all-to-all-start = ((bf16[8,48,128]{2,1,0:T(8,128)(2,1)}), bf16[8,48,128]{2,1,0:T(8,128)(2,1)S(1)}, u32[]{:S(2)}, u32[]{:S(2)}) async-start(bf16[8,48,128]{2,1,0:T(8,128)(2,1)} %get-tuple-element.22), calls=%async_computation | async-start | bytes 196608 | tf_op jit(solution)/shard_map/all_to_all | solution.py:382
  12.3 1.2 collective-permute-done.1.refs_2_
  13.5 3.0 %collective-permute-done.refs_1_ = bf16[128,1024]{1,0:T(8,128)(2,1)S(1)} collective-permute-done((bf16[128,1024]{1,0:T(8,128)(2,1)}, bf16[128,1024]{1,0:T(8,128)(2,1)S(1)}, u32[]{:S(2)}, u32[]{:S(2)}) %collective-permute-start) | collective-permute-done | bytes 262176 | tf_op jit(solution)/shard_map/ppermute | solution.py:350
  16.5 3.4 %all-to-all-done.small_ref = bf16[8,48,128]{2,1,0:T(8,128)(2,1)S(1)} async-done(((bf16[8,48,128]{2,1,0:T(8,128)(2,1)}), bf16[8,48,128]{2,1,0:T(8,128)(2,1)S(1)}, u32[]{:S(2)}, u32[]{:S(2)}) %all-to-all-start) | async-done | bytes 98336 | tf_op jit(solution)/shard_map/all_to_all | solution.py:382
  19.9 0.7 copy-done.1
  20.6 1.4 plane_parts.1
  22.1 9.9 %all-to-all-start.1 = ((bf16[32,224,128]{2,1,0:T(8,128)(2,1)}), bf16[32,224,128]{2,1,0:T(8,128)(2,1)}, u32[]{:S(2)}, u32[]{:S(2)}) async-start(bf16[32,224,128]{2,1,0:T(8,128)(2,1)} %get-tuple-element.25), calls=%async_computation.1 | async-start | bytes 3670016 | tf_op jit(solution)/shard_map/all_to_all | solution.py:386
  32.0 0.1 collective-permute-start.5
  32.1 1.4 collective-permute-start.2
  33.6 6.2 %collective-permute-done.5.refs_4_ = bf16[128,1024]{1,0:T(8,128)(2,1)S(1)} collective-permute-done((bf16[128,1024]{1,0:T(8,128)(2,1)S(1)}, bf16[128,1024]{1,0:T(8,128)(2,1)S(1)}, u32[]{:S(2)}, u32[]{:S(2)}) %collective-permute-start.5) | collective-permute-done | bytes 262176 | tf_op jit(solution)/shard_map/ppermute | solution.py:351
  39.8 1.2 collective-permute-start.6
  41.0 0.0 collective-permute-done.2.refs_3_
  41.0 0.2 collective-permute-start.3
  41.3 5.4 %collective-permute-done.6.refs_6_ = bf16[128,1024]{1,0:T(8,128)(2,1)S(1)} collective-permute-done((bf16[128,1024]{1,0:T(8,128)(2,1)S(1)}, bf16[128,1024]{1,0:T(8,128)(2,1)S(1)}, u32[]{:S(2)}, u32[]{:S(2)}) %collective-permute-start.6) | collective-permute-done | bytes 262176 | tf_op jit(solution)/shard_map/ppermute | solution.py:351
  46.7 2.4 %collective-permute-start.7 = (bf16[64,1024]{1,0:T(8,128)(2,1)S(1)}, bf16[64,1024]{1,0:T(8,128)(2,1)S(1)}, u32[]{:S(2)}, u32[]{:S(2)}) collective-permute-start(bf16[64,1024]{1,0:T(8,128)(2,1)S(1)} %slice.29), channel_id=1, source_target_pairs={{0,224},{32,0},{64,32},{96,64},{128,96},{160,128},{192,160},{224,1... | collective-permute-start | bytes 393224 | tf_op jit(solution)/shard_map/ppermute | solution.py:355
  49.2 0.0 collective-permute-done.3.refs_5_
  49.2 0.1 collective-permute-start.4
  49.3 1.8 %collective-permute-done.7.refs_8_ = bf16[64,1024]{1,0:T(8,128)(2,1)S(1)} collective-permute-done((bf16[64,1024]{1,0:T(8,128)(2,1)S(1)}, bf16[64,1024]{1,0:T(8,128)(2,1)S(1)}, u32[]{:S(2)}, u32[]{:S(2)}) %collective-permute-start.7) | collective-permute-done | bytes 131104 | tf_op jit(solution)/shard_map/ppermute | solution.py:355
  51.1 3.2 %collective-permute-done.4.refs_7_ = bf16[64,1024]{1,0:T(8,128)(2,1)S(1)} collective-permute-done((bf16[64,1024]{1,0:T(8,128)(2,1)S(1)}, bf16[64,1024]{1,0:T(8,128)(2,1)S(1)}, u32[]{:S(2)}, u32[]{:S(2)}) %collective-permute-start.4) | collective-permute-done | bytes 131104 | tf_op jit(solution)/shard_map/ppermute | solution.py:355
  54.3 2.6 %all-to-all-done.1 = bf16[32,224,128]{2,1,0:T(8,128)(2,1)} async-done(((bf16[32,224,128]{2,1,0:T(8,128)(2,1)}), bf16[32,224,128]{2,1,0:T(8,128)(2,1)}, u32[]{:S(2)}, u32[]{:S(2)}) %all-to-all-start.1) | async-done | bytes 1835040 | tf_op jit(solution)/shard_map/all_to_all | solution.py:386
  57.0 1.2 slice.23.w_ref
  58.2 0.0 copy-done.4
  58.2 0.0 copy-done.5
  58.2 4.6 %attention.1 = bf16[8,128,128]{2,1,0:T(8,128)(2,1)} custom-call(s32[1]{0:T(128)} %bitcast.5.me_ref, f32[8]{0:T(128)S(1)} %copy-done.5, f32[8,1,128]{2,1,0:T(1,128)S(1)} %get-tuple-element.27.chain_ref, bf16[32,96,128]{2,1,0:T(8,128)(2,1)S(1)} %slice.23.w_ref, bf16[128,1024]{1,0:T(8,128)(2,1)S(1)} %copy-done.4, ...), custom_call_target="tpu_custom_call" | custom-call | flops 1400000000 | bytes 3000000 | tf_op jit(solution)/shard_map/attention/pallas_call | solution.py:222
  62.8 3.6 %all-to-all-start.2 = ((bf16[8,128,128]{2,1,0:T(8,128)(2,1)}), bf16[8,128,128]{2,1,0:T(8,128)(2,1)S(1)}, u32[]{:S(2)}, u32[]{:S(2)}) async-start(bf16[8,128,128]{2,1,0:T(8,128)(2,1)} %attention.1), calls=%async_computation.2 | async-start | bytes 524288 | tf_op jit(solution)/shard_map/all_to_all | solution.py:396
  66.4 1.3 fusion
  67.7 2.4 %collective-permute-start.11 = (bf16[32,32,128]{2,1,0:T(8,128)(2,1)S(1)}, bf16[32,32,128]{2,1,0:T(8,128)(2,1)S(1)}, u32[]{:S(2)}, u32[]{:S(2)}) collective-permute-start(bf16[32,32,128]{2,1,0:T(8,128)(2,1)S(1)} %get-tuple-element.39.refs_3_), channel_id=1, source_target_pairs={{0,1},{1,0},{2,3},{3,2},{4,5},{5,4},{6,7},{7,6},{8,9},{9,8},{10,11... | collective-permute-start | bytes 786440 | tf_op jit(solution)/shard_map/ppermute | solution.py:395
  70.0 0.1 collective-permute-start.10
  70.1 0.4 collective-permute-start.9
  70.5 0.1 collective-permute-start.8
  70.6 0.1 copy.12
  70.8 0.1 copy.14
  70.9 0.4 pick_table.1.refs_10_
  71.2 0.7 gate_tables.1.gate_ref
  72.0 0.0 collective-permute-done.11.refs_7_
  72.0 0.0 collective-permute-done.10.refs_6_
  72.0 0.0 collective-permute-done.9.refs_5_
  72.0 0.3 collective-permute-done.8.refs_4_
  72.3 3.5 %all-to-all-done.2.heads_ref = bf16[8,128,128]{2,1,0:T(8,128)(2,1)S(1)} async-done(((bf16[8,128,128]{2,1,0:T(8,128)(2,1)}), bf16[8,128,128]{2,1,0:T(8,128)(2,1)S(1)}, u32[]{:S(2)}, u32[]{:S(2)}) %all-to-all-start.2) | async-done | bytes 262176 | tf_op jit(solution)/shard_map/all_to_all | solution.py:396
  75.8 2.6 %dispatch.1 = (f32[128,1024]{1,0:T(8,128)S(1)}, bf16[32,32,1024]{2,1,0:T(8,128)(2,1)S(1)}, bf16[1024,2816]{1,0:T(8,128)(2,1)S(1)}) custom-call(s32[1]{0:T(128)} %bitcast.core_ref, bf16[8,128,128]{2,1,0:T(8,128)(2,1)S(1)} %all-to-all-done.2.heads_ref, bf16[32,32,128]{2,1,0:T(8,128)(2,1)S(1)} %get-tuple-element.42.refs_0_, ...), custom_call_target="tpu_custom_call" | custom-call | flops 600000000 | bytes 5000000 | tf_op jit(solution)/shard_map/dispatch/pallas_call | solution.py:272
  78.4 0.0 copy-start.3
  78.5 37.8 %all_to_all.25 = bf16[32,32,1024]{2,1,0:T(8,128)(2,1)S(1)} all-to-all(bf16[32,32,1024]{2,1,0:T(8,128)(2,1)S(1)} %get-tuple-element.37), channel_id=1, replica_groups=mesh['ctx'=8,'expert'=32] {'expert'}, dimensions={0} | all-to-all | bytes 4194304 | tf_op jit(solution)/shard_map/all_to_all | solution.py:403
  116.3 10.0 %experts.1 = bf16[1024,1024]{1,0:T(8,128)(2,1)S(1)} custom-call(bf16[1024,1024]{1,0:T(8,128)(2,1)S(1)} %bitcast.20, bf16[1024,2816]{1,0:T(8,128)(2,1)S(1)} %get-tuple-element.38.up_ref, bf16[1408,1024]{1,0:T(8,128)(2,1)S(1)} %bitcast.29), custom_call_target="tpu_custom_call" | custom-call | flops 8858370048 | bytes 9000000 | tf_op jit(solution)/shard_map/experts/pallas_call | solution.py:310
  126.3 31.9 %all_to_all.26 = bf16[32,32,1024]{2,1,0:T(8,128)(2,1)S(1)} all-to-all(bf16[32,32,1024]{2,1,0:T(8,128)(2,1)S(1)} %bitcast.21), channel_id=1, replica_groups=mesh['ctx'=8,'expert'=32] {'expert'}, dimensions={0} | all-to-all | bytes 4194304 | tf_op jit(solution)/shard_map/all_to_all | solution.py:405
  158.2 1.4 combine.1
  (15 shorter events, 0.0 us)
Async XLA Ops:
  1.8 11.7 %collective-permute-start.1 = (bf16[128,1024]{1,0:T(8,128)(2,1)}, bf16[128,1024]{1,0:T(8,128)(2,1)S(1)}, u32[]{:S(2)}, u32[]{:S(2)}) collective-permute-start(bf16[128,1024]{1,0:T(8,128)(2,1)} %get-tuple-element.23.refs_0_), channel_id=1, source_target_pairs={{0,224},{32,0},{64,32},{96,64},{128,96},{160,128},{192,160},{224,1... | collective-permute-start | bytes 786440 | tf_op jit(solution)/shard_map/ppermute | solution.py:351
  8.2 8.3 %collective-permute-start = (bf16[128,1024]{1,0:T(8,128)(2,1)}, bf16[128,1024]{1,0:T(8,128)(2,1)S(1)}, u32[]{:S(2)}, u32[]{:S(2)}) collective-permute-start(bf16[128,1024]{1,0:T(8,128)(2,1)} %get-tuple-element.23.refs_0_), channel_id=1, source_target_pairs={{0,32},{32,64},{64,96},{96,128},{128,160},{160,192},{192,224},{224... | collective-permute-start | bytes 786440 | tf_op jit(solution)/shard_map/ppermute | solution.py:350
  8.2 11.7 %all-to-all-start = ((bf16[8,48,128]{2,1,0:T(8,128)(2,1)}), bf16[8,48,128]{2,1,0:T(8,128)(2,1)S(1)}, u32[]{:S(2)}, u32[]{:S(2)}) async-start(bf16[8,48,128]{2,1,0:T(8,128)(2,1)} %get-tuple-element.22), calls=%async_computation | async-start | bytes 196608 | tf_op jit(solution)/shard_map/all_to_all | solution.py:382
  19.9 0.7 copy-start.1
  22.1 36.1 %copy-start.4 = (bf16[128,1024]{1,0:T(8,128)(2,1)S(1)}, bf16[128,1024]{1,0:T(8,128)(2,1)}, u32[]{:S(2)}) copy-start(bf16[128,1024]{1,0:T(8,128)(2,1)} %get-tuple-element.23.refs_0_) | copy-start | bytes 786436
  22.1 36.1 %copy-start.5 = (f32[8]{0:T(128)S(1)}, f32[8]{0:T(128)}, u32[]{:S(2)}) copy-start(f32[8]{0:T(128)} %bias_ref.1) | copy-start | bytes 100
  22.1 34.9 %all-to-all-start.1 = ((bf16[32,224,128]{2,1,0:T(8,128)(2,1)}), bf16[32,224,128]{2,1,0:T(8,128)(2,1)}, u32[]{:S(2)}, u32[]{:S(2)}) async-start(bf16[32,224,128]{2,1,0:T(8,128)(2,1)} %get-tuple-element.25), calls=%async_computation.1 | async-start | bytes 3670016 | tf_op jit(solution)/shard_map/all_to_all | solution.py:386
  32.0 7.8 %collective-permute-start.5 = (bf16[128,1024]{1,0:T(8,128)(2,1)S(1)}, bf16[128,1024]{1,0:T(8,128)(2,1)S(1)}, u32[]{:S(2)}, u32[]{:S(2)}) collective-permute-start(bf16[128,1024]{1,0:T(8,128)(2,1)S(1)} %collective-permute-done.1.refs_2_), channel_id=1, source_target_pairs={{0,224},{32,0},{64,32},{96,64},{128,96},{160,128},{192,160},{224,1... | collective-permute-start | bytes 786440 | tf_op jit(solution)/shard_map/ppermute | solution.py:351
  32.1 8.9 %collective-permute-start.2 = (bf16[128,1024]{1,0:T(8,128)(2,1)S(1)}, bf16[128,1024]{1,0:T(8,128)(2,1)S(1)}, u32[]{:S(2)}, u32[]{:S(2)}) collective-permute-start(bf16[128,1024]{1,0:T(8,128)(2,1)S(1)} %collective-permute-done.refs_1_), channel_id=1, source_target_pairs={{0,32},{32,64},{64,96},{96,128},{128,160},{160,192},{192,224},{224... | collective-permute-start | bytes 786440 | tf_op jit(solution)/shard_map/ppermute | solution.py:350
  39.8 6.9 %collective-permute-start.6 = (bf16[128,1024]{1,0:T(8,128)(2,1)S(1)}, bf16[128,1024]{1,0:T(8,128)(2,1)S(1)}, u32[]{:S(2)}, u32[]{:S(2)}) collective-permute-start(bf16[128,1024]{1,0:T(8,128)(2,1)S(1)} %collective-permute-done.5.refs_4_), channel_id=1, source_target_pairs={{0,224},{32,0},{64,32},{96,64},{128,96},{160,128},{192,160},{224,1... | collective-permute-start | bytes 786440 | tf_op jit(solution)/shard_map/ppermute | solution.py:351
  41.0 8.1 %collective-permute-start.3 = (bf16[128,1024]{1,0:T(8,128)(2,1)S(1)}, bf16[128,1024]{1,0:T(8,128)(2,1)S(1)}, u32[]{:S(2)}, u32[]{:S(2)}) collective-permute-start(bf16[128,1024]{1,0:T(8,128)(2,1)S(1)} %collective-permute-done.2.refs_3_), channel_id=1, source_target_pairs={{0,32},{32,64},{64,96},{96,128},{128,160},{160,192},{192,224},{224... | collective-permute-start | bytes 786440 | tf_op jit(solution)/shard_map/ppermute | solution.py:350
  46.7 4.4 %collective-permute-start.7 = (bf16[64,1024]{1,0:T(8,128)(2,1)S(1)}, bf16[64,1024]{1,0:T(8,128)(2,1)S(1)}, u32[]{:S(2)}, u32[]{:S(2)}) collective-permute-start(bf16[64,1024]{1,0:T(8,128)(2,1)S(1)} %slice.29), channel_id=1, source_target_pairs={{0,224},{32,0},{64,32},{96,64},{128,96},{160,128},{192,160},{224,1... | collective-permute-start | bytes 393224 | tf_op jit(solution)/shard_map/ppermute | solution.py:355
  49.2 5.2 %collective-permute-start.4 = (bf16[64,1024]{1,0:T(8,128)(2,1)S(1)}, bf16[64,1024]{1,0:T(8,128)(2,1)S(1)}, u32[]{:S(2)}, u32[]{:S(2)}) collective-permute-start(bf16[64,1024]{1,0:T(8,128)(2,1)S(1)} %slice.28), channel_id=1, source_target_pairs={{0,32},{32,64},{64,96},{96,128},{128,160},{160,192},{192,224},{224... | collective-permute-start | bytes 393224 | tf_op jit(solution)/shard_map/ppermute | solution.py:355
  62.8 7.8 %copy-start.6 = (s32[1,128,6]{1,0,2:T(1,128)S(1)}, s32[1,128,6]{1,0,2:T(1,128)}, u32[]{:S(2)}) copy-start(s32[1,128,6]{1,0,2:T(1,128)} %param.13) | copy-start | bytes 9220
  62.8 7.9 %copy-start.7 = (f32[1,128,6]{1,0,2:T(1,128)S(1)}, f32[1,128,6]{1,0,2:T(1,128)}, u32[]{:S(2)}) copy-start(f32[1,128,6]{1,0,2:T(1,128)} %param.14) | copy-start | bytes 9220
  62.8 13.0 %copy-start = (bf16[1,128,1024]{2,1,0:T(8,128)(2,1)S(1)}, bf16[1,128,1024]{2,1,0:T(8,128)(2,1)}, u32[]{:S(2)}) copy-start(bf16[1,128,1024]{2,1,0:T(8,128)(2,1)} %param.11) | copy-start | bytes 786436
  62.8 13.0 %copy-start.2 = (f32[1024]{0:T(1024)S(1)}, f32[1024]{0:T(1024)}, u32[]{:S(2)}) copy-start(f32[1024]{0:T(1024)} %param.16) | copy-start | bytes 12292
  62.8 13.0 %all-to-all-start.2 = ((bf16[8,128,128]{2,1,0:T(8,128)(2,1)}), bf16[8,128,128]{2,1,0:T(8,128)(2,1)S(1)}, u32[]{:S(2)}, u32[]{:S(2)}) async-start(bf16[8,128,128]{2,1,0:T(8,128)(2,1)} %attention.1), calls=%async_computation.2 | async-start | bytes 524288 | tf_op jit(solution)/shard_map/all_to_all | solution.py:396
  67.7 4.3 %collective-permute-start.11 = (bf16[32,32,128]{2,1,0:T(8,128)(2,1)S(1)}, bf16[32,32,128]{2,1,0:T(8,128)(2,1)S(1)}, u32[]{:S(2)}, u32[]{:S(2)}) collective-permute-start(bf16[32,32,128]{2,1,0:T(8,128)(2,1)S(1)} %get-tuple-element.39.refs_3_), channel_id=1, source_target_pairs={{0,1},{1,0},{2,3},{3,2},{4,5},{5,4},{6,7},{7,6},{8,9},{9,8},{10,11... | collective-permute-start | bytes 786440 | tf_op jit(solution)/shard_map/ppermute | solution.py:395
  70.0 1.9 %collective-permute-start.10 = (bf16[32,32,128]{2,1,0:T(8,128)(2,1)S(1)}, bf16[32,32,128]{2,1,0:T(8,128)(2,1)S(1)}, u32[]{:S(2)}, u32[]{:S(2)}) collective-permute-start(bf16[32,32,128]{2,1,0:T(8,128)(2,1)S(1)} %get-tuple-element.40.refs_2_), channel_id=1, source_target_pairs={{0,1},{1,0},{2,3},{3,2},{4,5},{5,4},{6,7},{7,6},{8,9},{9,8},{10,11... | collective-permute-start | bytes 786440 | tf_op jit(solution)/shard_map/ppermute | solution.py:395
  70.1 1.9 %collective-permute-start.9 = (bf16[32,32,128]{2,1,0:T(8,128)(2,1)S(1)}, bf16[32,32,128]{2,1,0:T(8,128)(2,1)S(1)}, u32[]{:S(2)}, u32[]{:S(2)}) collective-permute-start(bf16[32,32,128]{2,1,0:T(8,128)(2,1)S(1)} %get-tuple-element.41.refs_1_), channel_id=1, source_target_pairs={{0,1},{1,0},{2,3},{3,2},{4,5},{5,4},{6,7},{7,6},{8,9},{9,8},{10,11... | collective-permute-start | bytes 786440 | tf_op jit(solution)/shard_map/ppermute | solution.py:395
  70.5 1.8 %collective-permute-start.8 = (bf16[32,32,128]{2,1,0:T(8,128)(2,1)S(1)}, bf16[32,32,128]{2,1,0:T(8,128)(2,1)S(1)}, u32[]{:S(2)}, u32[]{:S(2)}) collective-permute-start(bf16[32,32,128]{2,1,0:T(8,128)(2,1)S(1)} %get-tuple-element.42.refs_0_), channel_id=1, source_target_pairs={{0,1},{1,0},{2,3},{3,2},{4,5},{5,4},{6,7},{7,6},{8,9},{9,8},{10,11... | collective-permute-start | bytes 786440 | tf_op jit(solution)/shard_map/ppermute | solution.py:395
  78.4 37.8 %copy-start.3 = (bf16[1,1408,1024]{2,1,0:T(8,128)(2,1)S(1)}, bf16[1,1408,1024]{2,1,0:T(8,128)(2,1)}, u32[]{:S(2)}) copy-start(bf16[1,1408,1024]{2,1,0:T(8,128)(2,1)} %param.21) | copy-start | bytes 8650756
